TPU v7x, 512 devices: a whole 4x4x16 slice. The times are simulated.
512 devices in a mesh: expert: 64 (over x, z), shard: 8 (over y, core).
Axes of the slice: x: 4, y: 4, z: 16, core: 2. Of those that a mesh axis runs over, the one named last changes fastest.
Arguments:
- tokens: bfloat16 [8192, 4096], P('expert'), may hold values from -6 to 6
- slot_lists: int32 [64, 64, 8], P(None, 'expert'), may hold values from -1 to 127, as said below
- slot_gates: float32 [64, 64, 8], P(None, 'expert'), may hold values from 0.1 to 1
- counts: int32 [8192], P('expert'), may hold values from 0 to 64, as said below
- gate_weight: bfloat16 [64, 4096, 1024], P('expert', None, 'shard'), may hold values from -0.09375 to 0.09375
- up_weight: bfloat16 [64, 4096, 1024], P('expert', None, 'shard'), may hold values from -0.09375 to 0.09375
- down_weight: bfloat16 [64, 1024, 4096], P('expert', 'shard'), may hold values from -0.1875 to 0.1875
Outputs:
- combined: bfloat16 [8192, 4096], P('expert', 'shard')
Inputs may be any that keep to these rules, and one draw needn't show every extreme that they name: Each block slot_lists[e, o] names distinct tokens of owner o in its leading entries, one or more, and holds -1 after them; in every draw one expert's blocks are full from every owner, and every expert names token 0 of owner 0. counts[t] is the number of live slots, over all experts, that name token t.
All inputs are finite; a program needn't handle non-finite values.
Results may differ from a plain program's by a relative error of at most 0.019.
Values may be sent and summed in bfloat16 or wider, within the bound.
No kernel may reach another device: no remote copies, remote signals or barrier semaphores. Data moves between devices by JAX's collectives and lax.ppermute only.
A program may use at most 64 MiB of HBM per device.

v0:
```python
import jax
import jax.numpy as jnp
from jax import lax
from jax.sharding import PartitionSpec as P


def local(tokens, slot_lists, slot_gates, counts, gate_weight, up_weight, down_weight):
    shard_count = lax.axis_size("shard")
    features = tokens.shape[1]
    column_count = features // shard_count
    column_start = lax.axis_index("shard") * column_count
    local_tokens = tokens.shape[0]
    expert_rows = slot_lists.shape[0]
    slot_count = slot_lists.shape[2]
    usable = slot_lists >= 0
    safe_rows = jnp.where(usable, slot_lists, 0).reshape(-1)
    row_mask = usable.reshape(-1, 1)
    taken = jnp.take(tokens, safe_rows, axis=0)
    picked = jnp.where(row_mask, taken, jnp.zeros_like(taken))
    picked = picked.reshape(expert_rows, 1, slot_count, features)
    arrived = lax.all_to_all(picked, "expert", split_axis=0, concat_axis=1, tiled=True)
    gate_act = jnp.einsum(
        "enkd,edh->enkh", arrived, gate_weight, preferred_element_type=jnp.float32
    )
    up_act = jnp.einsum("enkd,edh->enkh", arrived, up_weight, preferred_element_type=jnp.float32)
    hidden = (jax.nn.silu(gate_act) * up_act).astype(jnp.bfloat16)
    outputs = jnp.einsum(
        "enkh,ehd->enkd", hidden, down_weight, preferred_element_type=jnp.float32
    ).astype(jnp.bfloat16)
    summed = lax.psum(outputs, "shard").astype(jnp.float32)
    own_share = lax.dynamic_slice_in_dim(summed, column_start, column_count, 3)
    returned = lax.all_to_all(
        own_share.astype(jnp.bfloat16), "expert", split_axis=1, concat_axis=0, tiled=True
    )
    gate_values = jnp.where(usable, slot_gates, jnp.zeros_like(slot_gates)).reshape(-1)
    weighted = returned.reshape(-1, column_count).astype(jnp.float32) * gate_values[:, None]
    targets = jnp.where(usable, slot_lists, local_tokens).reshape(-1)
    totals = jax.ops.segment_sum(weighted, targets, num_segments=local_tokens + 1)[:local_tokens]
    divisor = jnp.maximum(counts.astype(jnp.float32), 1.0)
    return (totals / divisor[:, None]).astype(jnp.bfloat16)


def solution(mesh):
    return jax.shard_map(
        local,
        mesh=mesh,
        in_specs=(
            P("expert", None),
            P(None, "expert", None),
            P(None, "expert", None),
            P("expert"),
            P("expert", None, "shard"),
            P("expert", None, "shard"),
            P("expert", "shard", None),
        ),
        out_specs=P("expert", "shard"),
        check_vma=False,
    )
```

profile of v0, /device:TPU:6, one launch (start us, length us, event | category | flops | bytes accessed | tf_op | source)
XLA Modules:
  0.0 374.8 jit_solution(13922672720514396880)
XLA Ops:
  6.5 0.0 copy-start
  6.5 0.0 all-reduce.2.cloned.1.call-start
  6.5 0.8 broadcast_select_fusion.2
  7.3 0.7 compare_and_fusion
  8.0 0.7 fusion.32
  8.7 0.1 copy.18
  8.8 0.1 reshape.109
  8.9 0.1 copy.17
  9.0 0.1 copy.16
  9.1 0.0 copy-done
  9.1 4.4 %gather_fusion = bf16[512,4096]{1,0:T(8,128)(2,1)} fusion(bf16[128,4096]{1,0:T(8,128)(2,1)S(1)} %copy-done, s32[1024]{0:T(1024)S(1)} %pad_clamp_fusion), kind=kCustom, calls=%fused_computation | custom fusion | bytes 8390656 | tf_op jit(solution)/shard_map/jit(_take)/gather | solution.py:18
  13.5 2.6 fusion.1
  16.1 0.0 copy-start.2
  16.1 206.2 %all_to_all.8 = bf16[64,1,8,4096]{3,2,1,0:T(8,128)(2,1)S(1)} all-to-all(bf16[64,1,8,4096]{3,2,1,0:T(8,128)(2,1)S(1)} %fusion.1), channel_id=1, replica_groups=mesh['expert'=64,'shard'=8] {'expert'}, dimensions={0} | all-to-all | bytes 8388608 | tf_op jit(solution)/shard_map/all_to_all | solution.py:21
  222.3 1.9 copy-done.1
  224.2 0.0 copy-done.2
  224.2 1.3 fusion.4
  225.5 0.0 copy-done.3
  225.5 0.3 copy-done.4
  225.8 8.6 %fusion = bf16[1,64,8,4096]{3,2,1,0:T(8,128)(2,1)} fusion(bf16[1,128,4096]{2,1,0:T(8,128)(2,1)S(1)} %copy-done.3, bf16[64,1,8,4096]{3,2,1,0:T(8,128)(2,1)} %copy-done.1, bf16[1,4096,128]{2,1,0:T(8,128)(2,1)S(1)} %copy-done.4, f32[64,8,128]{2,1,0:T(8,128)S(1)} %fusion.4), kind=kOutput, calls=%fused_computation.3 | convolution fusion | flops 1076232192 | bytes 10747904 | tf_op jit(solution)/shard_map/enkh,ehd->enkd/dot_general | solution.py:27
  234.4 0.0 all-reduce.2.cloned.1.call-update
  234.4 81.7 %all-reduce.2.cloned.1.call-done = bf16[1,64,8,4096]{3,2,1,0:T(8,128)(2,1)} async-done(((bf16[1,64,8,4096]{3,2,1,0:T(8,128)(2,1)}), bf16[1,64,8,4096]{3,2,1,0:T(8,128)(2,1)}) %all-reduce.2.cloned.1.call-update) | async-done | bytes 4194320 | tf_op jit(solution)/shard_map/psum | solution.py:30
  316.1 1.9 fusion.20
  318.0 15.9 %all-to-all-start.1 = ((bf16[1,64,8,512]{3,2,0,1:T(8,128)(2,1)}), bf16[1,64,8,512]{3,2,0,1:T(8,128)(2,1)S(1)}, u32[]{:S(2)}, u32[]{:S(2)}) async-start(bf16[1,64,8,512]{3,2,0,1:T(8,128)(2,1)} %fusion.20), calls=%async_computation.1 | async-start | bytes 1048576 | tf_op jit(solution)/shard_map/all_to_all | solution.py:32
  333.9 0.1 copy.15
  334.0 0.1 reshape.125
  334.1 0.0 copy-done.5
  334.1 0.1 copy.21
  334.2 0.1 mul.25
  334.3 29.1 %all-to-all-done.1 = bf16[1,64,8,512]{3,2,0,1:T(8,128)(2,1)S(1)} async-done(((bf16[1,64,8,512]{3,2,0,1:T(8,128)(2,1)}), bf16[1,64,8,512]{3,2,0,1:T(8,128)(2,1)S(1)}, u32[]{:S(2)}, u32[]{:S(2)}) %all-to-all-start.1) | async-done | bytes 524320 | tf_op jit(solution)/shard_map/all_to_all | solution.py:32
  363.4 3.8 %scatter_custom_fusion = f32[129,512]{1,0:T(8,128)S(1)} fusion(s32[512]{0:T(512)S(1)} %reshape.125, bf16[1,64,8,512]{3,2,0,1:T(8,128)(2,1)S(1)} %all-to-all-done.1, f32[512]{0:T(512)S(1)} %mul.25, f32[]{:T(128)} %constant.10.clone.1), kind=kCustom, calls=%fused_computation.13 | custom fusion | flops 786432 | bytes 790532 | tf_op jit(solution)/shard_map/scatter-add | solution.py:38
  367.2 0.7 fusion.23
  (12 shorter events, 0.0 us)
Async XLA Ops:
  6.5 2.6 copy-start
  6.5 309.6 %all-reduce.2.cloned.1.call-start = ((), (), s32[]{:S(2)}) async-start(), calls=%async_computation.2 | async-start | bytes 8388608 | tf_op jit(solution)/shard_map/psum | solution.py:30
  16.1 208.2 %copy-start.2 = (bf16[1,4096,128]{2,1,0:T(8,128)(2,1)S(1)}, bf16[1,4096,128]{2,1,0:T(8,128)(2,1)}, u32[]{:S(2)}) copy-start(bf16[1,4096,128]{2,1,0:T(8,128)(2,1)} %param.11) | copy-start | bytes 3145732
  222.3 1.9 copy-start.1
  224.2 1.3 copy-start.3
  224.2 1.5 copy-start.4
  234.4 99.7 %copy-start.5 = (s32[64,1,8]{0,2,1:T(8,128)S(1)}, s32[64,1,8]{0,2,1:T(8,128)}, u32[]{:S(2)}) copy-start(s32[64,1,8]{0,2,1:T(8,128)} %param.8) | copy-start | bytes 6148
  234.4 99.7 %copy-start.6 = (f32[64,1,8]{0,2,1:T(8,128)S(1)}, f32[64,1,8]{0,2,1:T(8,128)}, u32[]{:S(2)}) copy-start(f32[64,1,8]{0,2,1:T(8,128)} %param.9) | copy-start | bytes 6148
  234.4 99.9 %copy-start.7 = (s32[128]{0:T(128)S(1)}, s32[128]{0:T(128)}, u32[]{:S(2)}) copy-start(s32[128]{0:T(128)} %param.10) | copy-start | bytes 1540
  318.0 45.4 %all-to-all-start.1 = ((bf16[1,64,8,512]{3,2,0,1:T(8,128)(2,1)}), bf16[1,64,8,512]{3,2,0,1:T(8,128)(2,1)S(1)}, u32[]{:S(2)}, u32[]{:S(2)}) async-start(bf16[1,64,8,512]{3,2,0,1:T(8,128)(2,1)} %fusion.20), calls=%async_computation.1 | async-start | bytes 1048576 | tf_op jit(solution)/shard_map/all_to_all | solution.py:32
Sparse Core Ops, SparseCore 0:
  234.5 81.5 all-reduce.1
where the time goes:
time: 376 us; the launch traced here: 375 us
  blocking collectives  206 us (55%)
  waiting for transfers between devices  111 us (30%)
  starting transfers between devices  15.9 us (4%)
  between operations  13.5 us (4%)
  other arithmetic  11.2 us (3%)
  matrix products  9.87 us (3%)
  local copies, waits for them, and re-layouts  7.33 us (2%)
    all_to_all x1, blocking collectives, local(): lax.all_to_all(picked, 'expert', split_axis=0, concat_axis=1, tiled=True)  206 us
    psum x1, waiting for transfers between devices, local(): summed = lax.psum(outputs, 'shard').astype(jnp.float32)  81.7 us
    all_to_all x1, waiting for transfers between devices, local(): lax.all_to_all(own_share.astype(jnp.bfloat16), 'expert', split_axis=1, co...  29.1 us
    all_to_all x1, starting transfers between devices, local(): lax.all_to_all(own_share.astype(jnp.bfloat16), 'expert', split_axis=1, co...  15.9 us
    dot_general x1, matrix products, local(): jnp.einsum('enkh,ehd->enkd', hidden, down_weight, preferred_element_type=...  8.62 us
  transfers between devices with their start and end apart: 2, of which 2 were waited for; matrix products, arithmetic and copies ran while one was open for 0% of the time, Pallas kernels for 0%

commit v1 on v0

v1 whole, which is shorter than its diff:
```python
import jax
import jax.numpy as jnp
import numpy as np
from jax import lax
from jax.sharding import Mesh, PartitionSpec as P

E = ("x", "z")
S = ("y", "core")
NY = 4
BF = jnp.bfloat16
F32 = jnp.float32


def dot(a, b):
    return jnp.dot(a, b, preferred_element_type=F32)


def swap_cores(a):
    return lax.ppermute(a, "core", [(0, 1), (1, 0)])


def local(tokens, slot_lists, slot_gates, counts, gate_weight, up_weight, down_weight):
    y = lax.axis_index("y")
    c = lax.axis_index("core")
    width = tokens.shape[1] // (2 * NY)
    group = 2 * width
    rows = slot_lists.shape[0] * slot_lists.shape[2]
    local_tokens = tokens.shape[0]
    gate_weight, up_weight, down_weight = gate_weight[0], up_weight[0], down_weight[0]

    own = lax.dynamic_slice_in_dim(tokens, (y * 2 + c) * width, width, 1)
    flat = slot_lists.reshape(rows, 1)
    onehot = (flat == lax.broadcasted_iota(jnp.int32, (rows, local_tokens), 1)).astype(BF)
    picked = dot(onehot, own).astype(BF)
    arrived = lax.all_to_all(picked.reshape(-1, 8, width), E, 0, 0, tiled=True).reshape(rows, width)

    gu, dn = [], []
    for d in range(NY):
        to = (y + d) % NY
        g = lax.dynamic_slice_in_dim(gate_weight, to * group, group, 0)
        u = lax.dynamic_slice_in_dim(up_weight, to * group, group, 0)
        w = jnp.concatenate([g, u], axis=1)
        v = lax.dynamic_slice_in_dim(down_weight, to * group, group, 1)
        if d:
            ring = [(j, (j + d) % NY) for j in range(NY)]
            w = lax.ppermute(w, "y", ring)
            v = lax.ppermute(v, "y", ring)
        gu.append(w)
        dn.append(v)

    arrived, gu, dn = lax.optimization_barrier((arrived, gu, dn))
    other = swap_cores(arrived)
    parts = []
    for d in range(NY):
        w_own = lax.dynamic_slice_in_dim(gu[d], c * width, width, 0)
        w_other = lax.dynamic_slice_in_dim(gu[d], (1 - c) * width, width, 0)
        parts.append((dot(arrived, w_own) + dot(other, w_other)).astype(BF))
    ordered = jnp.stack([parts[(NY - k) % NY] for k in range(NY)] * 2)
    ordered = lax.dynamic_slice_in_dim(ordered, NY - y, NY, 0)
    sums = lax.all_to_all(ordered, "y", 0, 0, tiled=True).astype(F32).sum(0)
    half = sums.shape[1] // 2
    hidden = (jax.nn.silu(sums[:, :half]) * sums[:, half:]).astype(BF)
    gathered = lax.all_to_all(jnp.broadcast_to(hidden, (NY,) + hidden.shape), "y", 0, 0, tiled=True)
    out = 0.0
    for d in range(NY):
        h = lax.dynamic_index_in_dim(gathered, (y - d) % NY, 0, keepdims=False)
        out = out + dot(h, dn[d])
    keep = lax.dynamic_slice_in_dim(out, c * width, width, 1)
    give = lax.dynamic_slice_in_dim(out, (1 - c) * width, width, 1).astype(BF)
    result = (keep + swap_cores(give).astype(F32)).astype(BF)
    returned = lax.all_to_all(result.reshape(-1, 8, width), E, 0, 0, tiled=True).reshape(rows, width)

    hit = slot_lists.reshape(1, rows) == lax.broadcasted_iota(jnp.int32, (local_tokens, rows), 0)
    weight = jnp.where(hit, slot_gates.reshape(1, rows), 0.0)
    totals = 0.0
    for _ in range(3):
        piece = weight.astype(BF)
        weight = weight - piece.astype(F32)
        totals = totals + dot(piece, returned)
    divisor = jnp.maximum(counts.astype(F32), 1.0)
    return (totals / divisor[:, None]).astype(BF)


def solution(mesh):
    fine = Mesh(np.asarray(mesh.devices).reshape(4, 16, NY, 2), ("x", "z", "y", "core"))
    return jax.shard_map(
        local,
        mesh=fine,
        in_specs=(
            P(E, None),
            P(None, E, None),
            P(None, E, None),
            P(E),
            P(E, None, S),
            P(E, None, S),
            P(E, S, None),
        ),
        out_specs=P(E, S),
        check_vma=False,
    )
```

time: 376 us -> 164 us (0.44)
  blocking collectives: 206 us -> 20.2 us
  starting transfers between devices: 15.9 us -> 63.5 us
  waiting for transfers between devices: 111 us -> 63.9 us
  between operations: 13.5 us -> 0.54 us
  other arithmetic: 11.2 us -> 1.49 us
    all_to_all x1, blocking collectives: 206 us -> 20.2 us  [local(): sums = lax.all_to_all(ordered, 'y', 0, 0, tiled=True).astype(F32).sum(0)]
    psum x1 -> x0, waiting for transfers between devices: 81.7 us -> none  [local(): summed = lax.psum(outputs, 'shard').astype(jnp.float32)]
    ppermute x0 -> x8, starting transfers between devices: none -> 26.1 us  [the longest x3 13.6 us: local(): w = lax.ppermute(w, 'y', ring)]
    ppermute x0 -> x8, waiting for transfers between devices: none -> 23.7 us  [the longest x3 19.9 us: local(): v = lax.ppermute(v, 'y', ring)]
    all_to_all x1 -> x3, starting transfers between devices: 15.9 us -> 37.4 us  [the longest x1 18.8 us: local(): lax.all_to_all(picked.reshape(-1, 8, width), E, 0, 0, tiled=True)]
    all_to_all x1 -> x3, waiting for transfers between devices: 29.1 us -> 40.3 us  [the longest x1 31.8 us: local(): lax.all_to_all(result.reshape(-1, 8, width), E, 0, 0, tiled=True)]
    gather x1 -> x0, local copies, waits for them, and re-layouts: 4.36 us -> none  [local(): taken = jnp.take(tokens, safe_rows, axis=0)]
    scatter-add x1 -> x0, other arithmetic: 3.76 us -> none  [local(): jax.ops.segment_sum(weighted, targets, num_segments=local_tokens + 1)]
  transfers between devices with their start and end apart: 2 -> 11, of which waited for: 2 -> 7; matrix products, arithmetic and copies ran while one was open for 0% -> 1% of each run, Pallas kernels for 0% -> 0%
where the time goes in v1:
time: 164 us
  waiting for transfers between devices  63.9 us (39%)
  starting transfers between devices  63.5 us (39%)
  blocking collectives  20.2 us (12%)
  matrix products  8.54 us (5%)
  local copies, waits for them, and re-layouts  5.61 us (3%)
    all_to_all x1, waiting for transfers between devices, local(): lax.all_to_all(result.reshape(-1, 8, width), E, 0, 0, tiled=True)  31.8 us
    all_to_all x1, blocking collectives, local(): sums = lax.all_to_all(ordered, 'y', 0, 0, tiled=True).astype(F32).sum(0)  20.2 us
    ppermute x3, waiting for transfers between devices, local(): v = lax.ppermute(v, 'y', ring)  19.9 us
    all_to_all x1, starting transfers between devices, local(): lax.all_to_all(picked.reshape(-1, 8, width), E, 0, 0, tiled=True)  18.8 us
    all_to_all x1, starting transfers between devices, local(): lax.all_to_all(result.reshape(-1, 8, width), E, 0, 0, tiled=True)  15.1 us
    ppermute x3, starting transfers between devices, local(): w = lax.ppermute(w, 'y', ring)  13.6 us
    ppermute x3, starting transfers between devices, local(): v = lax.ppermute(v, 'y', ring)  8.74 us
    dot_general x16, matrix products, dot(): return jnp.dot(a, b, preferred_element_type=F32)  8.54 us
  transfers between devices with their start and end apart: 11, of which 7 were waited for; matrix products, arithmetic and copies ran while one was open for 1% of the time, Pallas kernels for 0%

profile of v1, /device:TPU:6, one launch (start us, length us, event | category | flops | bytes accessed | tf_op | source)
XLA Modules:
  0.0 163.8 jit_solution(12245591608675844463)
XLA Ops:
  0.0 0.9 copy.8
  1.2 1.2 fusion
  2.4 18.8 %all-to-all-start = ((bf16[64,8,512]{2,1,0:T(8,128)(2,1)}), bf16[64,8,512]{2,1,0:T(8,128)(2,1)S(1)}, u32[]{:S(2)}, u32[]{:S(2)}) async-start(bf16[64,8,512]{2,1,0:T(8,128)(2,1)} %fusion), calls=%async_computation | async-start | bytes 1048576 | tf_op jit(solution)/shard_map/all_to_all | solution.py:35
  21.3 1.3 dynamic-slice_bitcast_fusion.4
  22.7 3.6 %collective-permute-start = (bf16[1024,256]{1,0:T(8,128)(2,1)S(1)}, bf16[1024,256]{1,0:T(8,128)(2,1)S(1)}, u32[]{:S(2)}, u32[]{:S(2)}) collective-permute-start(bf16[1024,256]{1,0:T(8,128)(2,1)S(1)} %pad_maximum_fusion.1), channel_id=1, source_target_pairs={{0,2},{2,4},{4,6},{6,0},{1,3},{3,5},{5,7},{7,1},{8,10},{10,12},{12... | collective-permute-start | bytes 1572872 | tf_op jit(solution)/shard_map/ppermute | solution.py:46
  26.4 4.8 %collective-permute-start.1 = (bf16[1024,256]{1,0:T(8,128)(2,1)S(1)}, bf16[1024,256]{1,0:T(8,128)(2,1)S(1)}, u32[]{:S(2)}, u32[]{:S(2)}) collective-permute-start(bf16[1024,256]{1,0:T(8,128)(2,1)S(1)} %pad_maximum_fusion.2), channel_id=1, source_target_pairs={{0,4},{2,6},{4,0},{6,2},{1,5},{3,7},{5,1},{7,3},{8,12},{10,14},{12... | collective-permute-start | bytes 1572872 | tf_op jit(solution)/shard_map/ppermute | solution.py:46
  31.3 1.9 %collective-permute-start.3 = (bf16[128,1024]{1,0:T(8,128)(2,1)S(1)}, bf16[128,1024]{1,0:T(8,128)(2,1)S(1)}, u32[]{:S(2)}, u32[]{:S(2)}) collective-permute-start(bf16[128,1024]{1,0:T(8,128)(2,1)S(1)} %get-tuple-element.24), channel_id=1, source_target_pairs={{0,2},{2,4},{4,6},{6,0},{1,3},{3,5},{5,7},{7,1},{8,10},{10,12},{12... | collective-permute-start | bytes 786440 | tf_op jit(solution)/shard_map/ppermute | solution.py:47
  33.3 5.1 %collective-permute-start.2 = (bf16[1024,256]{1,0:T(8,128)(2,1)S(1)}, bf16[1024,256]{1,0:T(8,128)(2,1)}, u32[]{:S(2)}, u32[]{:S(2)}) collective-permute-start(bf16[1024,256]{1,0:T(8,128)(2,1)S(1)} %pad_maximum_fusion.3), channel_id=1, source_target_pairs={{0,6},{2,0},{4,2},{6,4},{1,7},{3,1},{5,3},{7,5},{8,14},{10,8},{12,... | collective-permute-start | bytes 1572872 | tf_op jit(solution)/shard_map/ppermute | solution.py:46
  38.5 1.9 %collective-permute-start.4 = (bf16[128,1024]{1,0:T(8,128)(2,1)S(1)}, bf16[128,1024]{1,0:T(8,128)(2,1)S(1)}, u32[]{:S(2)}, u32[]{:S(2)}) collective-permute-start(bf16[128,1024]{1,0:T(8,128)(2,1)S(1)} %get-tuple-element.26), channel_id=1, source_target_pairs={{0,4},{2,6},{4,0},{6,2},{1,5},{3,7},{5,1},{7,3},{8,12},{10,14},{12... | collective-permute-start | bytes 786440 | tf_op jit(solution)/shard_map/ppermute | solution.py:47
  40.4 16.1 %collective-permute-done.3 = bf16[128,1024]{1,0:T(8,128)(2,1)S(1)} collective-permute-done((bf16[128,1024]{1,0:T(8,128)(2,1)S(1)}, bf16[128,1024]{1,0:T(8,128)(2,1)S(1)}, u32[]{:S(2)}, u32[]{:S(2)}) %collective-permute-start.3) | collective-permute-done | bytes 262176 | tf_op jit(solution)/shard_map/ppermute | solution.py:47
  56.5 4.9 %collective-permute-start.5 = (bf16[128,1024]{1,0:T(8,128)(2,1)S(1)}, bf16[128,1024]{1,0:T(8,128)(2,1)S(1)}, u32[]{:S(2)}, u32[]{:S(2)}) collective-permute-start(bf16[128,1024]{1,0:T(8,128)(2,1)S(1)} %get-tuple-element.23), channel_id=1, source_target_pairs={{0,6},{2,0},{4,2},{6,4},{1,7},{3,1},{5,3},{7,5},{8,14},{10,8},{12,... | collective-permute-start | bytes 786440 | tf_op jit(solution)/shard_map/ppermute | solution.py:47
  61.5 1.3 collective-permute-done.4
  62.8 2.5 %collective-permute-done.5 = bf16[128,1024]{1,0:T(8,128)(2,1)S(1)} collective-permute-done((bf16[128,1024]{1,0:T(8,128)(2,1)S(1)}, bf16[128,1024]{1,0:T(8,128)(2,1)S(1)}, u32[]{:S(2)}, u32[]{:S(2)}) %collective-permute-start.5) | collective-permute-done | bytes 262176 | tf_op jit(solution)/shard_map/ppermute | solution.py:47
  65.3 0.7 copy-done.5
  66.0 0.8 copy-done.3
  66.8 1.9 %collective-permute-start.6 = (bf16[512,512]{1,0:T(8,128)(2,1)S(1)}, bf16[512,512]{1,0:T(8,128)(2,1)S(1)}, u32[]{:S(2)}, u32[]{:S(2)}) collective-permute-start(bf16[512,512]{1,0:T(8,128)(2,1)S(1)} %bitcast.74), channel_id=1, source_target_pairs={{0,1},{1,0},{2,3},{3,2},{4,5},{5,4},{6,7},{7,6},{8,9},{9,8},{10,11... | collective-permute-start | bytes 1572872 | tf_op jit(solution)/shard_map/ppermute | solution.py:19
  68.7 1.9 %collective-permute-done.6 = bf16[512,512]{1,0:T(8,128)(2,1)S(1)} collective-permute-done((bf16[512,512]{1,0:T(8,128)(2,1)S(1)}, bf16[512,512]{1,0:T(8,128)(2,1)S(1)}, u32[]{:S(2)}, u32[]{:S(2)}) %collective-permute-start.6) | collective-permute-done | bytes 524320 | tf_op jit(solution)/shard_map/ppermute | solution.py:19
  71.2 1.3 fusion.24
  72.5 1.2 constant_dynamic-update-slice_fusion.6
  75.2 20.2 %all_to_all.20 = bf16[4,512,256]{2,1,0:T(8,128)(2,1)S(1)} all-to-all(bf16[4,512,256]{2,1,0:T(8,128)(2,1)S(1)} %constant_dynamic-slice_fusion), channel_id=1, replica_groups=mesh['x'=4,'z'=16,'y'=4,'core'=2] {'y'}, dimensions={0} | all-to-all | bytes 2097152 | tf_op jit(solution)/shard_map/all_to_all | solution.py:60
  95.6 0.9 broadcast_in_dim.21
  96.5 3.5 %all-to-all-start.2 = ((bf16[4,512,128]{2,1,0:T(8,128)(2,1)}), bf16[4,512,128]{2,1,0:T(8,128)(2,1)S(1)}, u32[]{:S(2)}, u32[]{:S(2)}) async-start(bf16[4,512,128]{2,1,0:T(8,128)(2,1)} %broadcast_in_dim.21), calls=%async_computation.2 | async-start | bytes 1048576 | tf_op jit(solution)/shard_map/all_to_all | solution.py:63
  100.0 8.5 %all-to-all-done.2 = bf16[4,512,128]{2,1,0:T(8,128)(2,1)S(1)} async-done(((bf16[4,512,128]{2,1,0:T(8,128)(2,1)}), bf16[4,512,128]{2,1,0:T(8,128)(2,1)S(1)}, u32[]{:S(2)}, u32[]{:S(2)}) %all-to-all-start.2) | async-done | bytes 524320 | tf_op jit(solution)/shard_map/all_to_all | solution.py:63
  109.0 0.4 fusion.38
  109.4 0.4 fusion.36
  109.9 0.4 add_add_fusion
  110.5 1.9 %collective-permute-start.7 = (bf16[512,512]{1,0:T(8,128)(2,1)S(1)}, bf16[512,512]{1,0:T(8,128)(2,1)S(1)}, u32[]{:S(2)}, u32[]{:S(2)}) collective-permute-start(bf16[512,512]{1,0:T(8,128)(2,1)S(1)} %dynamic-slice_convert_fusion), channel_id=1, source_target_pairs={{0,1},{1,0},{2,3},{3,2},{4,5},{5,4},{6,7},{7,6},{8,9},{9,8},{10,11... | collective-permute-start | bytes 1572872 | tf_op jit(solution)/shard_map/ppermute | solution.py:19
  112.4 1.9 %collective-permute-done.7 = bf16[512,512]{1,0:T(8,128)(2,1)S(1)} collective-permute-done((bf16[512,512]{1,0:T(8,128)(2,1)S(1)}, bf16[512,512]{1,0:T(8,128)(2,1)S(1)}, u32[]{:S(2)}, u32[]{:S(2)}) %collective-permute-start.7) | collective-permute-done | bytes 524320 | tf_op jit(solution)/shard_map/ppermute | solution.py:19
  114.3 1.0 fusion.11
  115.3 15.1 %all-to-all-start.3 = ((bf16[64,8,512]{2,1,0:T(8,128)(2,1)}), bf16[64,8,512]{2,1,0:T(8,128)(2,1)S(1)}, u32[]{:S(2)}, u32[]{:S(2)}) async-start(bf16[64,8,512]{2,1,0:T(8,128)(2,1)} %fusion.11), calls=%async_computation.3 | async-start | bytes 1048576 | tf_op jit(solution)/shard_map/all_to_all | solution.py:71
  130.6 31.8 %all-to-all-done.3 = bf16[64,8,512]{2,1,0:T(8,128)(2,1)S(1)} async-done(((bf16[64,8,512]{2,1,0:T(8,128)(2,1)}), bf16[64,8,512]{2,1,0:T(8,128)(2,1)S(1)}, u32[]{:S(2)}, u32[]{:S(2)}) %all-to-all-start.3) | async-done | bytes 524320 | tf_op jit(solution)/shard_map/all_to_all | solution.py:71
  162.9 0.9 fusion.10
  (54 shorter events, 4.1 us)
Async XLA Ops:
  0.0 1.2 copy-start
  0.0 21.3 %copy-start.2 = (bf16[1,4096,128]{2,1,0:T(8,128)(2,1)S(1)}, bf16[1,4096,128]{2,1,0:T(8,128)(2,1)}, u32[]{:S(2)}) copy-start(bf16[1,4096,128]{2,1,0:T(8,128)(2,1)} %param.12) | copy-start | bytes 3145732
  2.4 63.6 %all-to-all-start = ((bf16[64,8,512]{2,1,0:T(8,128)(2,1)}), bf16[64,8,512]{2,1,0:T(8,128)(2,1)S(1)}, u32[]{:S(2)}, u32[]{:S(2)}) async-start(bf16[64,8,512]{2,1,0:T(8,128)(2,1)} %fusion), calls=%async_computation | async-start | bytes 1048576 | tf_op jit(solution)/shard_map/all_to_all | solution.py:35
  22.6 8.6 %copy-start.1 = (bf16[1,128,4096]{2,1,0:T(8,128)(2,1)S(1)}, bf16[1,128,4096]{2,1,0:T(8,128)(2,1)}, u32[]{:S(2)}) copy-start(bf16[1,128,4096]{2,1,0:T(8,128)(2,1)} %param.13) | copy-start | bytes 3145732
  22.7 42.6 %collective-permute-start = (bf16[1024,256]{1,0:T(8,128)(2,1)S(1)}, bf16[1024,256]{1,0:T(8,128)(2,1)S(1)}, u32[]{:S(2)}, u32[]{:S(2)}) collective-permute-start(bf16[1024,256]{1,0:T(8,128)(2,1)S(1)} %pad_maximum_fusion.1), channel_id=1, source_target_pairs={{0,2},{2,4},{4,6},{6,0},{1,3},{3,5},{5,7},{7,1},{8,10},{10,12},{12... | collective-permute-start | bytes 1572872 | tf_op jit(solution)/shard_map/ppermute | solution.py:46
  26.4 38.9 %collective-permute-start.1 = (bf16[1024,256]{1,0:T(8,128)(2,1)S(1)}, bf16[1024,256]{1,0:T(8,128)(2,1)S(1)}, u32[]{:S(2)}, u32[]{:S(2)}) collective-permute-start(bf16[1024,256]{1,0:T(8,128)(2,1)S(1)} %pad_maximum_fusion.2), channel_id=1, source_target_pairs={{0,4},{2,6},{4,0},{6,2},{1,5},{3,7},{5,1},{7,3},{8,12},{10,14},{12... | collective-permute-start | bytes 1572872 | tf_op jit(solution)/shard_map/ppermute | solution.py:46
  31.3 25.2 %collective-permute-start.3 = (bf16[128,1024]{1,0:T(8,128)(2,1)S(1)}, bf16[128,1024]{1,0:T(8,128)(2,1)S(1)}, u32[]{:S(2)}, u32[]{:S(2)}) collective-permute-start(bf16[128,1024]{1,0:T(8,128)(2,1)S(1)} %get-tuple-element.24), channel_id=1, source_target_pairs={{0,2},{2,4},{4,6},{6,0},{1,3},{3,5},{5,7},{7,1},{8,10},{10,12},{12... | collective-permute-start | bytes 786440 | tf_op jit(solution)/shard_map/ppermute | solution.py:47
  33.3 32.7 %collective-permute-start.2 = (bf16[1024,256]{1,0:T(8,128)(2,1)S(1)}, bf16[1024,256]{1,0:T(8,128)(2,1)}, u32[]{:S(2)}, u32[]{:S(2)}) collective-permute-start(bf16[1024,256]{1,0:T(8,128)(2,1)S(1)} %pad_maximum_fusion.3), channel_id=1, source_target_pairs={{0,6},{2,0},{4,2},{6,4},{1,7},{3,1},{5,3},{7,5},{8,14},{10,8},{12,... | collective-permute-start | bytes 1572872 | tf_op jit(solution)/shard_map/ppermute | solution.py:46
  38.5 24.3 %collective-permute-start.4 = (bf16[128,1024]{1,0:T(8,128)(2,1)S(1)}, bf16[128,1024]{1,0:T(8,128)(2,1)S(1)}, u32[]{:S(2)}, u32[]{:S(2)}) collective-permute-start(bf16[128,1024]{1,0:T(8,128)(2,1)S(1)} %get-tuple-element.26), channel_id=1, source_target_pairs={{0,4},{2,6},{4,0},{6,2},{1,5},{3,7},{5,1},{7,3},{8,12},{10,14},{12... | collective-permute-start | bytes 786440 | tf_op jit(solution)/shard_map/ppermute | solution.py:47
  56.5 4.9 %copy-start.7 = (bf16[128,1024]{1,0:T(8,128)(2,1)}, bf16[128,1024]{1,0:T(8,128)(2,1)S(1)}, u32[]{:S(2)}) copy-start(bf16[128,1024]{1,0:T(8,128)(2,1)S(1)} %collective-permute-done.3) | copy-start | bytes 786436
  56.5 8.8 %collective-permute-start.5 = (bf16[128,1024]{1,0:T(8,128)(2,1)S(1)}, bf16[128,1024]{1,0:T(8,128)(2,1)S(1)}, u32[]{:S(2)}, u32[]{:S(2)}) collective-permute-start(bf16[128,1024]{1,0:T(8,128)(2,1)S(1)} %get-tuple-element.23), channel_id=1, source_target_pairs={{0,6},{2,0},{4,2},{6,4},{1,7},{3,1},{5,3},{7,5},{8,14},{10,8},{12,... | collective-permute-start | bytes 786440 | tf_op jit(solution)/shard_map/ppermute | solution.py:47
  62.8 2.5 %copy-start.9 = (bf16[128,1024]{1,0:T(8,128)(2,1)}, bf16[128,1024]{1,0:T(8,128)(2,1)S(1)}, u32[]{:S(2)}) copy-start(bf16[128,1024]{1,0:T(8,128)(2,1)S(1)} %collective-permute-done.4) | copy-start | bytes 786436
  65.3 0.7 copy-start.5
  66.0 0.8 copy-start.3
  66.8 3.8 %collective-permute-start.6 = (bf16[512,512]{1,0:T(8,128)(2,1)S(1)}, bf16[512,512]{1,0:T(8,128)(2,1)S(1)}, u32[]{:S(2)}, u32[]{:S(2)}) collective-permute-start(bf16[512,512]{1,0:T(8,128)(2,1)S(1)} %bitcast.74), channel_id=1, source_target_pairs={{0,1},{1,0},{2,3},{3,2},{4,5},{5,4},{6,7},{7,6},{8,9},{9,8},{10,11... | collective-permute-start | bytes 1572872 | tf_op jit(solution)/shard_map/ppermute | solution.py:19
  70.9 2.8 %copy-start.4 = (bf16[1024,256]{1,0:T(8,128)(2,1)S(1)}, bf16[1024,256]{1,0:T(8,128)(2,1)}, u32[]{:S(2)}) copy-start(bf16[1024,256]{1,0:T(8,128)(2,1)} %copy-done.3) | copy-start | bytes 1572868
  95.4 13.2 %copy-start.10 = (bf16[128,1024]{1,0:T(8,128)(2,1)S(1)}, bf16[128,1024]{1,0:T(8,128)(2,1)}, u32[]{:S(2)}) copy-start(bf16[128,1024]{1,0:T(8,128)(2,1)} %copy-done.9) | copy-start | bytes 786436
  96.5 12.1 %all-to-all-start.2 = ((bf16[4,512,128]{2,1,0:T(8,128)(2,1)}), bf16[4,512,128]{2,1,0:T(8,128)(2,1)S(1)}, u32[]{:S(2)}, u32[]{:S(2)}) async-start(bf16[4,512,128]{2,1,0:T(8,128)(2,1)} %broadcast_in_dim.21), calls=%async_computation.2 | async-start | bytes 1048576 | tf_op jit(solution)/shard_map/all_to_all | solution.py:63
  100.0 9.4 %copy-start.8 = (bf16[128,1024]{1,0:T(8,128)(2,1)S(1)}, bf16[128,1024]{1,0:T(8,128)(2,1)}, u32[]{:S(2)}) copy-start(bf16[128,1024]{1,0:T(8,128)(2,1)} %copy-done.7) | copy-start | bytes 786436
  109.0 1.0 copy-start.6
  110.4 20.1 %copy-start.11 = (f32[64,1,8]{0,2,1:T(8,128)S(1)}, f32[64,1,8]{0,2,1:T(8,128)}, u32[]{:S(2)}) copy-start(f32[64,1,8]{0,2,1:T(8,128)} %param.9) | copy-start | bytes 6148
  110.4 20.2 %copy-start.12 = (s32[128]{0:T(128)S(1)}, s32[128]{0:T(128)}, u32[]{:S(2)}) copy-start(s32[128]{0:T(128)} %param.10) | copy-start | bytes 1540
  110.5 3.8 %collective-permute-start.7 = (bf16[512,512]{1,0:T(8,128)(2,1)S(1)}, bf16[512,512]{1,0:T(8,128)(2,1)S(1)}, u32[]{:S(2)}, u32[]{:S(2)}) collective-permute-start(bf16[512,512]{1,0:T(8,128)(2,1)S(1)} %dynamic-slice_convert_fusion), channel_id=1, source_target_pairs={{0,1},{1,0},{2,3},{3,2},{4,5},{5,4},{6,7},{7,6},{8,9},{9,8},{10,11... | collective-permute-start | bytes 1572872 | tf_op jit(solution)/shard_map/ppermute | solution.py:19
  115.3 47.1 %all-to-all-start.3 = ((bf16[64,8,512]{2,1,0:T(8,128)(2,1)}), bf16[64,8,512]{2,1,0:T(8,128)(2,1)S(1)}, u32[]{:S(2)}, u32[]{:S(2)}) async-start(bf16[64,8,512]{2,1,0:T(8,128)(2,1)} %fusion.11), calls=%async_computation.3 | async-start | bytes 1048576 | tf_op jit(solution)/shard_map/all_to_all | solution.py:71

commit v2 on v1

v2 whole, which is shorter than its diff:
```python
import functools

import jax
import jax.numpy as jnp
import numpy as np
from jax import lax
from jax.experimental import pallas as pl
from jax.experimental.pallas import tpu as pltpu
from jax.sharding import Mesh, PartitionSpec as P

E = ("x", "z")
S = ("y", "core")
NY = 4
HS = 128
BF = jnp.bfloat16
F32 = jnp.float32
HINT = 60 * 10**9
VMEM_LIMIT = 32 * 1024 * 1024
WHOLE = 60 * 1024 * 1024

SMEM = pl.BlockSpec(memory_space=pltpu.SMEM)
VMEM = pl.BlockSpec(memory_space=pltpu.VMEM)
ANY = pl.BlockSpec(memory_space=pl.ANY)


def dot(a, b):
    return jnp.dot(a, b, preferred_element_type=F32)


def call(kernel, out_shape, in_specs, out_specs, flops=0, bytes_accessed=1 << 20, vmem=VMEM_LIMIT, **more):
    return pl.pallas_call(
        kernel,
        out_shape=out_shape,
        in_specs=in_specs,
        out_specs=out_specs,
        compiler_params=pltpu.CompilerParams(vmem_limit_bytes=vmem),
        cost_estimate=pl.CostEstimate(flops=flops, bytes_accessed=bytes_accessed, transcendentals=0),
        **more,
    )


def swap_cores(a):
    return lax.ppermute(a, "core", [(0, 1), (1, 0)])


def block_copies(to, gate, up, down, out, sems):
    group = out.shape[1]
    first = pl.multiple_of(to * group, group)
    copies = [
        pltpu.make_async_copy(gate.at[pl.ds(first, group)], out.at[0], sems.at[0]),
        pltpu.make_async_copy(up.at[pl.ds(first, group)], out.at[1], sems.at[1]),
    ]
    for j in range(group // HS):
        column = pl.multiple_of(first + j * HS, HS)
        copies.append(
            pltpu.make_async_copy(
                down.at[:, pl.ds(column, HS)], out.at[2, pl.ds(j * HS, HS)], sems.at[2 + j]
            )
        )
    return copies


def spread(values, rows):
    slots, experts = values.shape
    lane = lax.broadcasted_iota(jnp.int32, (experts, rows), 1)
    expert = lax.broadcasted_iota(jnp.int32, (experts, rows), 0)
    wide = dot(values.astype(BF), (lane // slots == expert).astype(BF))
    lane = lax.broadcasted_iota(jnp.int32, (slots, rows), 1)
    slot = lax.broadcasted_iota(jnp.int32, (slots, rows), 0)
    return jnp.sum(jnp.where(lane % slots == slot, wide, 0.0), axis=0, keepdims=True)


def start_kernel(at, slots, tokens, gate, up, down, picked, b1, b2, b3, own, sems, own_sem):
    width = own.shape[1]
    local_tokens = tokens.shape[0]
    first = pl.multiple_of((at[0] * 2 + at[1]) * width, width)
    fetch = pltpu.make_async_copy(tokens.at[:, pl.ds(first, width)], own, own_sem)
    fetch.start()
    copies = []
    for d, out in ((2, b2), (1, b1), (3, b3)):
        copies += block_copies(lax.rem(at[0] + d, NY), gate, up, down, out, sems.at[d - 1])
    for copy in copies:
        copy.start()
    rows = picked.shape[0]
    names = spread(slots[...].astype(F32), rows)
    token = lax.broadcasted_iota(jnp.int32, (local_tokens, rows), 0).astype(F32)
    hit = (names == token).astype(BF)
    fetch.wait()
    picked[...] = lax.dot_general(
        hit, own[...], (((0,), (0,)), ((), ())), preferred_element_type=F32
    ).astype(BF)
    for copy in copies:
        copy.wait()


def start(at, slots, tokens, gate, up, down):
    group = gate.shape[0] // NY
    width = tokens.shape[1] // (2 * NY)
    rows = slots.shape[0] * slots.shape[1]
    block = jax.ShapeDtypeStruct((3, group, HS), BF)
    return call(
        start_kernel,
        (jax.ShapeDtypeStruct((rows, width), BF), block, block, block),
        [SMEM, VMEM, ANY, ANY, ANY, ANY],
        (VMEM, VMEM, VMEM, VMEM),
        bytes_accessed=5 << 20,
        vmem=WHOLE,
        scratch_shapes=[
            pltpu.VMEM((tokens.shape[0], width), BF),
            pltpu.SemaphoreType.DMA((NY - 1, 2 + group // HS)),
            pltpu.SemaphoreType.DMA,
        ],
    )(at, slots, tokens, gate, up, down)


def own_block_kernel(at, gate, up, down, out, sems):
    copies = block_copies(at[0], gate, up, down, out, sems)
    for copy in copies:
        copy.start()
    for copy in copies:
        copy.wait()


def own_block(at, gate, up, down):
    group = gate.shape[0] // NY
    return call(
        own_block_kernel,
        jax.ShapeDtypeStruct((3, group, HS), BF),
        [SMEM, ANY, ANY, ANY],
        VMEM,
        vmem=WHOLE,
        scratch_shapes=[pltpu.SemaphoreType.DMA((2 + group // HS,))],
    )(at, gate, up, down)


def ready_kernel(first, second, out, sem):
    copy = pltpu.make_async_copy(first.at[0, pl.ds(0, out.shape[0])], out, sem)
    copy.start()
    copy.wait()


def ready(first, second):
    return call(
        ready_kernel,
        jax.ShapeDtypeStruct((16, HS), BF),
        [ANY, ANY],
        VMEM,
        flops=HINT,
        scratch_shapes=[pltpu.SemaphoreType.DMA],
    )(first, second)


def partial_kernel(distances, at, own, other, *refs):
    blocks, out = refs[: len(distances)], refs[-1]
    rows, width = own.shape
    step = 256
    mine = pl.multiple_of(at[1] * width, width)
    theirs = pl.multiple_of((1 - at[1]) * width, width)
    for d, w in zip(distances, blocks):
        owner = lax.rem(at[0] + NY - d, NY)
        a = jnp.concatenate([w[0, pl.ds(mine, width)], w[1, pl.ds(mine, width)]], axis=1)
        b = jnp.concatenate([w[0, pl.ds(theirs, width)], w[1, pl.ds(theirs, width)]], axis=1)
        for r in range(0, rows, step):
            total = dot(own[pl.ds(r, step)], a) + dot(other[pl.ds(r, step)], b)
            out[owner, pl.ds(r, step)] = total.astype(BF)


def partial_sums(at, own, other, blocks, distances, last):
    rows, width = own.shape
    operands = [at, own, other] + [blocks[d] for d in distances]
    specs = [SMEM] + [VMEM] * (len(operands) - 1)
    more = {}
    if last[0].shape == (NY, rows, 2 * HS):
        more = {"input_output_aliases": {len(operands): 0}}
    operands += last
    specs.append(VMEM)
    return call(
        functools.partial(partial_kernel, distances),
        jax.ShapeDtypeStruct((NY, rows, 2 * HS), BF),
        specs,
        VMEM,
        flops=2 * rows * 2 * width * len(distances) * 2 * HS,
        **more,
    )(*operands)


def hidden_kernel(sums, out):
    total = sums[0].astype(F32)
    for k in range(1, NY):
        total = total + sums[k].astype(F32)
    gate, up = total[:, :HS], total[:, HS:]
    hidden = (gate / (1.0 + jnp.exp(-gate)) * up).astype(BF)
    for k in range(NY):
        out[k] = hidden


def hidden_copies(sums):
    return call(
        hidden_kernel, jax.ShapeDtypeStruct((NY, sums.shape[1], HS), BF), [VMEM], VMEM
    )(sums)


def out_kernel(mine, at, hidden, w0, w1, w2, w3, out):
    rows = hidden.shape[1]
    width = out.shape[1]
    step = 256
    first = (at[1] if mine else 1 - at[1]) * width
    owners = [lax.rem(at[0] + NY - d, NY) for d in range(NY)]
    for j in range(0, width, 2 * HS):
        one = pl.multiple_of(first + j, HS)
        two = pl.multiple_of(first + j + HS, HS)
        b = jnp.concatenate(
            [
                jnp.concatenate([w[2, pl.ds(one, HS)], w[2, pl.ds(two, HS)]], axis=1)
                for w in (w0, w1, w2, w3)
            ],
            axis=0,
        )
        for r in range(0, rows, step):
            a = jnp.concatenate([hidden[k, pl.ds(r, step)] for k in owners], axis=1)
            out[pl.ds(r, step), pl.ds(j, 2 * HS)] = dot(a, b).astype(out.dtype)


def out_sums(at, hidden, blocks, width, mine):
    rows = hidden.shape[1]
    return call(
        functools.partial(out_kernel, mine),
        jax.ShapeDtypeStruct((rows, width), F32 if mine else BF),
        [SMEM] + [VMEM] * 5,
        VMEM,
        flops=2 * rows * width * NY * HS,
    )(at, hidden, *blocks)


def local(tokens, slot_lists, slot_gates, counts, gate_weight, up_weight, down_weight):
    y = lax.axis_index("y")
    c = lax.axis_index("core")
    at = jnp.stack([y, c]).astype(jnp.int32)
    width = tokens.shape[1] // (2 * NY)
    rows = slot_lists.shape[0] * slot_lists.shape[2]
    local_tokens = tokens.shape[0]
    gate_weight, up_weight, down_weight = gate_weight[0], up_weight[0], down_weight[0]

    slots = slot_lists.transpose(2, 1, 0).reshape(slot_lists.shape[2], slot_lists.shape[0])
    picked, *sent = start(at, slots, tokens, gate_weight, up_weight, down_weight)
    arrived = lax.all_to_all(picked.reshape(-1, 8, width), E, 0, 0, tiled=True).reshape(rows, width)
    blocks = [own_block(at, gate_weight, up_weight, down_weight)]
    for d in range(1, NY):
        blocks.append(lax.ppermute(sent[d - 1], "y", [(j, (j + d) % NY) for j in range(NY)]))
    arrived, early = lax.optimization_barrier((arrived, ready(blocks[0], blocks[2])))
    other = swap_cores(arrived)
    parts = partial_sums(at, arrived, other, blocks, (0, 2, 1), (early,))
    parts = partial_sums(at, arrived, other, blocks, (3,), (parts,))
    sums = lax.all_to_all(parts, "y", 0, 0, tiled=True)
    gathered = lax.all_to_all(hidden_copies(sums), "y", 0, 0, tiled=True)
    give = swap_cores(out_sums(at, gathered, blocks, width, False))
    keep = out_sums(at, gathered, blocks, width, True)
    result = (keep + give.astype(F32)).astype(BF)
    returned = lax.all_to_all(result.reshape(-1, 8, width), E, 0, 0, tiled=True).reshape(rows, width)

    hit = slot_lists.reshape(1, rows) == lax.broadcasted_iota(jnp.int32, (local_tokens, rows), 0)
    weight = jnp.where(hit, slot_gates.reshape(1, rows), 0.0)
    totals = 0.0
    for _ in range(3):
        piece = weight.astype(BF)
        weight = weight - piece.astype(F32)
        totals = totals + dot(piece, returned)
    divisor = jnp.maximum(counts.astype(F32), 1.0)
    return (totals / divisor[:, None]).astype(BF)


def solution(mesh):
    fine = Mesh(np.asarray(mesh.devices).reshape(4, 16, NY, 2), ("x", "z", "y", "core"))
    return jax.shard_map(
        local,
        mesh=fine,
        in_specs=(
            P(E, None),
            P(None, E, None),
            P(None, E, None),
            P(E),
            P(E, None, S),
            P(E, None, S),
            P(E, S, None),
        ),
        out_specs=P(E, S),
        check_vma=False,
    )
```

time: 164 us -> 145 us (0.88)
  starting transfers between devices: 63.5 us -> 42.1 us
  Pallas kernels: 0 us -> 12.9 us
  waiting for transfers between devices: 63.9 us -> 53.5 us
  blocking collectives: 20.2 us -> 29.7 us
  matrix products: 8.54 us -> 1.36 us
  local copies, waits for them, and re-layouts: 5.61 us -> 2.64 us
    all_to_all x1, waiting for transfers between devices: 0.01 us -> 20.1 us  [local(): lax.all_to_all(picked.reshape(-1, 8, width), E, 0, 0, tiled=True)]
    ppermute x6 -> x3, waiting for transfers between devices: 19.9 us -> 0.01 us  [local(): lax.ppermute(sent[d - 1], 'y', [(j, (j + d) % NY) for j in range(NY)])]
    pallas_call x0 -> x8, Pallas kernels: none -> 12.9 us  [the longest x1 4.56 us: start(): call(start_kernel, (jax.ShapeDtypeStruct((rows, width), BF), block, block...]
    ppermute x6 -> x3, starting transfers between devices: 22.3 us -> 12.1 us  [local(): lax.ppermute(sent[d - 1], 'y', [(j, (j + d) % NY) for j in range(NY)])]
    all_to_all x1 -> x2, blocking collectives: 20.2 us -> 29.7 us  [the longest x1 18.1 us: local(): sums = lax.all_to_all(parts, 'y', 0, 0, tiled=True)]
    all_to_all x1 -> x0, waiting for transfers between devices: 8.5 us -> none  [local(): lax.all_to_all(jnp.broadcast_to(hidden, (NY,) + hidden.shape), 'y', 0, 0,...]
    all_to_all x1, starting transfers between devices: 15.1 us -> 7.08 us  [local(): lax.all_to_all(result.reshape(-1, 8, width), E, 0, 0, tiled=True)]
    dot_general x16 -> x3, matrix products: 8.54 us -> 1.36 us  [dot(): return jnp.dot(a, b, preferred_element_type=F32)]
  transfers between devices with their start and end apart: 11 -> 7, of which waited for: 7 -> 4; matrix products, arithmetic and copies ran while one was open for 1% -> 0% of each run, Pallas kernels for 0% -> 4%
where the time goes in v2:
time: 145 us; the launch traced here: 144 us
  waiting for transfers between devices  53.5 us (37%)
  starting transfers between devices  42.1 us (29%)
  blocking collectives  29.7 us (20%)
  Pallas kernels  12.9 us (9%)
  local copies, waits for them, and re-layouts  2.64 us (2%)
  other arithmetic  1.54 us (1%)
    all_to_all x1, waiting for transfers between devices, local(): lax.all_to_all(result.reshape(-1, 8, width), E, 0, 0, tiled=True)  30.4 us
    all_to_all x1, waiting for transfers between devices, local(): lax.all_to_all(picked.reshape(-1, 8, width), E, 0, 0, tiled=True)  20.1 us
    all_to_all x1, starting transfers between devices, local(): lax.all_to_all(picked.reshape(-1, 8, width), E, 0, 0, tiled=True)  19 us
    all_to_all x1, blocking collectives, local(): sums = lax.all_to_all(parts, 'y', 0, 0, tiled=True)  18.1 us
    ppermute x3, starting transfers between devices, local(): lax.ppermute(sent[d - 1], 'y', [(j, (j + d) % NY) for j in range(NY)])  12.1 us
    all_to_all x1, blocking collectives, local(): gathered = lax.all_to_all(hidden_copies(sums), 'y', 0, 0, tiled=True)  11.6 us
    all_to_all x1, starting transfers between devices, local(): lax.all_to_all(result.reshape(-1, 8, width), E, 0, 0, tiled=True)  7.08 us
    pallas_call x1, Pallas kernels, start(): call(start_kernel, (jax.ShapeDtypeStruct((rows, width), BF), block, block...  4.56 us
  transfers between devices with their start and end apart: 7, of which 4 were waited for; matrix products, arithmetic and copies ran while one was open for 0% of the time, Pallas kernels for 4%

profile of v2, /device:TPU:6, one launch (start us, length us, event | category | flops | bytes accessed | tf_op | source)
XLA Modules:
  0.0 143.9 jit_solution(3456478675741672066)
XLA Ops:
  0.0 0.6 pad_add_fusion.at
  0.6 4.6 %shard_map.73 = (bf16[512,512]{1,0:T(8,128)(2,1)}, bf16[3,1024,128]{2,1,0:T(8,128)(2,1)}, bf16[3,1024,128]{2,1,0:T(8,128)(2,1)}, bf16[3,1024,128]{2,1,0:T(8,128)(2,1)}) custom-call(s32[2]{0:T(128)} %pad_add_fusion.at, s32[8,64]{1,0:T(8,128)} %bitcast.30, bf16[128,4096]{1,0:T(8,128)(2,1)} %tokens.1, bf16[4096,128]{1,0:T(8,128)(2,1)} %bitcast.23, ...), custom_call_target="tpu_custom_call" | custom-call | bytes 5242880 | tf_op jit(solution)/shard_map/pallas_call | solution.py:101
  5.2 5.1 %collective-permute-start = (bf16[3,1024,128]{2,1,0:T(8,128)(2,1)}, bf16[3,1024,128]{2,1,0:T(8,128)(2,1)S(1)}, u32[]{:S(2)}, u32[]{:S(2)}) collective-permute-start(bf16[3,1024,128]{2,1,0:T(8,128)(2,1)} %get-tuple-element.12), channel_id=1, source_target_pairs={{0,4},{2,6},{4,0},{6,2},{1,5},{3,7},{5,1},{7,3},{8,12},{10,14},{12... | collective-permute-start | bytes 2359304 | tf_op jit(solution)/shard_map/ppermute | solution.py:249
  10.3 19.0 %all-to-all-start = ((bf16[64,8,512]{2,1,0:T(8,128)(2,1)}), bf16[64,8,512]{2,1,0:T(8,128)(2,1)}, u32[]{:S(2)}, u32[]{:S(2)}) async-start(bf16[64,8,512]{2,1,0:T(8,128)(2,1)} %bitcast.29), calls=%async_computation | async-start | bytes 1048576 | tf_op jit(solution)/shard_map/all_to_all | solution.py:246
  29.3 2.6 %collective-permute-start.3 = (bf16[3,1024,128]{2,1,0:T(8,128)(2,1)}, bf16[3,1024,128]{2,1,0:T(8,128)(2,1)S(1)}, u32[]{:S(2)}, u32[]{:S(2)}) collective-permute-start(bf16[3,1024,128]{2,1,0:T(8,128)(2,1)} %get-tuple-element.15), channel_id=1, source_target_pairs={{0,2},{2,4},{4,6},{6,0},{1,3},{3,5},{5,7},{7,1},{8,10},{10,12},{12... | collective-permute-start | bytes 2359304 | tf_op jit(solution)/shard_map/ppermute | solution.py:249
  31.9 4.5 %collective-permute-start.2 = (bf16[3,1024,128]{2,1,0:T(8,128)(2,1)}, bf16[3,1024,128]{2,1,0:T(8,128)(2,1)S(1)}, u32[]{:S(2)}, u32[]{:S(2)}) collective-permute-start(bf16[3,1024,128]{2,1,0:T(8,128)(2,1)} %get-tuple-element.14), channel_id=1, source_target_pairs={{0,6},{2,0},{4,2},{6,4},{1,7},{3,1},{5,3},{7,5},{8,14},{10,8},{12,... | collective-permute-start | bytes 2359304 | tf_op jit(solution)/shard_map/ppermute | solution.py:249
  36.3 2.7 %shard_map.74.first.refs_0_.w0 = bf16[3,1024,128]{2,1,0:T(8,128)(2,1)} custom-call(s32[2]{0:T(128)} %pad_add_fusion.at, bf16[4096,128]{1,0:T(8,128)(2,1)} %bitcast.24, bf16[4096,128]{1,0:T(8,128)(2,1)} %bitcast.26, bf16[128,4096]{1,0:T(8,128)(2,1)} %bitcast.28), custom_call_target="tpu_custom_call" | custom-call | bytes 1048576 | tf_op jit(solution)/shard_map/pallas_call | solution.py:126
  39.1 1.1 copy-done
  40.2 20.1 %all-to-all-done = bf16[64,8,512]{2,1,0:T(8,128)(2,1)} async-done(((bf16[64,8,512]{2,1,0:T(8,128)(2,1)}), bf16[64,8,512]{2,1,0:T(8,128)(2,1)}, u32[]{:S(2)}, u32[]{:S(2)}) %all-to-all-start) | async-done | bytes 524320 | tf_op jit(solution)/shard_map/all_to_all | solution.py:246
  60.3 1.9 %collective-permute-start.1 = (bf16[512,512]{1,0:T(8,128)(2,1)}, bf16[512,512]{1,0:T(8,128)(2,1)S(1)}, u32[]{:S(2)}, u32[]{:S(2)}) collective-permute-start(bf16[512,512]{1,0:T(8,128)(2,1)} %bitcast.8.own), channel_id=1, source_target_pairs={{0,1},{1,0},{2,3},{3,2},{4,5},{5,4},{6,7},{7,6},{8,9},{9,8},{10,11... | collective-permute-start | bytes 1572872 | tf_op jit(solution)/shard_map/ppermute | solution.py:43
  62.2 2.1 %collective-permute-done.1.other = bf16[512,512]{1,0:T(8,128)(2,1)S(1)} collective-permute-done((bf16[512,512]{1,0:T(8,128)(2,1)}, bf16[512,512]{1,0:T(8,128)(2,1)S(1)}, u32[]{:S(2)}, u32[]{:S(2)}) %collective-permute-start.1) | collective-permute-done | bytes 524320 | tf_op jit(solution)/shard_map/ppermute | solution.py:43
  64.3 2.0 %shard_map.76.refs_1_ = bf16[4,512,256]{2,1,0:T(8,128)(2,1)S(1)} custom-call(s32[2]{0:T(128)S(1)} %copy-done.2, bf16[512,512]{1,0:T(8,128)(2,1)} %bitcast.8.own, bf16[512,512]{1,0:T(8,128)(2,1)S(1)} %collective-permute-done.1.other, bf16[3,1024,128]{2,1,0:T(8,128)(2,1)S(1)} %copy-done.1, bf16[3,1024,128]{2,1,0:T(8,128)(2,1)S(1)} %collective-permute-done.second.refs_1_.w2, ...), custom_call_target="tpu_custom_call" | custom-call | flops 805306368 | bytes 1048576 | tf_op jit(solution)/shard_map/pallas_call | solution.py:177
  66.4 1.5 %shard_map.77 = bf16[4,512,256]{2,1,0:T(8,128)(2,1)S(1)} custom-call(s32[2]{0:T(128)S(1)} %copy-done.2, bf16[512,512]{1,0:T(8,128)(2,1)} %bitcast.8.own, bf16[512,512]{1,0:T(8,128)(2,1)S(1)} %collective-permute-done.1.other, bf16[3,1024,128]{2,1,0:T(8,128)(2,1)S(1)} %collective-permute-done.2.refs_0_.w3, ...), custom_call_target="tpu_custom_call", output_to_operand_aliasing={{}: (4, {})} | custom-call | flops 268435456 | bytes 1048576 | tf_op jit(solution)/shard_map/pallas_call | solution.py:177
  67.9 18.1 %all_to_all.20.sums = bf16[4,512,256]{2,1,0:T(8,128)(2,1)S(1)} all-to-all(bf16[4,512,256]{2,1,0:T(8,128)(2,1)S(1)} %shard_map.77), channel_id=1, replica_groups=mesh['x'=4,'z'=16,'y'=4,'core'=2] {'y'}, dimensions={0} | all-to-all | bytes 2097152 | tf_op jit(solution)/shard_map/all_to_all | solution.py:254
  85.9 0.2 shard_map.78
  86.1 11.6 %all_to_all.21.hidden = bf16[4,512,128]{2,1,0:T(8,128)(2,1)S(1)} all-to-all(bf16[4,512,128]{2,1,0:T(8,128)(2,1)S(1)} %shard_map.78), channel_id=1, replica_groups=mesh['x'=4,'z'=16,'y'=4,'core'=2] {'y'}, dimensions={0} | all-to-all | bytes 1048576 | tf_op jit(solution)/shard_map/all_to_all | solution.py:255
  97.8 1.0 shard_map.80
  98.8 1.9 %collective-permute-start.4 = (bf16[512,512]{1,0:T(8,128)(2,1)S(1)}, bf16[512,512]{1,0:T(8,128)(2,1)S(1)}, u32[]{:S(2)}, u32[]{:S(2)}) collective-permute-start(bf16[512,512]{1,0:T(8,128)(2,1)S(1)} %shard_map.80), channel_id=1, source_target_pairs={{0,1},{1,0},{2,3},{3,2},{4,5},{5,4},{6,7},{7,6},{8,9},{9,8},{10,11... | collective-permute-start | bytes 1572872 | tf_op jit(solution)/shard_map/ppermute | solution.py:43
  100.7 1.0 shard_map.79
  101.7 0.9 collective-permute-done.4
  102.6 0.9 fusion.2
  103.5 7.1 %all-to-all-start.3 = ((bf16[64,8,512]{2,1,0:T(8,128)(2,1)}), bf16[64,8,512]{2,1,0:T(8,128)(2,1)S(1)}, u32[]{:S(2)}, u32[]{:S(2)}) async-start(bf16[64,8,512]{2,1,0:T(8,128)(2,1)} %fusion.2), calls=%async_computation.3 | async-start | bytes 1048576 | tf_op jit(solution)/shard_map/all_to_all | solution.py:259
  110.6 0.1 copy.9
  110.7 0.6 copy-done.4
  111.3 0.1 copy.10
  111.4 0.1 broadcast_in_dim.15
  111.5 0.1 eq.10
  111.6 0.6 copy-done.5
  112.1 30.4 %all-to-all-done.3 = bf16[64,8,512]{2,1,0:T(8,128)(2,1)S(1)} async-done(((bf16[64,8,512]{2,1,0:T(8,128)(2,1)}), bf16[64,8,512]{2,1,0:T(8,128)(2,1)S(1)}, u32[]{:S(2)}, u32[]{:S(2)}) %all-to-all-start.3) | async-done | bytes 524320 | tf_op jit(solution)/shard_map/all_to_all | solution.py:259
  142.6 0.2 fusion.5
  142.8 0.2 convolution_add_fusion.1
  143.0 0.9 fusion.1
  (14 shorter events, 0.0 us)
Async XLA Ops:
  5.2 33.9 %collective-permute-start = (bf16[3,1024,128]{2,1,0:T(8,128)(2,1)}, bf16[3,1024,128]{2,1,0:T(8,128)(2,1)S(1)}, u32[]{:S(2)}, u32[]{:S(2)}) collective-permute-start(bf16[3,1024,128]{2,1,0:T(8,128)(2,1)} %get-tuple-element.12), channel_id=1, source_target_pairs={{0,4},{2,6},{4,0},{6,2},{1,5},{3,7},{5,1},{7,3},{8,12},{10,14},{12... | collective-permute-start | bytes 2359304 | tf_op jit(solution)/shard_map/ppermute | solution.py:249
  10.3 50.0 %all-to-all-start = ((bf16[64,8,512]{2,1,0:T(8,128)(2,1)}), bf16[64,8,512]{2,1,0:T(8,128)(2,1)}, u32[]{:S(2)}, u32[]{:S(2)}) async-start(bf16[64,8,512]{2,1,0:T(8,128)(2,1)} %bitcast.29), calls=%async_computation | async-start | bytes 1048576 | tf_op jit(solution)/shard_map/all_to_all | solution.py:246
  29.3 33.0 %collective-permute-start.3 = (bf16[3,1024,128]{2,1,0:T(8,128)(2,1)}, bf16[3,1024,128]{2,1,0:T(8,128)(2,1)S(1)}, u32[]{:S(2)}, u32[]{:S(2)}) collective-permute-start(bf16[3,1024,128]{2,1,0:T(8,128)(2,1)} %get-tuple-element.15), channel_id=1, source_target_pairs={{0,2},{2,4},{4,6},{6,0},{1,3},{3,5},{5,7},{7,1},{8,10},{10,12},{12... | collective-permute-start | bytes 2359304 | tf_op jit(solution)/shard_map/ppermute | solution.py:249
  31.9 34.5 %collective-permute-start.2 = (bf16[3,1024,128]{2,1,0:T(8,128)(2,1)}, bf16[3,1024,128]{2,1,0:T(8,128)(2,1)S(1)}, u32[]{:S(2)}, u32[]{:S(2)}) collective-permute-start(bf16[3,1024,128]{2,1,0:T(8,128)(2,1)} %get-tuple-element.14), channel_id=1, source_target_pairs={{0,6},{2,0},{4,2},{6,4},{1,7},{3,1},{5,3},{7,5},{8,14},{10,8},{12,... | collective-permute-start | bytes 2359304 | tf_op jit(solution)/shard_map/ppermute | solution.py:249
  39.0 1.1 copy-start
  40.2 24.1 %copy-start.1 = (bf16[3,1024,128]{2,1,0:T(8,128)(2,1)S(1)}, bf16[3,1024,128]{2,1,0:T(8,128)(2,1)}, u32[]{:S(2)}) copy-start(bf16[3,1024,128]{2,1,0:T(8,128)(2,1)} %shard_map.74.first.refs_0_.w0) | copy-start | bytes 2359300
  40.2 24.1 %copy-start.2 = (s32[2]{0:T(128)S(1)}, s32[2]{0:T(128)}, u32[]{:S(2)}) copy-start(s32[2]{0:T(128)} %pad_add_fusion.at) | copy-start | bytes 28
  60.3 4.0 %collective-permute-start.1 = (bf16[512,512]{1,0:T(8,128)(2,1)}, bf16[512,512]{1,0:T(8,128)(2,1)S(1)}, u32[]{:S(2)}, u32[]{:S(2)}) collective-permute-start(bf16[512,512]{1,0:T(8,128)(2,1)} %bitcast.8.own), channel_id=1, source_target_pairs={{0,1},{1,0},{2,3},{3,2},{4,5},{5,4},{6,7},{7,6},{8,9},{9,8},{10,11... | collective-permute-start | bytes 1572872 | tf_op jit(solution)/shard_map/ppermute | solution.py:43
  98.8 3.8 %collective-permute-start.4 = (bf16[512,512]{1,0:T(8,128)(2,1)S(1)}, bf16[512,512]{1,0:T(8,128)(2,1)S(1)}, u32[]{:S(2)}, u32[]{:S(2)}) collective-permute-start(bf16[512,512]{1,0:T(8,128)(2,1)S(1)} %shard_map.80), channel_id=1, source_target_pairs={{0,1},{1,0},{2,3},{3,2},{4,5},{5,4},{6,7},{7,6},{8,9},{9,8},{10,11... | collective-permute-start | bytes 1572872 | tf_op jit(solution)/shard_map/ppermute | solution.py:43
  103.5 7.1 %copy-start.3 = (s32[64,1,8]{0,2,1:T(8,128)S(1)}, s32[64,1,8]{0,2,1:T(8,128)}, u32[]{:S(2)}) copy-start(s32[64,1,8]{0,2,1:T(8,128)} %param.8) | copy-start | bytes 6148
  103.5 39.1 %all-to-all-start.3 = ((bf16[64,8,512]{2,1,0:T(8,128)(2,1)}), bf16[64,8,512]{2,1,0:T(8,128)(2,1)S(1)}, u32[]{:S(2)}, u32[]{:S(2)}) async-start(bf16[64,8,512]{2,1,0:T(8,128)(2,1)} %fusion.2), calls=%async_computation.3 | async-start | bytes 1048576 | tf_op jit(solution)/shard_map/all_to_all | solution.py:259
  110.6 0.7 copy-start.4
  111.5 0.7 copy-start.5

commit v3 on v2

v3 whole, which is shorter than its diff:
```python
import functools

import jax
import jax.numpy as jnp
import numpy as np
from jax import lax
from jax.experimental import pallas as pl
from jax.experimental.pallas import tpu as pltpu
from jax.sharding import Mesh, PartitionSpec as P

E = ("x", "z")
S = ("y", "core")
NY = 4
HS = 128
BF = jnp.bfloat16
F32 = jnp.float32
HINT = 60 * 10**9
VMEM_LIMIT = 32 * 1024 * 1024
WHOLE = 60 * 1024 * 1024

SMEM = pl.BlockSpec(memory_space=pltpu.SMEM)
VMEM = pl.BlockSpec(memory_space=pltpu.VMEM)
ANY = pl.BlockSpec(memory_space=pl.ANY)


def dot(a, b):
    return jnp.dot(a, b, preferred_element_type=F32)


def call(kernel, out_shape, in_specs, out_specs, flops=0, bytes_accessed=1 << 20, vmem=VMEM_LIMIT, **more):
    return pl.pallas_call(
        kernel,
        out_shape=out_shape,
        in_specs=in_specs,
        out_specs=out_specs,
        compiler_params=pltpu.CompilerParams(vmem_limit_bytes=vmem),
        cost_estimate=pl.CostEstimate(flops=flops, bytes_accessed=bytes_accessed, transcendentals=0),
        **more,
    )


def swap_cores(a):
    return lax.ppermute(a, "core", [(0, 1), (1, 0)])


def block_copies(to, gate, up, down, out, sems):
    group = out.shape[1]
    first = pl.multiple_of(to * group, group)
    copies = [
        pltpu.make_async_copy(gate.at[pl.ds(first, group)], out.at[0], sems.at[0]),
        pltpu.make_async_copy(up.at[pl.ds(first, group)], out.at[1], sems.at[1]),
    ]
    for j in range(group // HS):
        column = pl.multiple_of(first + j * HS, HS)
        copies.append(
            pltpu.make_async_copy(
                down.at[:, pl.ds(column, HS)], out.at[2, pl.ds(j * HS, HS)], sems.at[2 + j]
            )
        )
    return copies


def spread(values, rows):
    slots, experts = values.shape
    lane = lax.broadcasted_iota(jnp.int32, (experts, rows), 1)
    expert = lax.broadcasted_iota(jnp.int32, (experts, rows), 0)
    wide = dot(values.astype(BF), (lane // slots == expert).astype(BF))
    lane = lax.broadcasted_iota(jnp.int32, (slots, rows), 1)
    slot = lax.broadcasted_iota(jnp.int32, (slots, rows), 0)
    return jnp.sum(jnp.where(lane % slots == slot, wide, 0.0), axis=0, keepdims=True)


def position():
    return lax.axis_index("y"), lax.axis_index("core")


def start_kernel(far, slots, tokens, gate, up, down, picked, block, own, rows_out, held, sems, own_sem, out_sems):
    y, c = position()
    width = own.shape[1]
    local_tokens = tokens.shape[0]
    first = pl.multiple_of((y * 2 + c) * width, width)
    fetch = pltpu.make_async_copy(tokens.at[:, pl.ds(first, width)], own, own_sem)
    fetch.start()
    copies = block_copies(lax.rem(y + far, NY), gate, up, down, held, sems)
    for copy in copies:
        copy.start()
    rows = picked.shape[0]
    names = spread(slots[...].astype(F32), rows)
    token = lax.broadcasted_iota(jnp.int32, (local_tokens, rows), 0).astype(F32)
    hit = (names == token).astype(BF)
    fetch.wait()
    for copy in copies:
        copy.wait()
    send = pltpu.make_async_copy(held, block, out_sems.at[0])
    send.start()
    sends = [send]
    step = rows // 2
    for n in range(2):
        part = pl.ds(n * step, step)
        rows_out[part] = lax.dot_general(
            hit[:, n * step : (n + 1) * step], own[...], (((0,), (0,)), ((), ())), preferred_element_type=F32
        ).astype(BF)
        send = pltpu.make_async_copy(rows_out.at[part], picked.at[part], out_sems.at[1 + n])
        send.start()
        sends.append(send)
    for send in sends:
        send.wait()


def start(far, slots, tokens, gate, up, down):
    group = gate.shape[0] // NY
    width = tokens.shape[1] // (2 * NY)
    rows = slots.shape[0] * slots.shape[1]
    return call(
        functools.partial(start_kernel, far),
        (jax.ShapeDtypeStruct((rows, width), BF), jax.ShapeDtypeStruct((3, group, HS), BF)),
        [VMEM, ANY, ANY, ANY, ANY],
        (ANY, ANY),
        bytes_accessed=5 << 20,
        vmem=WHOLE,
        scratch_shapes=[
            pltpu.VMEM((tokens.shape[0], width), BF),
            pltpu.VMEM((rows, width), BF),
            pltpu.VMEM((3, group, HS), BF),
            pltpu.SemaphoreType.DMA((2 + group // HS,)),
            pltpu.SemaphoreType.DMA,
            pltpu.SemaphoreType.DMA((3,)),
        ],
    )(slots, tokens, gate, up, down)


def pack_kernel(d, gate, up, down, out, sems):
    copies = block_copies(lax.rem(position()[0] + d, NY), gate, up, down, out, sems)
    for copy in copies:
        copy.start()
    for copy in copies:
        copy.wait()


def pack(d, gate, up, down):
    group = gate.shape[0] // NY
    return call(
        functools.partial(pack_kernel, d),
        jax.ShapeDtypeStruct((3, group, HS), BF),
        [ANY, ANY, ANY],
        VMEM,
        vmem=WHOLE,
        scratch_shapes=[pltpu.SemaphoreType.DMA((2 + group // HS,))],
    )(gate, up, down)


def ready_kernel(first, second, out, sem):
    copy = pltpu.make_async_copy(first.at[0, pl.ds(0, out.shape[0])], out, sem)
    copy.start()
    copy.wait()


def ready(first, second):
    return call(
        ready_kernel,
        jax.ShapeDtypeStruct((16, HS), BF),
        [ANY, ANY],
        VMEM,
        flops=HINT,
        scratch_shapes=[pltpu.SemaphoreType.DMA],
    )(first, second)


def partial_kernel(own_ref, other, w0, w1, w2, w3, early, out, own, sem):
    fetch = pltpu.make_async_copy(own_ref, own, sem)
    fetch.start()
    y, c = position()
    rows, width = own.shape
    step = 256
    mine = pl.multiple_of(c * width, width)
    theirs = pl.multiple_of((1 - c) * width, width)
    for d, w in enumerate((w0, w1, w2, w3)):
        owner = lax.rem(y + NY - d, NY)
        b = jnp.concatenate([w[0, pl.ds(theirs, width)], w[1, pl.ds(theirs, width)]], axis=1)
        a = jnp.concatenate([w[0, pl.ds(mine, width)], w[1, pl.ds(mine, width)]], axis=1)
        for r in range(0, rows, step):
            total = dot(other[pl.ds(r, step)], b)
            if d == 0 and r == 0:
                fetch.wait()
            total = total + dot(own[pl.ds(r, step)], a)
            out[owner, pl.ds(r, step)] = total.astype(BF)


def partial_sums(own, other, blocks, early):
    rows, width = own.shape
    return call(
        partial_kernel,
        jax.ShapeDtypeStruct((NY, rows, 2 * HS), BF),
        [ANY] + [VMEM] * 5 + [ANY],
        VMEM,
        flops=2 * rows * 2 * width * NY * 2 * HS,
        scratch_shapes=[pltpu.VMEM((rows, width), BF), pltpu.SemaphoreType.DMA],
    )(own, other, *blocks, early)


def hidden_kernel(sums, out):
    total = sums[0].astype(F32)
    for k in range(1, NY):
        total = total + sums[k].astype(F32)
    gate, up = total[:, :HS], total[:, HS:]
    hidden = (gate / (1.0 + jnp.exp(-gate)) * up).astype(BF)
    for k in range(NY):
        out[k] = hidden


def hidden_copies(sums):
    return call(
        hidden_kernel, jax.ShapeDtypeStruct((NY, sums.shape[1], HS), BF), [VMEM], VMEM
    )(sums)


def out_kernel(mine, hidden, w0, w1, w2, w3, out):
    y, c = position()
    rows = hidden.shape[1]
    width = out.shape[1]
    first = (c if mine else 1 - c) * width
    owners = [lax.rem(y + NY - d, NY) for d in range(NY)]
    a = jnp.concatenate([hidden[k] for k in owners], axis=1)
    for j in range(0, width, 2 * HS):
        one = pl.multiple_of(first + j, HS)
        two = pl.multiple_of(first + j + HS, HS)
        b = jnp.concatenate(
            [
                jnp.concatenate([w[2, pl.ds(one, HS)], w[2, pl.ds(two, HS)]], axis=1)
                for w in (w0, w1, w2, w3)
            ],
            axis=0,
        )
        out[:, pl.ds(j, 2 * HS)] = dot(a, b).astype(out.dtype)


def out_sums(hidden, blocks, width, mine):
    rows = hidden.shape[1]
    return call(
        functools.partial(out_kernel, mine),
        jax.ShapeDtypeStruct((rows, width), F32 if mine else BF),
        [VMEM] * 5,
        VMEM,
        flops=2 * rows * width * NY * HS,
    )(hidden, *blocks)


def weight_kernel(slots, gates, out):
    tokens, rows = out.shape[1:]
    names = spread(slots[...].astype(F32), rows)
    hit = names == lax.broadcasted_iota(jnp.int32, (tokens, rows), 0).astype(F32)
    left = gates[...]
    for p in range(out.shape[0]):
        piece = left.astype(BF).astype(F32)
        left = left - piece
        out[p] = jnp.where(hit, spread(piece, rows), 0.0).astype(BF)


def token_weights(slots, gates, tokens):
    rows = slots.shape[0] * slots.shape[1]
    return call(
        weight_kernel, jax.ShapeDtypeStruct((3, tokens, rows), BF), [VMEM, VMEM], VMEM
    )(slots, gates)


def finish_kernel(weights, returned, counts, out):
    divisor = jnp.maximum(counts[...].astype(F32), 1.0)
    rows = returned[...]
    total = dot(weights[2], rows) + dot(weights[1], rows)
    total = total + dot(weights[0], rows)
    out[...] = (total / divisor).astype(BF)


def finish(weights, returned, counts):
    return call(
        finish_kernel,
        jax.ShapeDtypeStruct((weights.shape[1], returned.shape[1]), BF),
        [VMEM] * 3,
        VMEM,
    )(weights, returned, counts)


def local(tokens, slot_lists, slot_gates, counts, gate_weight, up_weight, down_weight):
    width = tokens.shape[1] // (2 * NY)
    experts, _, slots = slot_lists.shape
    rows = experts * slots
    weights = gate_weight[0], up_weight[0], down_weight[0]
    names = slot_lists.transpose(2, 1, 0).reshape(slots, experts)
    gates = slot_gates.transpose(2, 1, 0).reshape(slots, experts)

    far = 2
    picked, first = start(far, names, tokens, *weights)
    blocks = []
    for d in range(NY):
        block = first if d == far else pack(d, *weights)
        blocks.append(lax.ppermute(block, "y", [(j, (j + d) % NY) for j in range(NY)]) if d else block)
    arrived = lax.all_to_all(picked.reshape(-1, 8, width), E, 0, 0, tiled=True).reshape(rows, width)
    arrived, early = lax.optimization_barrier((arrived, ready(blocks[0], blocks[far])))
    other = swap_cores(arrived)
    parts = partial_sums(arrived, other, blocks, early)
    sums = lax.all_to_all(parts, "y", 0, 0, tiled=True)
    hidden = lax.all_to_all(hidden_copies(sums), "y", 0, 0, tiled=True)
    give = swap_cores(out_sums(hidden, blocks, width, False))
    keep = out_sums(hidden, blocks, width, True)
    result = (keep + give.astype(F32)).astype(BF)
    returned = lax.all_to_all(result.reshape(-1, 8, width), E, 0, 0, tiled=True)
    return finish(
        token_weights(names, gates, tokens.shape[0]),
        returned.reshape(rows, width),
        counts.reshape(-1, 1),
    )


def solution(mesh):
    fine = Mesh(np.asarray(mesh.devices).reshape(4, 16, NY, 2), ("x", "z", "y", "core"))
    return jax.shard_map(
        local,
        mesh=fine,
        in_specs=(
            P(E, None),
            P(None, E, None),
            P(None, E, None),
            P(E),
            P(E, None, S),
            P(E, None, S),
            P(E, S, None),
        ),
        out_specs=P(E, S),
        check_vma=False,
    )
```

time: 145 us -> 140 us (0.966)
  waiting for transfers between devices: 53.5 us -> 51.1 us
    all_to_all x1, waiting for transfers between devices: 20.1 us -> 16.6 us  [local(): lax.all_to_all(picked.reshape(-1, 8, width), E, 0, 0, tiled=True)]
    pallas_call x4 -> x7, Pallas kernels: 10.8 us -> 12.7 us  [the longest x3 6.13 us: pack(): call(functools.partial(pack_kernel, d), jax.ShapeDtypeStruct((3, group, H...]
  transfers between devices with their start and end apart: 7 -> 7, of which waited for: 4 -> 4; matrix products, arithmetic and copies ran while one was open for 0% -> 0% of each run, Pallas kernels for 4% -> 5%
where the time goes in v3:
time: 140 us
  waiting for transfers between devices  51.1 us (36%)
  starting transfers between devices  41.9 us (30%)
  blocking collectives  29.7 us (21%)
  Pallas kernels  13.8 us (10%)
  local copies, waits for them, and re-layouts  1.9 us (1%)
    all_to_all x1, waiting for transfers between devices, local(): returned = lax.all_to_all(result.reshape(-1, 8, width), E, 0, 0, tiled=True)  31 us
    all_to_all x1, starting transfers between devices, local(): lax.all_to_all(picked.reshape(-1, 8, width), E, 0, 0, tiled=True)  19 us
    all_to_all x1, blocking collectives, local(): sums = lax.all_to_all(parts, 'y', 0, 0, tiled=True)  18.1 us
    all_to_all x1, waiting for transfers between devices, local(): lax.all_to_all(picked.reshape(-1, 8, width), E, 0, 0, tiled=True)  16.6 us
    ppermute x3, starting transfers between devices, local(): lax.ppermute(block, 'y', [(j, (j + d) % NY) for j in range(NY)])  12.2 us
    all_to_all x1, blocking collectives, local(): hidden = lax.all_to_all(hidden_copies(sums), 'y', 0, 0, tiled=True)  11.6 us
    all_to_all x1, starting transfers between devices, local(): returned = lax.all_to_all(result.reshape(-1, 8, width), E, 0, 0, tiled=True)  6.95 us
    pallas_call x3, Pallas kernels, pack(): call(functools.partial(pack_kernel, d), jax.ShapeDtypeStruct((3, group, H...  6.13 us
  transfers between devices with their start and end apart: 7, of which 4 were waited for; matrix products, arithmetic and copies ran while one was open for 0% of the time, Pallas kernels for 5%

profile of v3, /device:TPU:6, one launch (start us, length us, event | category | flops | bytes accessed | tf_op | source)
XLA Modules:
  0.0 139.6 jit_solution(2451691851804579302)
XLA Ops:
  0.0 3.1 %shard_map.74 = (bf16[512,512]{1,0:T(8,128)(2,1)}, bf16[3,1024,128]{2,1,0:T(8,128)(2,1)}) custom-call(s32[8,64]{1,0:T(8,128)} %bitcast.16, bf16[128,4096]{1,0:T(8,128)(2,1)} %tokens.1, bf16[4096,128]{1,0:T(8,128)(2,1)} %bitcast.19, bf16[4096,128]{1,0:T(8,128)(2,1)} %bitcast.23, bf16[128,4096]{1,0:T(8,128)(2,1)} %bitcast.27), custom_call_target="tpu_custom_call" | custom-call | bytes 5242880 | tf_op jit(solution)/shard_map/pallas_call | solution.py:114
  3.1 5.1 %collective-permute-start = (bf16[3,1024,128]{2,1,0:T(8,128)(2,1)}, bf16[3,1024,128]{2,1,0:T(8,128)(2,1)S(1)}, u32[]{:S(2)}, u32[]{:S(2)}) collective-permute-start(bf16[3,1024,128]{2,1,0:T(8,128)(2,1)} %get-tuple-element.10), channel_id=1, source_target_pairs={{0,4},{2,6},{4,0},{6,2},{1,5},{3,7},{5,1},{7,3},{8,12},{10,14},{12... | collective-permute-start | bytes 2359304 | tf_op jit(solution)/shard_map/ppermute | solution.py:296
  8.2 19.0 %all-to-all-start = ((bf16[64,8,512]{2,1,0:T(8,128)(2,1)}), bf16[64,8,512]{2,1,0:T(8,128)(2,1)}, u32[]{:S(2)}, u32[]{:S(2)}) async-start(bf16[64,8,512]{2,1,0:T(8,128)(2,1)} %bitcast.31), calls=%async_computation | async-start | bytes 1048576 | tf_op jit(solution)/shard_map/all_to_all | solution.py:297
  27.2 2.0 %shard_map.77 = bf16[3,1024,128]{2,1,0:T(8,128)(2,1)} custom-call(bf16[4096,128]{1,0:T(8,128)(2,1)} %bitcast.20, bf16[4096,128]{1,0:T(8,128)(2,1)} %bitcast.24, bf16[128,4096]{1,0:T(8,128)(2,1)} %bitcast.28), custom_call_target="tpu_custom_call" | custom-call | bytes 1048576 | tf_op jit(solution)/shard_map/pallas_call | solution.py:142
  29.2 2.6 %collective-permute-start.2 = (bf16[3,1024,128]{2,1,0:T(8,128)(2,1)}, bf16[3,1024,128]{2,1,0:T(8,128)(2,1)S(1)}, u32[]{:S(2)}, u32[]{:S(2)}) collective-permute-start(bf16[3,1024,128]{2,1,0:T(8,128)(2,1)} %shard_map.77), channel_id=1, source_target_pairs={{0,2},{2,4},{4,6},{6,0},{1,3},{3,5},{5,7},{7,1},{8,10},{10,12},{12... | collective-permute-start | bytes 2359304 | tf_op jit(solution)/shard_map/ppermute | solution.py:296
  31.8 2.0 %shard_map.78 = bf16[3,1024,128]{2,1,0:T(8,128)(2,1)} custom-call(bf16[4096,128]{1,0:T(8,128)(2,1)} %bitcast.21, bf16[4096,128]{1,0:T(8,128)(2,1)} %bitcast.25, bf16[128,4096]{1,0:T(8,128)(2,1)} %bitcast.29), custom_call_target="tpu_custom_call" | custom-call | bytes 1048576 | tf_op jit(solution)/shard_map/pallas_call | solution.py:142
  33.8 4.5 %collective-permute-start.3 = (bf16[3,1024,128]{2,1,0:T(8,128)(2,1)}, bf16[3,1024,128]{2,1,0:T(8,128)(2,1)S(1)}, u32[]{:S(2)}, u32[]{:S(2)}) collective-permute-start(bf16[3,1024,128]{2,1,0:T(8,128)(2,1)} %shard_map.78), channel_id=1, source_target_pairs={{0,6},{2,0},{4,2},{6,4},{1,7},{3,1},{5,3},{7,5},{8,14},{10,8},{12,... | collective-permute-start | bytes 2359304 | tf_op jit(solution)/shard_map/ppermute | solution.py:296
  38.3 2.1 %shard_map.75.first.w0 = bf16[3,1024,128]{2,1,0:T(8,128)(2,1)} custom-call(bf16[4096,128]{1,0:T(8,128)(2,1)} %bitcast.22, bf16[4096,128]{1,0:T(8,128)(2,1)} %bitcast.26, bf16[128,4096]{1,0:T(8,128)(2,1)} %bitcast.30), custom_call_target="tpu_custom_call" | custom-call | bytes 1048576 | tf_op jit(solution)/shard_map/pallas_call | solution.py:142
  40.4 0.0 collective-permute-done.second.w2
  40.4 1.1 copy-done
  41.6 16.6 %all-to-all-done = bf16[64,8,512]{2,1,0:T(8,128)(2,1)} async-done(((bf16[64,8,512]{2,1,0:T(8,128)(2,1)}), bf16[64,8,512]{2,1,0:T(8,128)(2,1)}, u32[]{:S(2)}, u32[]{:S(2)}) %all-to-all-start) | async-done | bytes 524320 | tf_op jit(solution)/shard_map/all_to_all | solution.py:297
  58.2 1.9 %collective-permute-start.1 = (bf16[512,512]{1,0:T(8,128)(2,1)}, bf16[512,512]{1,0:T(8,128)(2,1)S(1)}, u32[]{:S(2)}, u32[]{:S(2)}) collective-permute-start(bf16[512,512]{1,0:T(8,128)(2,1)} %bitcast.9.own_ref), channel_id=1, source_target_pairs={{0,1},{1,0},{2,3},{3,2},{4,5},{5,4},{6,7},{7,6},{8,9},{9,8},{10,11... | collective-permute-start | bytes 1572872 | tf_op jit(solution)/shard_map/ppermute | solution.py:43
  60.1 0.0 collective-permute-done.2.w1
  60.1 0.0 collective-permute-done.3.w3
  60.1 2.1 %collective-permute-done.1.other = bf16[512,512]{1,0:T(8,128)(2,1)S(1)} collective-permute-done((bf16[512,512]{1,0:T(8,128)(2,1)}, bf16[512,512]{1,0:T(8,128)(2,1)S(1)}, u32[]{:S(2)}, u32[]{:S(2)}) %collective-permute-start.1) | collective-permute-done | bytes 524320 | tf_op jit(solution)/shard_map/ppermute | solution.py:43
  62.2 0.0 copy-done.1
  62.2 2.3 %shard_map.79 = bf16[4,512,256]{2,1,0:T(8,128)(2,1)S(1)} custom-call(bf16[512,512]{1,0:T(8,128)(2,1)} %bitcast.9.own_ref, bf16[512,512]{1,0:T(8,128)(2,1)S(1)} %collective-permute-done.1.other, bf16[3,1024,128]{2,1,0:T(8,128)(2,1)S(1)} %copy-done.1, bf16[3,1024,128]{2,1,0:T(8,128)(2,1)S(1)} %collective-permute-done.2.w1, ...), custom_call_target="tpu_custom_call" | custom-call | flops 1073741824 | bytes 1048576 | tf_op jit(solution)/shard_map/pallas_call | solution.py:191
  64.5 18.1 %all_to_all.20.sums = bf16[4,512,256]{2,1,0:T(8,128)(2,1)S(1)} all-to-all(bf16[4,512,256]{2,1,0:T(8,128)(2,1)S(1)} %shard_map.79), channel_id=1, replica_groups=mesh['x'=4,'z'=16,'y'=4,'core'=2] {'y'}, dimensions={0} | all-to-all | bytes 2097152 | tf_op jit(solution)/shard_map/all_to_all | solution.py:301
  82.6 0.2 shard_map.80
  82.8 11.6 %all_to_all.21.hidden = bf16[4,512,128]{2,1,0:T(8,128)(2,1)S(1)} all-to-all(bf16[4,512,128]{2,1,0:T(8,128)(2,1)S(1)} %shard_map.80), channel_id=1, replica_groups=mesh['x'=4,'z'=16,'y'=4,'core'=2] {'y'}, dimensions={0} | all-to-all | bytes 1048576 | tf_op jit(solution)/shard_map/all_to_all | solution.py:302
  94.4 0.4 shard_map.82
  94.9 1.9 %collective-permute-start.4 = (bf16[512,512]{1,0:T(8,128)(2,1)S(1)}, bf16[512,512]{1,0:T(8,128)(2,1)S(1)}, u32[]{:S(2)}, u32[]{:S(2)}) collective-permute-start(bf16[512,512]{1,0:T(8,128)(2,1)S(1)} %shard_map.82), channel_id=1, source_target_pairs={{0,1},{1,0},{2,3},{3,2},{4,5},{5,4},{6,7},{7,6},{8,9},{9,8},{10,11... | collective-permute-start | bytes 1572872 | tf_op jit(solution)/shard_map/ppermute | solution.py:43
  96.8 0.5 shard_map.81
  97.3 1.4 %collective-permute-done.4 = bf16[512,512]{1,0:T(8,128)(2,1)S(1)} collective-permute-done((bf16[512,512]{1,0:T(8,128)(2,1)S(1)}, bf16[512,512]{1,0:T(8,128)(2,1)S(1)}, u32[]{:S(2)}, u32[]{:S(2)}) %collective-permute-start.4) | collective-permute-done | bytes 524320 | tf_op jit(solution)/shard_map/ppermute | solution.py:43
  98.7 1.0 fusion
  99.6 6.9 %all-to-all-start.3 = ((bf16[64,8,512]{2,1,0:T(8,128)(2,1)}), bf16[64,8,512]{2,1,0:T(8,128)(2,1)S(1)}, u32[]{:S(2)}, u32[]{:S(2)}) async-start(bf16[64,8,512]{2,1,0:T(8,128)(2,1)} %fusion), calls=%async_computation.3 | async-start | bytes 1048576 | tf_op jit(solution)/shard_map/all_to_all | solution.py:306
  106.6 0.2 shard_map.73.weights
  106.8 0.0 copy-start.4
  106.8 0.6 copy-done.4
  107.5 0.1 copy.8.counts
  107.6 31.0 %all-to-all-done.3 = bf16[64,8,512]{2,1,0:T(8,128)(2,1)S(1)} async-done(((bf16[64,8,512]{2,1,0:T(8,128)(2,1)}), bf16[64,8,512]{2,1,0:T(8,128)(2,1)S(1)}, u32[]{:S(2)}, u32[]{:S(2)}) %all-to-all-start.3) | async-done | bytes 524320 | tf_op jit(solution)/shard_map/all_to_all | solution.py:306
  138.6 1.0 shard_map.83
  (7 shorter events, 0.0 us)
Async XLA Ops:
  3.1 37.3 %collective-permute-start = (bf16[3,1024,128]{2,1,0:T(8,128)(2,1)}, bf16[3,1024,128]{2,1,0:T(8,128)(2,1)S(1)}, u32[]{:S(2)}, u32[]{:S(2)}) collective-permute-start(bf16[3,1024,128]{2,1,0:T(8,128)(2,1)} %get-tuple-element.10), channel_id=1, source_target_pairs={{0,4},{2,6},{4,0},{6,2},{1,5},{3,7},{5,1},{7,3},{8,12},{10,14},{12... | collective-permute-start | bytes 2359304 | tf_op jit(solution)/shard_map/ppermute | solution.py:296
  8.2 50.0 %all-to-all-start = ((bf16[64,8,512]{2,1,0:T(8,128)(2,1)}), bf16[64,8,512]{2,1,0:T(8,128)(2,1)}, u32[]{:S(2)}, u32[]{:S(2)}) async-start(bf16[64,8,512]{2,1,0:T(8,128)(2,1)} %bitcast.31), calls=%async_computation | async-start | bytes 1048576 | tf_op jit(solution)/shard_map/all_to_all | solution.py:297
  29.2 30.9 %collective-permute-start.2 = (bf16[3,1024,128]{2,1,0:T(8,128)(2,1)}, bf16[3,1024,128]{2,1,0:T(8,128)(2,1)S(1)}, u32[]{:S(2)}, u32[]{:S(2)}) collective-permute-start(bf16[3,1024,128]{2,1,0:T(8,128)(2,1)} %shard_map.77), channel_id=1, source_target_pairs={{0,2},{2,4},{4,6},{6,0},{1,3},{3,5},{5,7},{7,1},{8,10},{10,12},{12... | collective-permute-start | bytes 2359304 | tf_op jit(solution)/shard_map/ppermute | solution.py:296
  33.8 26.3 %collective-permute-start.3 = (bf16[3,1024,128]{2,1,0:T(8,128)(2,1)}, bf16[3,1024,128]{2,1,0:T(8,128)(2,1)S(1)}, u32[]{:S(2)}, u32[]{:S(2)}) collective-permute-start(bf16[3,1024,128]{2,1,0:T(8,128)(2,1)} %shard_map.78), channel_id=1, source_target_pairs={{0,6},{2,0},{4,2},{6,4},{1,7},{3,1},{5,3},{7,5},{8,14},{10,8},{12,... | collective-permute-start | bytes 2359304 | tf_op jit(solution)/shard_map/ppermute | solution.py:296
  40.4 1.1 copy-start
  41.5 20.7 %copy-start.1 = (bf16[3,1024,128]{2,1,0:T(8,128)(2,1)S(1)}, bf16[3,1024,128]{2,1,0:T(8,128)(2,1)}, u32[]{:S(2)}) copy-start(bf16[3,1024,128]{2,1,0:T(8,128)(2,1)} %shard_map.75.first.w0) | copy-start | bytes 2359300
  58.2 4.0 %collective-permute-start.1 = (bf16[512,512]{1,0:T(8,128)(2,1)}, bf16[512,512]{1,0:T(8,128)(2,1)S(1)}, u32[]{:S(2)}, u32[]{:S(2)}) collective-permute-start(bf16[512,512]{1,0:T(8,128)(2,1)} %bitcast.9.own_ref), channel_id=1, source_target_pairs={{0,1},{1,0},{2,3},{3,2},{4,5},{5,4},{6,7},{7,6},{8,9},{9,8},{10,11... | collective-permute-start | bytes 1572872 | tf_op jit(solution)/shard_map/ppermute | solution.py:43
  94.9 3.8 %collective-permute-start.4 = (bf16[512,512]{1,0:T(8,128)(2,1)S(1)}, bf16[512,512]{1,0:T(8,128)(2,1)S(1)}, u32[]{:S(2)}, u32[]{:S(2)}) collective-permute-start(bf16[512,512]{1,0:T(8,128)(2,1)S(1)} %shard_map.82), channel_id=1, source_target_pairs={{0,1},{1,0},{2,3},{3,2},{4,5},{5,4},{6,7},{7,6},{8,9},{9,8},{10,11... | collective-permute-start | bytes 1572872 | tf_op jit(solution)/shard_map/ppermute | solution.py:43
  98.7 7.9 %copy-start.2 = (s32[64,1,8]{0,2,1:T(8,128)S(1)}, s32[64,1,8]{0,2,1:T(8,128)}, u32[]{:S(2)}) copy-start(s32[64,1,8]{0,2,1:T(8,128)} %param.8) | copy-start | bytes 6148
  98.7 7.9 %copy-start.3 = (f32[64,1,8]{0,2,1:T(8,128)S(1)}, f32[64,1,8]{0,2,1:T(8,128)}, u32[]{:S(2)}) copy-start(f32[64,1,8]{0,2,1:T(8,128)} %param.9) | copy-start | bytes 6148
  99.6 38.9 %all-to-all-start.3 = ((bf16[64,8,512]{2,1,0:T(8,128)(2,1)}), bf16[64,8,512]{2,1,0:T(8,128)(2,1)S(1)}, u32[]{:S(2)}, u32[]{:S(2)}) async-start(bf16[64,8,512]{2,1,0:T(8,128)(2,1)} %fusion), calls=%async_computation.3 | async-start | bytes 1048576 | tf_op jit(solution)/shard_map/all_to_all | solution.py:306
  106.8 0.7 copy-start.4

commit v4 on v3

--- a/solution.py
+++ b/solution.py
@@ -74,35 +74,37 @@
     return lax.axis_index("y"), lax.axis_index("core")
 
 
-def start_kernel(far, slots, tokens, gate, up, down, picked, block, own, rows_out, held, sems, own_sem, out_sems):
+def start_kernel(far, slots_ref, tokens, gate, up, down, picked, block, slots, own, rows_out, held, sems, own_sems, out_sems):
     y, c = position()
     width = own.shape[1]
     local_tokens = tokens.shape[0]
     first = pl.multiple_of((y * 2 + c) * width, width)
-    fetch = pltpu.make_async_copy(tokens.at[:, pl.ds(first, width)], own, own_sem)
+    fetch_slots = pltpu.make_async_copy(slots_ref, slots, own_sems.at[0])
+    fetch = pltpu.make_async_copy(tokens.at[:, pl.ds(first, width)], own, own_sems.at[1])
+    fetch_slots.start()
     fetch.start()
     copies = block_copies(lax.rem(y + far, NY), gate, up, down, held, sems)
     for copy in copies:
         copy.start()
     rows = picked.shape[0]
+    token = lax.broadcasted_iota(jnp.int32, (local_tokens, rows), 0).astype(F32)
+    fetch_slots.wait()
     names = spread(slots[...].astype(F32), rows)
-    token = lax.broadcasted_iota(jnp.int32, (local_tokens, rows), 0).astype(F32)
     hit = (names == token).astype(BF)
     fetch.wait()
-    for copy in copies:
-        copy.wait()
-    send = pltpu.make_async_copy(held, block, out_sems.at[0])
-    send.start()
-    sends = [send]
     step = rows // 2
+    sends = []
     for n in range(2):
         part = pl.ds(n * step, step)
         rows_out[part] = lax.dot_general(
             hit[:, n * step : (n + 1) * step], own[...], (((0,), (0,)), ((), ())), preferred_element_type=F32
         ).astype(BF)
-        send = pltpu.make_async_copy(rows_out.at[part], picked.at[part], out_sems.at[1 + n])
-        send.start()
-        sends.append(send)
+        sends.append(pltpu.make_async_copy(rows_out.at[part], picked.at[part], out_sems.at[n]))
+        sends[-1].start()
+    for copy in copies:
+        copy.wait()
+    sends.append(pltpu.make_async_copy(held, block, out_sems.at[2]))
+    sends[-1].start()
     for send in sends:
         send.wait()
 
@@ -114,16 +116,17 @@
     return call(
         functools.partial(start_kernel, far),
         (jax.ShapeDtypeStruct((rows, width), BF), jax.ShapeDtypeStruct((3, group, HS), BF)),
-        [VMEM, ANY, ANY, ANY, ANY],
+        [ANY] * 5,
         (ANY, ANY),
         bytes_accessed=5 << 20,
         vmem=WHOLE,
         scratch_shapes=[
+            pltpu.VMEM(slots.shape, jnp.int32),
             pltpu.VMEM((tokens.shape[0], width), BF),
             pltpu.VMEM((rows, width), BF),
             pltpu.VMEM((3, group, HS), BF),
             pltpu.SemaphoreType.DMA((2 + group // HS,)),
-            pltpu.SemaphoreType.DMA,
+            pltpu.SemaphoreType.DMA((2,)),
             pltpu.SemaphoreType.DMA((3,)),
         ],
     )(slots, tokens, gate, up, down)
@@ -166,36 +169,42 @@
     )(first, second)
 
 
-def partial_kernel(own_ref, other, w0, w1, w2, w3, early, out, own, sem):
-    fetch = pltpu.make_async_copy(own_ref, own, sem)
-    fetch.start()
+def half_kernel(rows, w0, w1, w2, w3, early, out):
     y, c = position()
-    rows, width = own.shape
+    width = rows.shape[1]
     step = 256
-    mine = pl.multiple_of(c * width, width)
-    theirs = pl.multiple_of((1 - c) * width, width)
+    part = pl.ds(pl.multiple_of(c * width, width), width)
     for d, w in enumerate((w0, w1, w2, w3)):
         owner = lax.rem(y + NY - d, NY)
-        b = jnp.concatenate([w[0, pl.ds(theirs, width)], w[1, pl.ds(theirs, width)]], axis=1)
-        a = jnp.concatenate([w[0, pl.ds(mine, width)], w[1, pl.ds(mine, width)]], axis=1)
-        for r in range(0, rows, step):
-            total = dot(other[pl.ds(r, step)], b)
-            if d == 0 and r == 0:
-                fetch.wait()
-            total = total + dot(own[pl.ds(r, step)], a)
-            out[owner, pl.ds(r, step)] = total.astype(BF)
+        a = jnp.concatenate([w[0, part], w[1, part]], axis=1)
+        for r in range(0, rows.shape[0], step):
+            at = pl.ds(r, step)
+            out[owner, at] = dot(rows[at], a)
+
+
+def whole_kernel(rows, w0, w1, w2, w3, half, out):
+    y, c = position()
+    width = rows.shape[1]
+    step = 256
+    part = pl.ds(pl.multiple_of((1 - c) * width, width), width)
+    for d, w in enumerate((w0, w1, w2, w3)):
+        owner = lax.rem(y + NY - d, NY)
+        a = jnp.concatenate([w[0, part], w[1, part]], axis=1)
+        for r in range(0, rows.shape[0], step):
+            at = pl.ds(r, step)
+            out[owner, at] = (half[owner, at] + dot(rows[at], a)).astype(BF)
 
 
 def partial_sums(own, other, blocks, early):
     rows, width = own.shape
-    return call(
-        partial_kernel,
-        jax.ShapeDtypeStruct((NY, rows, 2 * HS), BF),
-        [ANY] + [VMEM] * 5 + [ANY],
-        VMEM,
-        flops=2 * rows * 2 * width * NY * 2 * HS,
-        scratch_shapes=[pltpu.VMEM((rows, width), BF), pltpu.SemaphoreType.DMA],
-    )(own, other, *blocks, early)
+    shape = (NY, rows, 2 * HS)
+    flops = 2 * rows * width * NY * 2 * HS
+    half = call(
+        half_kernel, jax.ShapeDtypeStruct(shape, F32), [VMEM] * 5 + [ANY], VMEM, flops=flops
+    )(own, *blocks, early)
+    return call(whole_kernel, jax.ShapeDtypeStruct(shape, BF), [VMEM] * 6, VMEM, flops=flops)(
+        other, *blocks, half
+    )
 
 
 def hidden_kernel(sums, out):
@@ -245,39 +254,66 @@
     )(hidden, *blocks)
 
 
-def weight_kernel(slots, gates, out):
+def result_kernel(keep, given, out, sums, sems):
+    rows = keep.shape[0]
+    step = rows // 4
+    sends = []
+    for n in range(4):
+        part = pl.ds(n * step, step)
+        sums[part] = (keep[part] + given[part].astype(F32)).astype(BF)
+        sends.append(pltpu.make_async_copy(sums.at[part], out.at[part], sems.at[n]))
+        sends[-1].start()
+    for send in sends:
+        send.wait()
+
+
+def result_rows(keep, given):
+    return call(
+        result_kernel,
+        jax.ShapeDtypeStruct(given.shape, BF),
+        [VMEM, VMEM],
+        ANY,
+        scratch_shapes=[pltpu.VMEM(given.shape, BF), pltpu.SemaphoreType.DMA((4,))],
+    )(keep, given)
+
+
+def weight_kernel(slots, gates, counts, out):
     tokens, rows = out.shape[1:]
     names = spread(slots[...].astype(F32), rows)
     hit = names == lax.broadcasted_iota(jnp.int32, (tokens, rows), 0).astype(F32)
     left = gates[...]
-    for p in range(out.shape[0]):
+    gate = jnp.zeros((1, rows), F32)
+    for p in range(3):
         piece = left.astype(BF).astype(F32)
         left = left - piece
-        out[p] = jnp.where(hit, spread(piece, rows), 0.0).astype(BF)
-
-
-def token_weights(slots, gates, tokens):
+        gate = gate + spread(piece, rows)
+    left = jnp.where(hit, gate, 0.0) / jnp.maximum(counts[...].astype(F32), 1.0)
+    for p in range(out.shape[0]):
+        piece = left.astype(BF)
+        left = left - piece.astype(F32)
+        out[p] = piece
+
+
+def token_weights(slots, gates, counts):
     rows = slots.shape[0] * slots.shape[1]
     return call(
-        weight_kernel, jax.ShapeDtypeStruct((3, tokens, rows), BF), [VMEM, VMEM], VMEM
-    )(slots, gates)
-
-
-def finish_kernel(weights, returned, counts, out):
-    divisor = jnp.maximum(counts[...].astype(F32), 1.0)
+        weight_kernel, jax.ShapeDtypeStruct((3, counts.shape[0], rows), BF), [VMEM] * 3, VMEM
+    )(slots, gates, counts)
+
+
+def finish_kernel(weights, returned, out):
     rows = returned[...]
     total = dot(weights[2], rows) + dot(weights[1], rows)
-    total = total + dot(weights[0], rows)
-    out[...] = (total / divisor).astype(BF)
-
-
-def finish(weights, returned, counts):
+    out[...] = (total + dot(weights[0], rows)).astype(BF)
+
+
+def finish(weights, returned):
     return call(
         finish_kernel,
         jax.ShapeDtypeStruct((weights.shape[1], returned.shape[1]), BF),
-        [VMEM] * 3,
+        [VMEM] * 2,
         VMEM,
-    )(weights, returned, counts)
+    )(weights, returned)
 
 
 def local(tokens, slot_lists, slot_gates, counts, gate_weight, up_weight, down_weight):
@@ -302,13 +338,9 @@
     hidden = lax.all_to_all(hidden_copies(sums), "y", 0, 0, tiled=True)
     give = swap_cores(out_sums(hidden, blocks, width, False))
     keep = out_sums(hidden, blocks, width, True)
-    result = (keep + give.astype(F32)).astype(BF)
+    result = result_rows(keep, give)
     returned = lax.all_to_all(result.reshape(-1, 8, width), E, 0, 0, tiled=True)
-    return finish(
-        token_weights(names, gates, tokens.shape[0]),
-        returned.reshape(rows, width),
-        counts.reshape(-1, 1),
-    )
+    return finish(token_weights(names, gates, counts.reshape(-1, 1)), returned.reshape(rows, width))
 
 
 def solution(mesh):

time: 140 us -> 139 us (level)
    ppermute x2, waiting for transfers between devices: 3.48 us -> 1.68 us  [swap_cores(): return lax.ppermute(a, 'core', [(0, 1), (1, 0)])]
    pallas_call x2 -> x4, Pallas kernels: 2.51 us -> 3.56 us  [the longest x1 1.75 us: partial_sums(): call(half_kernel, jax.ShapeDtypeStruct(shape, F32), [VMEM] * 5 + [ANY], V...]
  transfers between devices with their start and end apart: 7 -> 7, of which waited for: 4 -> 4; matrix products, arithmetic and copies ran while one was open for 0% -> 0% of each run, Pallas kernels for 5% -> 6%
where the time goes in v4:
time: 139 us; the launch traced here: 138 us
  waiting for transfers between devices  49.9 us (36%)
  starting transfers between devices  42.3 us (30%)
  blocking collectives  29.9 us (22%)
  Pallas kernels  14.5 us (10%)
    all_to_all x1, waiting for transfers between devices, local(): returned = lax.all_to_all(result.reshape(-1, 8, width), E, 0, 0, tiled=True)  31.6 us
    all_to_all x1, starting transfers between devices, local(): lax.all_to_all(picked.reshape(-1, 8, width), E, 0, 0, tiled=True)  19 us
    all_to_all x1, blocking collectives, local(): sums = lax.all_to_all(parts, 'y', 0, 0, tiled=True)  18.2 us
    all_to_all x1, waiting for transfers between devices, local(): lax.all_to_all(picked.reshape(-1, 8, width), E, 0, 0, tiled=True)  16.6 us
    ppermute x3, starting transfers between devices, local(): lax.ppermute(block, 'y', [(j, (j + d) % NY) for j in range(NY)])  12.2 us
    all_to_all x1, blocking collectives, local(): hidden = lax.all_to_all(hidden_copies(sums), 'y', 0, 0, tiled=True)  11.7 us
    all_to_all x1, starting transfers between devices, local(): returned = lax.all_to_all(result.reshape(-1, 8, width), E, 0, 0, tiled=True)  7.3 us
    pallas_call x3, Pallas kernels, pack(): call(functools.partial(pack_kernel, d), jax.ShapeDtypeStruct((3, group, H...  6.13 us
  transfers between devices with their start and end apart: 7, of which 4 were waited for; matrix products, arithmetic and copies ran while one was open for 0% of the time, Pallas kernels for 6%

profile of v4, /device:TPU:6, one launch (start us, length us, event | category | flops | bytes accessed | tf_op | source)
XLA Modules:
  0.0 138.0 jit_solution(11325462267195703815)
XLA Ops:
  0.0 2.6 %shard_map.74 = (bf16[512,512]{1,0:T(8,128)(2,1)}, bf16[3,1024,128]{2,1,0:T(8,128)(2,1)}) custom-call(s32[8,64]{1,0:T(8,128)} %bitcast.15, bf16[128,4096]{1,0:T(8,128)(2,1)} %tokens.1, bf16[4096,128]{1,0:T(8,128)(2,1)} %bitcast.18, bf16[4096,128]{1,0:T(8,128)(2,1)} %bitcast.22, bf16[128,4096]{1,0:T(8,128)(2,1)} %bitcast.26), custom_call_target="tpu_custom_call" | custom-call | bytes 5242880 | tf_op jit(solution)/shard_map/pallas_call | solution.py:116
  2.6 5.1 %collective-permute-start = (bf16[3,1024,128]{2,1,0:T(8,128)(2,1)}, bf16[3,1024,128]{2,1,0:T(8,128)(2,1)S(1)}, u32[]{:S(2)}, u32[]{:S(2)}) collective-permute-start(bf16[3,1024,128]{2,1,0:T(8,128)(2,1)} %get-tuple-element.10), channel_id=1, source_target_pairs={{0,4},{2,6},{4,0},{6,2},{1,5},{3,7},{5,1},{7,3},{8,12},{10,14},{12... | collective-permute-start | bytes 2359304 | tf_op jit(solution)/shard_map/ppermute | solution.py:332
  7.7 19.0 %all-to-all-start = ((bf16[64,8,512]{2,1,0:T(8,128)(2,1)}), bf16[64,8,512]{2,1,0:T(8,128)(2,1)}, u32[]{:S(2)}, u32[]{:S(2)}) async-start(bf16[64,8,512]{2,1,0:T(8,128)(2,1)} %bitcast.30), calls=%async_computation | async-start | bytes 1048576 | tf_op jit(solution)/shard_map/all_to_all | solution.py:333
  26.8 2.0 %shard_map.77 = bf16[3,1024,128]{2,1,0:T(8,128)(2,1)} custom-call(bf16[4096,128]{1,0:T(8,128)(2,1)} %bitcast.19, bf16[4096,128]{1,0:T(8,128)(2,1)} %bitcast.23, bf16[128,4096]{1,0:T(8,128)(2,1)} %bitcast.27), custom_call_target="tpu_custom_call" | custom-call | bytes 1048576 | tf_op jit(solution)/shard_map/pallas_call | solution.py:145
  28.8 2.6 %collective-permute-start.2 = (bf16[3,1024,128]{2,1,0:T(8,128)(2,1)}, bf16[3,1024,128]{2,1,0:T(8,128)(2,1)S(1)}, u32[]{:S(2)}, u32[]{:S(2)}) collective-permute-start(bf16[3,1024,128]{2,1,0:T(8,128)(2,1)} %shard_map.77), channel_id=1, source_target_pairs={{0,2},{2,4},{4,6},{6,0},{1,3},{3,5},{5,7},{7,1},{8,10},{10,12},{12... | collective-permute-start | bytes 2359304 | tf_op jit(solution)/shard_map/ppermute | solution.py:332
  31.4 2.0 %shard_map.78 = bf16[3,1024,128]{2,1,0:T(8,128)(2,1)} custom-call(bf16[4096,128]{1,0:T(8,128)(2,1)} %bitcast.20, bf16[4096,128]{1,0:T(8,128)(2,1)} %bitcast.24, bf16[128,4096]{1,0:T(8,128)(2,1)} %bitcast.28), custom_call_target="tpu_custom_call" | custom-call | bytes 1048576 | tf_op jit(solution)/shard_map/pallas_call | solution.py:145
  33.4 4.5 %collective-permute-start.3 = (bf16[3,1024,128]{2,1,0:T(8,128)(2,1)}, bf16[3,1024,128]{2,1,0:T(8,128)(2,1)S(1)}, u32[]{:S(2)}, u32[]{:S(2)}) collective-permute-start(bf16[3,1024,128]{2,1,0:T(8,128)(2,1)} %shard_map.78), channel_id=1, source_target_pairs={{0,6},{2,0},{4,2},{6,4},{1,7},{3,1},{5,3},{7,5},{8,14},{10,8},{12,... | collective-permute-start | bytes 2359304 | tf_op jit(solution)/shard_map/ppermute | solution.py:332
  37.9 2.1 %shard_map.75.first.w0 = bf16[3,1024,128]{2,1,0:T(8,128)(2,1)} custom-call(bf16[4096,128]{1,0:T(8,128)(2,1)} %bitcast.21, bf16[4096,128]{1,0:T(8,128)(2,1)} %bitcast.25, bf16[128,4096]{1,0:T(8,128)(2,1)} %bitcast.29), custom_call_target="tpu_custom_call" | custom-call | bytes 1048576 | tf_op jit(solution)/shard_map/pallas_call | solution.py:145
  40.0 0.0 collective-permute-done.second.w2
  40.0 1.1 copy-done
  41.1 16.6 %all-to-all-done = bf16[64,8,512]{2,1,0:T(8,128)(2,1)} async-done(((bf16[64,8,512]{2,1,0:T(8,128)(2,1)}), bf16[64,8,512]{2,1,0:T(8,128)(2,1)}, u32[]{:S(2)}, u32[]{:S(2)}) %all-to-all-start) | async-done | bytes 524320 | tf_op jit(solution)/shard_map/all_to_all | solution.py:333
  57.8 1.9 %collective-permute-start.1 = (bf16[512,512]{1,0:T(8,128)(2,1)}, bf16[512,512]{1,0:T(8,128)(2,1)S(1)}, u32[]{:S(2)}, u32[]{:S(2)}) collective-permute-start(bf16[512,512]{1,0:T(8,128)(2,1)} %bitcast.10.rows), channel_id=1, source_target_pairs={{0,1},{1,0},{2,3},{3,2},{4,5},{5,4},{6,7},{7,6},{8,9},{9,8},{10,11... | collective-permute-start | bytes 1572872 | tf_op jit(solution)/shard_map/ppermute | solution.py:43
  59.7 0.0 collective-permute-done.2.w1
  59.7 1.8 %shard_map.79.half = f32[4,512,256]{2,1,0:T(8,128)S(1)} custom-call(bf16[512,512]{1,0:T(8,128)(2,1)} %bitcast.10.rows, bf16[3,1024,128]{2,1,0:T(8,128)(2,1)S(1)} %copy-done.1, bf16[3,1024,128]{2,1,0:T(8,128)(2,1)S(1)} %collective-permute-done.2.w1, bf16[3,1024,128]{2,1,0:T(8,128)(2,1)S(1)} %collective-permute-done.second.w2, ...), custom_call_target="tpu_custom_call" | custom-call | flops 536870912 | bytes 1048576 | tf_op jit(solution)/shard_map/pallas_call | solution.py:202
  61.5 0.3 collective-permute-done.1.rows
  61.8 0.7 shard_map.80
  62.5 18.2 %all_to_all.20.sums = bf16[4,512,256]{2,1,0:T(8,128)(2,1)S(1)} all-to-all(bf16[4,512,256]{2,1,0:T(8,128)(2,1)S(1)} %shard_map.80), channel_id=1, replica_groups=mesh['x'=4,'z'=16,'y'=4,'core'=2] {'y'}, dimensions={0} | all-to-all | bytes 2097152 | tf_op jit(solution)/shard_map/all_to_all | solution.py:337
  80.7 0.2 shard_map.81
  80.9 11.7 %all_to_all.21.hidden = bf16[4,512,128]{2,1,0:T(8,128)(2,1)S(1)} all-to-all(bf16[4,512,128]{2,1,0:T(8,128)(2,1)S(1)} %shard_map.81), channel_id=1, replica_groups=mesh['x'=4,'z'=16,'y'=4,'core'=2] {'y'}, dimensions={0} | all-to-all | bytes 1048576 | tf_op jit(solution)/shard_map/all_to_all | solution.py:338
  92.6 0.4 shard_map.83
  93.0 1.9 %collective-permute-start.4 = (bf16[512,512]{1,0:T(8,128)(2,1)S(1)}, bf16[512,512]{1,0:T(8,128)(2,1)S(1)}, u32[]{:S(2)}, u32[]{:S(2)}) collective-permute-start(bf16[512,512]{1,0:T(8,128)(2,1)S(1)} %shard_map.83), channel_id=1, source_target_pairs={{0,1},{1,0},{2,3},{3,2},{4,5},{5,4},{6,7},{7,6},{8,9},{9,8},{10,11... | collective-permute-start | bytes 1572872 | tf_op jit(solution)/shard_map/ppermute | solution.py:43
  95.0 0.5 shard_map.82.keep
  95.4 0.0 copy-start.4
  95.4 0.0 copy-start.2
  95.4 0.0 copy-start.3
  95.5 1.4 collective-permute-done.4.given
  96.8 0.9 shard_map.84
  97.7 7.3 %all-to-all-start.3 = ((bf16[64,8,512]{2,1,0:T(8,128)(2,1)}), bf16[64,8,512]{2,1,0:T(8,128)(2,1)S(1)}, u32[]{:S(2)}, u32[]{:S(2)}) async-start(bf16[64,8,512]{2,1,0:T(8,128)(2,1)} %bitcast.11), calls=%async_computation.3 | async-start | bytes 1048576 | tf_op jit(solution)/shard_map/all_to_all | solution.py:342
  105.0 0.1 copy.8.counts
  105.1 0.2 shard_map.73.weights
  105.4 31.6 %all-to-all-done.3 = bf16[64,8,512]{2,1,0:T(8,128)(2,1)S(1)} async-done(((bf16[64,8,512]{2,1,0:T(8,128)(2,1)}), bf16[64,8,512]{2,1,0:T(8,128)(2,1)S(1)}, u32[]{:S(2)}, u32[]{:S(2)}) %all-to-all-start.3) | async-done | bytes 524320 | tf_op jit(solution)/shard_map/all_to_all | solution.py:342
  137.0 1.0 shard_map.85
  (8 shorter events, 0.0 us)
Async XLA Ops:
  2.6 37.3 %collective-permute-start = (bf16[3,1024,128]{2,1,0:T(8,128)(2,1)}, bf16[3,1024,128]{2,1,0:T(8,128)(2,1)S(1)}, u32[]{:S(2)}, u32[]{:S(2)}) collective-permute-start(bf16[3,1024,128]{2,1,0:T(8,128)(2,1)} %get-tuple-element.10), channel_id=1, source_target_pairs={{0,4},{2,6},{4,0},{6,2},{1,5},{3,7},{5,1},{7,3},{8,12},{10,14},{12... | collective-permute-start | bytes 2359304 | tf_op jit(solution)/shard_map/ppermute | solution.py:332
  7.7 50.0 %all-to-all-start = ((bf16[64,8,512]{2,1,0:T(8,128)(2,1)}), bf16[64,8,512]{2,1,0:T(8,128)(2,1)}, u32[]{:S(2)}, u32[]{:S(2)}) async-start(bf16[64,8,512]{2,1,0:T(8,128)(2,1)} %bitcast.30), calls=%async_computation | async-start | bytes 1048576 | tf_op jit(solution)/shard_map/all_to_all | solution.py:333
  28.8 30.9 %collective-permute-start.2 = (bf16[3,1024,128]{2,1,0:T(8,128)(2,1)}, bf16[3,1024,128]{2,1,0:T(8,128)(2,1)S(1)}, u32[]{:S(2)}, u32[]{:S(2)}) collective-permute-start(bf16[3,1024,128]{2,1,0:T(8,128)(2,1)} %shard_map.77), channel_id=1, source_target_pairs={{0,2},{2,4},{4,6},{6,0},{1,3},{3,5},{5,7},{7,1},{8,10},{10,12},{12... | collective-permute-start | bytes 2359304 | tf_op jit(solution)/shard_map/ppermute | solution.py:332
  33.4 26.3 %collective-permute-start.3 = (bf16[3,1024,128]{2,1,0:T(8,128)(2,1)}, bf16[3,1024,128]{2,1,0:T(8,128)(2,1)S(1)}, u32[]{:S(2)}, u32[]{:S(2)}) collective-permute-start(bf16[3,1024,128]{2,1,0:T(8,128)(2,1)} %shard_map.78), channel_id=1, source_target_pairs={{0,6},{2,0},{4,2},{6,4},{1,7},{3,1},{5,3},{7,5},{8,14},{10,8},{12,... | collective-permute-start | bytes 2359304 | tf_op jit(solution)/shard_map/ppermute | solution.py:332
  40.0 1.1 copy-start
  41.1 18.6 %copy-start.1 = (bf16[3,1024,128]{2,1,0:T(8,128)(2,1)S(1)}, bf16[3,1024,128]{2,1,0:T(8,128)(2,1)}, u32[]{:S(2)}) copy-start(bf16[3,1024,128]{2,1,0:T(8,128)(2,1)} %shard_map.75.first.w0) | copy-start | bytes 2359300
  57.8 4.0 %collective-permute-start.1 = (bf16[512,512]{1,0:T(8,128)(2,1)}, bf16[512,512]{1,0:T(8,128)(2,1)S(1)}, u32[]{:S(2)}, u32[]{:S(2)}) collective-permute-start(bf16[512,512]{1,0:T(8,128)(2,1)} %bitcast.10.rows), channel_id=1, source_target_pairs={{0,1},{1,0},{2,3},{3,2},{4,5},{5,4},{6,7},{7,6},{8,9},{9,8},{10,11... | collective-permute-start | bytes 1572872 | tf_op jit(solution)/shard_map/ppermute | solution.py:43
  93.0 3.8 %collective-permute-start.4 = (bf16[512,512]{1,0:T(8,128)(2,1)S(1)}, bf16[512,512]{1,0:T(8,128)(2,1)S(1)}, u32[]{:S(2)}, u32[]{:S(2)}) collective-permute-start(bf16[512,512]{1,0:T(8,128)(2,1)S(1)} %shard_map.83), channel_id=1, source_target_pairs={{0,1},{1,0},{2,3},{3,2},{4,5},{5,4},{6,7},{7,6},{8,9},{9,8},{10,11... | collective-permute-start | bytes 1572872 | tf_op jit(solution)/shard_map/ppermute | solution.py:43
  95.4 9.6 %copy-start.4 = (s32[128]{0:T(128)S(1)}, s32[128]{0:T(128)}, u32[]{:S(2)}) copy-start(s32[128]{0:T(128)} %param.10) | copy-start | bytes 1540
  95.4 9.7 %copy-start.2 = (s32[64,1,8]{0,2,1:T(8,128)S(1)}, s32[64,1,8]{0,2,1:T(8,128)}, u32[]{:S(2)}) copy-start(s32[64,1,8]{0,2,1:T(8,128)} %param.8) | copy-start | bytes 6148
  95.4 9.7 %copy-start.3 = (f32[64,1,8]{0,2,1:T(8,128)S(1)}, f32[64,1,8]{0,2,1:T(8,128)}, u32[]{:S(2)}) copy-start(f32[64,1,8]{0,2,1:T(8,128)} %param.9) | copy-start | bytes 6148
  97.7 39.3 %all-to-all-start.3 = ((bf16[64,8,512]{2,1,0:T(8,128)(2,1)}), bf16[64,8,512]{2,1,0:T(8,128)(2,1)S(1)}, u32[]{:S(2)}, u32[]{:S(2)}) async-start(bf16[64,8,512]{2,1,0:T(8,128)(2,1)} %bitcast.11), calls=%async_computation.3 | async-start | bytes 1048576 | tf_op jit(solution)/shard_map/all_to_all | solution.py:342

commit v5 on v4

--- a/solution.py
+++ b/solution.py
@@ -8,7 +8,9 @@
 from jax.experimental.pallas import tpu as pltpu
 from jax.sharding import Mesh, PartitionSpec as P
 
-E = ("x", "z")
+E = "expert"
+NX, NZ = 4, 16
+X0, Z0, Y0 = 0, 11, 2
 S = ("y", "core")
 NY = 4
 HS = 128
@@ -60,11 +62,29 @@
     return copies
 
 
+def expert_at(place):
+    return (place // NZ + X0) % NX * NZ + (place % NZ + Z0) % NZ
+
+
+def exchange(rows):
+    order = [expert_at(place) for place in range(rows.shape[0])]
+    return lax.all_to_all(rows, E, 0, 0, axis_index_groups=[order], tiled=True)
+
+
+def exchange_y(blocks):
+    order = [(place + Y0) % NY for place in range(NY)]
+    return lax.all_to_all(blocks, "y", 0, 0, axis_index_groups=[order], tiled=True)
+
+
+def place_y(y, d):
+    return lax.rem(y + 2 * NY - d - Y0, NY)
+
+
 def spread(values, rows):
     slots, experts = values.shape
     lane = lax.broadcasted_iota(jnp.int32, (experts, rows), 1)
     expert = lax.broadcasted_iota(jnp.int32, (experts, rows), 0)
-    wide = dot(values.astype(BF), (lane // slots == expert).astype(BF))
+    wide = dot(values.astype(BF), (expert_at(lane // slots) == expert).astype(BF))
     lane = lax.broadcasted_iota(jnp.int32, (slots, rows), 1)
     slot = lax.broadcasted_iota(jnp.int32, (slots, rows), 0)
     return jnp.sum(jnp.where(lane % slots == slot, wide, 0.0), axis=0, keepdims=True)
@@ -92,9 +112,9 @@
     names = spread(slots[...].astype(F32), rows)
     hit = (names == token).astype(BF)
     fetch.wait()
-    step = rows // 2
+    step = rows // 4
     sends = []
-    for n in range(2):
+    for n in range(4):
         part = pl.ds(n * step, step)
         rows_out[part] = lax.dot_general(
             hit[:, n * step : (n + 1) * step], own[...], (((0,), (0,)), ((), ())), preferred_element_type=F32
@@ -103,7 +123,7 @@
         sends[-1].start()
     for copy in copies:
         copy.wait()
-    sends.append(pltpu.make_async_copy(held, block, out_sems.at[2]))
+    sends.append(pltpu.make_async_copy(held, block, out_sems.at[4]))
     sends[-1].start()
     for send in sends:
         send.wait()
@@ -127,7 +147,7 @@
             pltpu.VMEM((3, group, HS), BF),
             pltpu.SemaphoreType.DMA((2 + group // HS,)),
             pltpu.SemaphoreType.DMA((2,)),
-            pltpu.SemaphoreType.DMA((3,)),
+            pltpu.SemaphoreType.DMA((5,)),
         ],
     )(slots, tokens, gate, up, down)
 
@@ -175,7 +195,7 @@
     step = 256
     part = pl.ds(pl.multiple_of(c * width, width), width)
     for d, w in enumerate((w0, w1, w2, w3)):
-        owner = lax.rem(y + NY - d, NY)
+        owner = place_y(y, d)
         a = jnp.concatenate([w[0, part], w[1, part]], axis=1)
         for r in range(0, rows.shape[0], step):
             at = pl.ds(r, step)
@@ -188,7 +208,7 @@
     step = 256
     part = pl.ds(pl.multiple_of((1 - c) * width, width), width)
     for d, w in enumerate((w0, w1, w2, w3)):
-        owner = lax.rem(y + NY - d, NY)
+        owner = place_y(y, d)
         a = jnp.concatenate([w[0, part], w[1, part]], axis=1)
         for r in range(0, rows.shape[0], step):
             at = pl.ds(r, step)
@@ -228,7 +248,7 @@
     rows = hidden.shape[1]
     width = out.shape[1]
     first = (c if mine else 1 - c) * width
-    owners = [lax.rem(y + NY - d, NY) for d in range(NY)]
+    owners = [place_y(y, d) for d in range(NY)]
     a = jnp.concatenate([hidden[k] for k in owners], axis=1)
     for j in range(0, width, 2 * HS):
         one = pl.multiple_of(first + j, HS)
@@ -288,31 +308,41 @@
         left = left - piece
         gate = gate + spread(piece, rows)
     left = jnp.where(hit, gate, 0.0) / jnp.maximum(counts[...].astype(F32), 1.0)
-    for p in range(out.shape[0]):
-        piece = left.astype(BF)
-        left = left - piece.astype(F32)
-        out[p] = piece
+    high = left.astype(BF)
+    out[0] = high
+    out[1] = (left - high.astype(F32)).astype(BF)
 
 
 def token_weights(slots, gates, counts):
     rows = slots.shape[0] * slots.shape[1]
     return call(
-        weight_kernel, jax.ShapeDtypeStruct((3, counts.shape[0], rows), BF), [VMEM] * 3, VMEM
+        weight_kernel, jax.ShapeDtypeStruct((2, counts.shape[0], rows), BF), [VMEM] * 3, VMEM
     )(slots, gates, counts)
 
 
-def finish_kernel(weights, returned, out):
-    rows = returned[...]
-    total = dot(weights[2], rows) + dot(weights[1], rows)
-    out[...] = (total + dot(weights[0], rows)).astype(BF)
+def finish_kernel(weights, returned, out, held, sems):
+    tokens, width = held.shape
+    step = width // 2
+    high, low = weights[0], weights[1]
+    sends = []
+    for n in range(2):
+        part = pl.ds(n * step, step)
+        rows = returned[:, part]
+        held[:, part] = (dot(low, rows) + dot(high, rows)).astype(BF)
+        sends.append(pltpu.make_async_copy(held.at[:, part], out.at[:, part], sems.at[n]))
+        sends[-1].start()
+    for send in sends:
+        send.wait()
 
 
 def finish(weights, returned):
+    shape = (weights.shape[1], returned.shape[1])
     return call(
         finish_kernel,
-        jax.ShapeDtypeStruct((weights.shape[1], returned.shape[1]), BF),
+        jax.ShapeDtypeStruct(shape, BF),
         [VMEM] * 2,
-        VMEM,
+        ANY,
+        scratch_shapes=[pltpu.VMEM(shape, BF), pltpu.SemaphoreType.DMA((2,))],
     )(weights, returned)
 
 
@@ -330,21 +360,21 @@
     for d in range(NY):
         block = first if d == far else pack(d, *weights)
         blocks.append(lax.ppermute(block, "y", [(j, (j + d) % NY) for j in range(NY)]) if d else block)
-    arrived = lax.all_to_all(picked.reshape(-1, 8, width), E, 0, 0, tiled=True).reshape(rows, width)
+    arrived = exchange(picked.reshape(-1, 8, width)).reshape(rows, width)
     arrived, early = lax.optimization_barrier((arrived, ready(blocks[0], blocks[far])))
     other = swap_cores(arrived)
     parts = partial_sums(arrived, other, blocks, early)
-    sums = lax.all_to_all(parts, "y", 0, 0, tiled=True)
-    hidden = lax.all_to_all(hidden_copies(sums), "y", 0, 0, tiled=True)
+    sums = exchange_y(parts)
+    hidden = exchange_y(hidden_copies(sums))
     give = swap_cores(out_sums(hidden, blocks, width, False))
     keep = out_sums(hidden, blocks, width, True)
     result = result_rows(keep, give)
-    returned = lax.all_to_all(result.reshape(-1, 8, width), E, 0, 0, tiled=True)
+    returned = exchange(result.reshape(-1, 8, width))
     return finish(token_weights(names, gates, counts.reshape(-1, 1)), returned.reshape(rows, width))
 
 
 def solution(mesh):
-    fine = Mesh(np.asarray(mesh.devices).reshape(4, 16, NY, 2), ("x", "z", "y", "core"))
+    fine = Mesh(np.asarray(mesh.devices).reshape(NX * NZ, NY, 2), (E, "y", "core"))
     return jax.shard_map(
         local,
         mesh=fine,

time: 139 us -> 132 us (0.950)
  waiting for transfers between devices: 49.9 us -> 37.9 us
  starting transfers between devices: 42.3 us -> 49.7 us
  blocking collectives: 29.9 us -> 27.4 us
    all_to_all x2, waiting for transfers between devices: 48.2 us -> 36.2 us  [exchange(): return lax.all_to_all(rows, E, 0, 0, axis_index_groups=[order], tiled=True)]
    all_to_all x2, starting transfers between devices: 26.3 us -> 33.7 us  [exchange(): return lax.all_to_all(rows, E, 0, 0, axis_index_groups=[order], tiled=True)]
    all_to_all x2, blocking collectives: 29.9 us -> 27.4 us  [exchange_y(): lax.all_to_all(blocks, 'y', 0, 0, axis_index_groups=[order], tiled=True)]
  transfers between devices with their start and end apart: 7 -> 7, of which waited for: 4 -> 4; matrix products, arithmetic and copies ran while one was open for 0% -> 0% of each run, Pallas kernels for 6% -> 7%
where the time goes in v5:
time: 132 us; the launch traced here: 131 us
  starting transfers between devices  49.7 us (38%)
  waiting for transfers between devices  37.9 us (29%)
  blocking collectives  27.4 us (21%)
  Pallas kernels  14.4 us (11%)
    all_to_all x2, waiting for transfers between devices, exchange(): return lax.all_to_all(rows, E, 0, 0, axis_index_groups=[order], tiled=True)  36.2 us
    all_to_all x2, starting transfers between devices, exchange(): return lax.all_to_all(rows, E, 0, 0, axis_index_groups=[order], tiled=True)  33.7 us
    all_to_all x2, blocking collectives, exchange_y(): lax.all_to_all(blocks, 'y', 0, 0, axis_index_groups=[order], tiled=True)  27.4 us
    ppermute x3, starting transfers between devices, local(): lax.ppermute(block, 'y', [(j, (j + d) % NY) for j in range(NY)])  12.2 us
    pallas_call x3, Pallas kernels, pack(): call(functools.partial(pack_kernel, d), jax.ShapeDtypeStruct((3, group, H...  6.13 us
    ppermute x2, starting transfers between devices, swap_cores(): return lax.ppermute(a, 'core', [(0, 1), (1, 0)])  3.83 us
  transfers between devices with their start and end apart: 7, of which 4 were waited for; matrix products, arithmetic and copies ran while one was open for 0% of the time, Pallas kernels for 7%

profile of v5, /device:TPU:6, one launch (start us, length us, event | category | flops | bytes accessed | tf_op | source)
XLA Modules:
  0.0 130.9 jit_solution(8169539968456072180)
XLA Ops:
  0.0 2.6 %shard_map.74 = (bf16[512,512]{1,0:T(8,128)(2,1)}, bf16[3,1024,128]{2,1,0:T(8,128)(2,1)}) custom-call(s32[8,64]{1,0:T(8,128)} %bitcast.15, bf16[128,4096]{1,0:T(8,128)(2,1)} %tokens.1, bf16[4096,128]{1,0:T(8,128)(2,1)} %bitcast.18, bf16[4096,128]{1,0:T(8,128)(2,1)} %bitcast.22, bf16[128,4096]{1,0:T(8,128)(2,1)} %bitcast.26), custom_call_target="tpu_custom_call" | custom-call | bytes 5242880 | tf_op jit(solution)/shard_map/pallas_call | solution.py:136
  2.6 5.1 %collective-permute-start = (bf16[3,1024,128]{2,1,0:T(8,128)(2,1)}, bf16[3,1024,128]{2,1,0:T(8,128)(2,1)S(1)}, u32[]{:S(2)}, u32[]{:S(2)}) collective-permute-start(bf16[3,1024,128]{2,1,0:T(8,128)(2,1)} %get-tuple-element.10), channel_id=1, source_target_pairs={{0,4},{2,6},{4,0},{6,2},{1,5},{3,7},{5,1},{7,3},{8,12},{10,14},{12... | collective-permute-start | bytes 2359304 | tf_op jit(solution)/shard_map/ppermute | solution.py:362
  7.7 19.5 %all-to-all-start = ((bf16[64,8,512]{2,1,0:T(8,128)(2,1)}), bf16[64,8,512]{2,1,0:T(8,128)(2,1)}, u32[]{:S(2)}, u32[]{:S(2)}) async-start(bf16[64,8,512]{2,1,0:T(8,128)(2,1)} %bitcast.30), calls=%async_computation | async-start | bytes 1048576 | tf_op jit(solution)/shard_map/all_to_all | solution.py:71
  27.3 2.0 %shard_map.77 = bf16[3,1024,128]{2,1,0:T(8,128)(2,1)} custom-call(bf16[4096,128]{1,0:T(8,128)(2,1)} %bitcast.19, bf16[4096,128]{1,0:T(8,128)(2,1)} %bitcast.23, bf16[128,4096]{1,0:T(8,128)(2,1)} %bitcast.27), custom_call_target="tpu_custom_call" | custom-call | bytes 1048576 | tf_op jit(solution)/shard_map/pallas_call | solution.py:165
  29.3 2.6 %collective-permute-start.2 = (bf16[3,1024,128]{2,1,0:T(8,128)(2,1)}, bf16[3,1024,128]{2,1,0:T(8,128)(2,1)S(1)}, u32[]{:S(2)}, u32[]{:S(2)}) collective-permute-start(bf16[3,1024,128]{2,1,0:T(8,128)(2,1)} %shard_map.77), channel_id=1, source_target_pairs={{0,2},{2,4},{4,6},{6,0},{1,3},{3,5},{5,7},{7,1},{8,10},{10,12},{12... | collective-permute-start | bytes 2359304 | tf_op jit(solution)/shard_map/ppermute | solution.py:362
  31.9 2.0 %shard_map.78 = bf16[3,1024,128]{2,1,0:T(8,128)(2,1)} custom-call(bf16[4096,128]{1,0:T(8,128)(2,1)} %bitcast.20, bf16[4096,128]{1,0:T(8,128)(2,1)} %bitcast.24, bf16[128,4096]{1,0:T(8,128)(2,1)} %bitcast.28), custom_call_target="tpu_custom_call" | custom-call | bytes 1048576 | tf_op jit(solution)/shard_map/pallas_call | solution.py:165
  33.9 4.5 %collective-permute-start.3 = (bf16[3,1024,128]{2,1,0:T(8,128)(2,1)}, bf16[3,1024,128]{2,1,0:T(8,128)(2,1)S(1)}, u32[]{:S(2)}, u32[]{:S(2)}) collective-permute-start(bf16[3,1024,128]{2,1,0:T(8,128)(2,1)} %shard_map.78), channel_id=1, source_target_pairs={{0,6},{2,0},{4,2},{6,4},{1,7},{3,1},{5,3},{7,5},{8,14},{10,8},{12,... | collective-permute-start | bytes 2359304 | tf_op jit(solution)/shard_map/ppermute | solution.py:362
  38.4 2.1 %shard_map.75.first.w0 = bf16[3,1024,128]{2,1,0:T(8,128)(2,1)} custom-call(bf16[4096,128]{1,0:T(8,128)(2,1)} %bitcast.21, bf16[4096,128]{1,0:T(8,128)(2,1)} %bitcast.25, bf16[128,4096]{1,0:T(8,128)(2,1)} %bitcast.29), custom_call_target="tpu_custom_call" | custom-call | bytes 1048576 | tf_op jit(solution)/shard_map/pallas_call | solution.py:165
  40.5 0.0 collective-permute-done.second.w2
  40.5 1.1 copy-done
  41.7 10.8 %all-to-all-done = bf16[64,8,512]{2,1,0:T(8,128)(2,1)} async-done(((bf16[64,8,512]{2,1,0:T(8,128)(2,1)}), bf16[64,8,512]{2,1,0:T(8,128)(2,1)}, u32[]{:S(2)}, u32[]{:S(2)}) %all-to-all-start) | async-done | bytes 524320 | tf_op jit(solution)/shard_map/all_to_all | solution.py:71
  52.4 1.9 %collective-permute-start.1 = (bf16[512,512]{1,0:T(8,128)(2,1)}, bf16[512,512]{1,0:T(8,128)(2,1)S(1)}, u32[]{:S(2)}, u32[]{:S(2)}) collective-permute-start(bf16[512,512]{1,0:T(8,128)(2,1)} %bitcast.10.rows), channel_id=1, source_target_pairs={{0,1},{1,0},{2,3},{3,2},{4,5},{5,4},{6,7},{7,6},{8,9},{9,8},{10,11... | collective-permute-start | bytes 1572872 | tf_op jit(solution)/shard_map/ppermute | solution.py:45
  54.3 0.0 collective-permute-done.3.w3
  54.4 1.7 %shard_map.79.half = f32[4,512,256]{2,1,0:T(8,128)S(1)} custom-call(bf16[512,512]{1,0:T(8,128)(2,1)} %bitcast.10.rows, bf16[3,1024,128]{2,1,0:T(8,128)(2,1)S(1)} %copy-done.1, bf16[3,1024,128]{2,1,0:T(8,128)(2,1)S(1)} %collective-permute-done.2.w1, bf16[3,1024,128]{2,1,0:T(8,128)(2,1)S(1)} %collective-permute-done.second.w2, ...), custom_call_target="tpu_custom_call" | custom-call | flops 536870912 | bytes 1048576 | tf_op jit(solution)/shard_map/pallas_call | solution.py:222
  56.1 0.3 collective-permute-done.1.rows
  56.4 0.7 shard_map.80
  57.1 17.1 %all_to_all.20.sums = bf16[4,512,256]{2,1,0:T(8,128)(2,1)S(1)} all-to-all(bf16[4,512,256]{2,1,0:T(8,128)(2,1)S(1)} %shard_map.80), channel_id=1, replica_groups={{4,6,0,2},{5,7,1,3},{12,14,8,10},{13,15,9,11},{20,22,16,18},{21,23,17,1..., dimensions={0} | all-to-all | bytes 2097152 | tf_op jit(solution)/shard_map/all_to_all | solution.py:76
  74.2 0.2 shard_map.81
  74.4 10.3 %all_to_all.21.hidden = bf16[4,512,128]{2,1,0:T(8,128)(2,1)S(1)} all-to-all(bf16[4,512,128]{2,1,0:T(8,128)(2,1)S(1)} %shard_map.81), channel_id=1, replica_groups={{4,6,0,2},{5,7,1,3},{12,14,8,10},{13,15,9,11},{20,22,16,18},{21,23,17,1..., dimensions={0} | all-to-all | bytes 1048576 | tf_op jit(solution)/shard_map/all_to_all | solution.py:76
  84.7 0.4 shard_map.83
  85.2 1.9 %collective-permute-start.4 = (bf16[512,512]{1,0:T(8,128)(2,1)S(1)}, bf16[512,512]{1,0:T(8,128)(2,1)S(1)}, u32[]{:S(2)}, u32[]{:S(2)}) collective-permute-start(bf16[512,512]{1,0:T(8,128)(2,1)S(1)} %shard_map.83), channel_id=1, source_target_pairs={{0,1},{1,0},{2,3},{3,2},{4,5},{5,4},{6,7},{7,6},{8,9},{9,8},{10,11... | collective-permute-start | bytes 1572872 | tf_op jit(solution)/shard_map/ppermute | solution.py:45
  87.1 0.5 shard_map.82.keep
  87.6 0.0 copy-start.4
  87.6 0.0 copy-start.2
  87.6 0.0 copy-start.3
  87.6 1.4 %collective-permute-done.4.given = bf16[512,512]{1,0:T(8,128)(2,1)S(1)} collective-permute-done((bf16[512,512]{1,0:T(8,128)(2,1)S(1)}, bf16[512,512]{1,0:T(8,128)(2,1)S(1)}, u32[]{:S(2)}, u32[]{:S(2)}) %collective-permute-start.4) | collective-permute-done | bytes 524320 | tf_op jit(solution)/shard_map/ppermute | solution.py:45
  89.0 0.9 shard_map.84
  89.8 14.2 %all-to-all-start.3 = ((bf16[64,8,512]{2,1,0:T(8,128)(2,1)}), bf16[64,8,512]{2,1,0:T(8,128)(2,1)S(1)}, u32[]{:S(2)}, u32[]{:S(2)}) async-start(bf16[64,8,512]{2,1,0:T(8,128)(2,1)} %bitcast.11), calls=%async_computation.3 | async-start | bytes 1048576 | tf_op jit(solution)/shard_map/all_to_all | solution.py:71
  104.1 0.1 copy.8.counts
  104.2 0.2 shard_map.73.weights
  104.4 25.5 %all-to-all-done.3 = bf16[64,8,512]{2,1,0:T(8,128)(2,1)S(1)} async-done(((bf16[64,8,512]{2,1,0:T(8,128)(2,1)}), bf16[64,8,512]{2,1,0:T(8,128)(2,1)S(1)}, u32[]{:S(2)}, u32[]{:S(2)}) %all-to-all-start.3) | async-done | bytes 524320 | tf_op jit(solution)/shard_map/all_to_all | solution.py:71
  129.9 1.0 shard_map.85
  (8 shorter events, 0.0 us)
Async XLA Ops:
  2.6 37.9 %collective-permute-start = (bf16[3,1024,128]{2,1,0:T(8,128)(2,1)}, bf16[3,1024,128]{2,1,0:T(8,128)(2,1)S(1)}, u32[]{:S(2)}, u32[]{:S(2)}) collective-permute-start(bf16[3,1024,128]{2,1,0:T(8,128)(2,1)} %get-tuple-element.10), channel_id=1, source_target_pairs={{0,4},{2,6},{4,0},{6,2},{1,5},{3,7},{5,1},{7,3},{8,12},{10,14},{12... | collective-permute-start | bytes 2359304 | tf_op jit(solution)/shard_map/ppermute | solution.py:362
  7.7 44.7 %all-to-all-start = ((bf16[64,8,512]{2,1,0:T(8,128)(2,1)}), bf16[64,8,512]{2,1,0:T(8,128)(2,1)}, u32[]{:S(2)}, u32[]{:S(2)}) async-start(bf16[64,8,512]{2,1,0:T(8,128)(2,1)} %bitcast.30), calls=%async_computation | async-start | bytes 1048576 | tf_op jit(solution)/shard_map/all_to_all | solution.py:71
  29.3 25.0 %collective-permute-start.2 = (bf16[3,1024,128]{2,1,0:T(8,128)(2,1)}, bf16[3,1024,128]{2,1,0:T(8,128)(2,1)S(1)}, u32[]{:S(2)}, u32[]{:S(2)}) collective-permute-start(bf16[3,1024,128]{2,1,0:T(8,128)(2,1)} %shard_map.77), channel_id=1, source_target_pairs={{0,2},{2,4},{4,6},{6,0},{1,3},{3,5},{5,7},{7,1},{8,10},{10,12},{12... | collective-permute-start | bytes 2359304 | tf_op jit(solution)/shard_map/ppermute | solution.py:362
  33.9 20.4 %collective-permute-start.3 = (bf16[3,1024,128]{2,1,0:T(8,128)(2,1)}, bf16[3,1024,128]{2,1,0:T(8,128)(2,1)S(1)}, u32[]{:S(2)}, u32[]{:S(2)}) collective-permute-start(bf16[3,1024,128]{2,1,0:T(8,128)(2,1)} %shard_map.78), channel_id=1, source_target_pairs={{0,6},{2,0},{4,2},{6,4},{1,7},{3,1},{5,3},{7,5},{8,14},{10,8},{12,... | collective-permute-start | bytes 2359304 | tf_op jit(solution)/shard_map/ppermute | solution.py:362
  40.5 1.1 copy-start
  41.6 12.7 %copy-start.1 = (bf16[3,1024,128]{2,1,0:T(8,128)(2,1)S(1)}, bf16[3,1024,128]{2,1,0:T(8,128)(2,1)}, u32[]{:S(2)}) copy-start(bf16[3,1024,128]{2,1,0:T(8,128)(2,1)} %shard_map.75.first.w0) | copy-start | bytes 2359300
  52.4 4.0 %collective-permute-start.1 = (bf16[512,512]{1,0:T(8,128)(2,1)}, bf16[512,512]{1,0:T(8,128)(2,1)S(1)}, u32[]{:S(2)}, u32[]{:S(2)}) collective-permute-start(bf16[512,512]{1,0:T(8,128)(2,1)} %bitcast.10.rows), channel_id=1, source_target_pairs={{0,1},{1,0},{2,3},{3,2},{4,5},{5,4},{6,7},{7,6},{8,9},{9,8},{10,11... | collective-permute-start | bytes 1572872 | tf_op jit(solution)/shard_map/ppermute | solution.py:45
  85.2 3.8 %collective-permute-start.4 = (bf16[512,512]{1,0:T(8,128)(2,1)S(1)}, bf16[512,512]{1,0:T(8,128)(2,1)S(1)}, u32[]{:S(2)}, u32[]{:S(2)}) collective-permute-start(bf16[512,512]{1,0:T(8,128)(2,1)S(1)} %shard_map.83), channel_id=1, source_target_pairs={{0,1},{1,0},{2,3},{3,2},{4,5},{5,4},{6,7},{7,6},{8,9},{9,8},{10,11... | collective-permute-start | bytes 1572872 | tf_op jit(solution)/shard_map/ppermute | solution.py:45
  87.6 16.5 %copy-start.4 = (s32[128]{0:T(128)S(1)}, s32[128]{0:T(128)}, u32[]{:S(2)}) copy-start(s32[128]{0:T(128)} %param.10) | copy-start | bytes 1540
  87.6 16.6 %copy-start.2 = (s32[64,1,8]{0,2,1:T(8,128)S(1)}, s32[64,1,8]{0,2,1:T(8,128)}, u32[]{:S(2)}) copy-start(s32[64,1,8]{0,2,1:T(8,128)} %param.8) | copy-start | bytes 6148
  87.6 16.6 %copy-start.3 = (f32[64,1,8]{0,2,1:T(8,128)S(1)}, f32[64,1,8]{0,2,1:T(8,128)}, u32[]{:S(2)}) copy-start(f32[64,1,8]{0,2,1:T(8,128)} %param.9) | copy-start | bytes 6148
  89.8 40.1 %all-to-all-start.3 = ((bf16[64,8,512]{2,1,0:T(8,128)(2,1)}), bf16[64,8,512]{2,1,0:T(8,128)(2,1)S(1)}, u32[]{:S(2)}, u32[]{:S(2)}) async-start(bf16[64,8,512]{2,1,0:T(8,128)(2,1)} %bitcast.11), calls=%async_computation.3 | async-start | bytes 1048576 | tf_op jit(solution)/shard_map/all_to_all | solution.py:71

commit v6 on v5

--- a/solution.py
+++ b/solution.py
@@ -10,7 +10,7 @@
 
 E = "expert"
 NX, NZ = 4, 16
-X0, Z0, Y0 = 0, 11, 2
+X0, Z0, Y_SUMS, Y_HIDDEN = 0, 11, 3, 2
 S = ("y", "core")
 NY = 4
 HS = 128
@@ -71,13 +71,13 @@
     return lax.all_to_all(rows, E, 0, 0, axis_index_groups=[order], tiled=True)
 
 
-def exchange_y(blocks):
-    order = [(place + Y0) % NY for place in range(NY)]
+def exchange_y(blocks, y0):
+    order = [(place + y0) % NY for place in range(NY)]
     return lax.all_to_all(blocks, "y", 0, 0, axis_index_groups=[order], tiled=True)
 
 
-def place_y(y, d):
-    return lax.rem(y + 2 * NY - d - Y0, NY)
+def place_y(y, d, y0):
+    return lax.rem(y + 2 * NY - d - y0, NY)
 
 
 def spread(values, rows):
@@ -111,9 +111,12 @@
     fetch_slots.wait()
     names = spread(slots[...].astype(F32), rows)
     hit = (names == token).astype(BF)
+    for copy in copies:
+        copy.wait()
+    sends = [pltpu.make_async_copy(held, block, out_sems.at[4])]
+    sends[0].start()
     fetch.wait()
     step = rows // 4
-    sends = []
     for n in range(4):
         part = pl.ds(n * step, step)
         rows_out[part] = lax.dot_general(
@@ -121,10 +124,6 @@
         ).astype(BF)
         sends.append(pltpu.make_async_copy(rows_out.at[part], picked.at[part], out_sems.at[n]))
         sends[-1].start()
-    for copy in copies:
-        copy.wait()
-    sends.append(pltpu.make_async_copy(held, block, out_sems.at[4]))
-    sends[-1].start()
     for send in sends:
         send.wait()
 
@@ -195,7 +194,7 @@
     step = 256
     part = pl.ds(pl.multiple_of(c * width, width), width)
     for d, w in enumerate((w0, w1, w2, w3)):
-        owner = place_y(y, d)
+        owner = place_y(y, d, Y_SUMS)
         a = jnp.concatenate([w[0, part], w[1, part]], axis=1)
         for r in range(0, rows.shape[0], step):
             at = pl.ds(r, step)
@@ -208,7 +207,7 @@
     step = 256
     part = pl.ds(pl.multiple_of((1 - c) * width, width), width)
     for d, w in enumerate((w0, w1, w2, w3)):
-        owner = place_y(y, d)
+        owner = place_y(y, d, Y_SUMS)
         a = jnp.concatenate([w[0, part], w[1, part]], axis=1)
         for r in range(0, rows.shape[0], step):
             at = pl.ds(r, step)
@@ -248,7 +247,7 @@
     rows = hidden.shape[1]
     width = out.shape[1]
     first = (c if mine else 1 - c) * width
-    owners = [place_y(y, d) for d in range(NY)]
+    owners = [place_y(y, d, Y_HIDDEN) for d in range(NY)]
     a = jnp.concatenate([hidden[k] for k in owners], axis=1)
     for j in range(0, width, 2 * HS):
         one = pl.multiple_of(first + j, HS)
@@ -364,8 +363,8 @@
     arrived, early = lax.optimization_barrier((arrived, ready(blocks[0], blocks[far])))
     other = swap_cores(arrived)
     parts = partial_sums(arrived, other, blocks, early)
-    sums = exchange_y(parts)
-    hidden = exchange_y(hidden_copies(sums))
+    sums = exchange_y(parts, Y_SUMS)
+    hidden = exchange_y(hidden_copies(sums), Y_HIDDEN)
     give = swap_cores(out_sums(hidden, blocks, width, False))
     keep = out_sums(hidden, blocks, width, True)
     result = result_rows(keep, give)

time: 132 us -> 132 us (level)
  no operation moved by 1% of the time
where the time goes in v6:
time: 132 us; the launch traced here: 131 us
  starting transfers between devices  49.8 us (38%)
  waiting for transfers between devices  37.9 us (29%)
  blocking collectives  27.3 us (21%)
  Pallas kernels  14.1 us (11%)
    all_to_all x2, waiting for transfers between devices, exchange(): return lax.all_to_all(rows, E, 0, 0, axis_index_groups=[order], tiled=True)  36.2 us
    all_to_all x2, starting transfers between devices, exchange(): return lax.all_to_all(rows, E, 0, 0, axis_index_groups=[order], tiled=True)  33.8 us
    all_to_all x2, blocking collectives, exchange_y(): lax.all_to_all(blocks, 'y', 0, 0, axis_index_groups=[order], tiled=True)  27.3 us
    ppermute x3, starting transfers between devices, local(): lax.ppermute(block, 'y', [(j, (j + d) % NY) for j in range(NY)])  12.2 us
    pallas_call x3, Pallas kernels, pack(): call(functools.partial(pack_kernel, d), jax.ShapeDtypeStruct((3, group, H...  6.13 us
    ppermute x2, starting transfers between devices, swap_cores(): return lax.ppermute(a, 'core', [(0, 1), (1, 0)])  3.83 us
  transfers between devices with their start and end apart: 7, of which 4 were waited for; matrix products, arithmetic and copies ran while one was open for 0% of the time, Pallas kernels for 7%

profile of v6, /device:TPU:6, one launch (start us, length us, event | category | flops | bytes accessed | tf_op | source)
XLA Modules:
  0.0 130.7 jit_solution(17832791211695926797)
XLA Ops:
  0.0 2.3 %shard_map.74 = (bf16[512,512]{1,0:T(8,128)(2,1)}, bf16[3,1024,128]{2,1,0:T(8,128)(2,1)}) custom-call(s32[8,64]{1,0:T(8,128)} %bitcast.15, bf16[128,4096]{1,0:T(8,128)(2,1)} %tokens.1, bf16[4096,128]{1,0:T(8,128)(2,1)} %bitcast.18, bf16[4096,128]{1,0:T(8,128)(2,1)} %bitcast.22, bf16[128,4096]{1,0:T(8,128)(2,1)} %bitcast.26), custom_call_target="tpu_custom_call" | custom-call | bytes 5242880 | tf_op jit(solution)/shard_map/pallas_call | solution.py:135
  2.3 5.1 %collective-permute-start = (bf16[3,1024,128]{2,1,0:T(8,128)(2,1)}, bf16[3,1024,128]{2,1,0:T(8,128)(2,1)S(1)}, u32[]{:S(2)}, u32[]{:S(2)}) collective-permute-start(bf16[3,1024,128]{2,1,0:T(8,128)(2,1)} %get-tuple-element.10), channel_id=1, source_target_pairs={{0,4},{2,6},{4,0},{6,2},{1,5},{3,7},{5,1},{7,3},{8,12},{10,14},{12... | collective-permute-start | bytes 2359304 | tf_op jit(solution)/shard_map/ppermute | solution.py:361
  7.5 19.5 %all-to-all-start = ((bf16[64,8,512]{2,1,0:T(8,128)(2,1)}), bf16[64,8,512]{2,1,0:T(8,128)(2,1)}, u32[]{:S(2)}, u32[]{:S(2)}) async-start(bf16[64,8,512]{2,1,0:T(8,128)(2,1)} %bitcast.30), calls=%async_computation | async-start | bytes 1048576 | tf_op jit(solution)/shard_map/all_to_all | solution.py:71
  27.0 2.0 %shard_map.77 = bf16[3,1024,128]{2,1,0:T(8,128)(2,1)} custom-call(bf16[4096,128]{1,0:T(8,128)(2,1)} %bitcast.19, bf16[4096,128]{1,0:T(8,128)(2,1)} %bitcast.23, bf16[128,4096]{1,0:T(8,128)(2,1)} %bitcast.27), custom_call_target="tpu_custom_call" | custom-call | bytes 1048576 | tf_op jit(solution)/shard_map/pallas_call | solution.py:164
  29.0 2.6 %collective-permute-start.2 = (bf16[3,1024,128]{2,1,0:T(8,128)(2,1)}, bf16[3,1024,128]{2,1,0:T(8,128)(2,1)S(1)}, u32[]{:S(2)}, u32[]{:S(2)}) collective-permute-start(bf16[3,1024,128]{2,1,0:T(8,128)(2,1)} %shard_map.77), channel_id=1, source_target_pairs={{0,2},{2,4},{4,6},{6,0},{1,3},{3,5},{5,7},{7,1},{8,10},{10,12},{12... | collective-permute-start | bytes 2359304 | tf_op jit(solution)/shard_map/ppermute | solution.py:361
  31.6 2.0 %shard_map.78 = bf16[3,1024,128]{2,1,0:T(8,128)(2,1)} custom-call(bf16[4096,128]{1,0:T(8,128)(2,1)} %bitcast.20, bf16[4096,128]{1,0:T(8,128)(2,1)} %bitcast.24, bf16[128,4096]{1,0:T(8,128)(2,1)} %bitcast.28), custom_call_target="tpu_custom_call" | custom-call | bytes 1048576 | tf_op jit(solution)/shard_map/pallas_call | solution.py:164
  33.7 4.5 %collective-permute-start.3 = (bf16[3,1024,128]{2,1,0:T(8,128)(2,1)}, bf16[3,1024,128]{2,1,0:T(8,128)(2,1)S(1)}, u32[]{:S(2)}, u32[]{:S(2)}) collective-permute-start(bf16[3,1024,128]{2,1,0:T(8,128)(2,1)} %shard_map.78), channel_id=1, source_target_pairs={{0,6},{2,0},{4,2},{6,4},{1,7},{3,1},{5,3},{7,5},{8,14},{10,8},{12,... | collective-permute-start | bytes 2359304 | tf_op jit(solution)/shard_map/ppermute | solution.py:361
  38.1 2.1 %shard_map.75.first.w0 = bf16[3,1024,128]{2,1,0:T(8,128)(2,1)} custom-call(bf16[4096,128]{1,0:T(8,128)(2,1)} %bitcast.21, bf16[4096,128]{1,0:T(8,128)(2,1)} %bitcast.25, bf16[128,4096]{1,0:T(8,128)(2,1)} %bitcast.29), custom_call_target="tpu_custom_call" | custom-call | bytes 1048576 | tf_op jit(solution)/shard_map/pallas_call | solution.py:164
  40.2 0.0 collective-permute-done.second.w2
  40.2 1.1 copy-done
  41.4 10.8 %all-to-all-done = bf16[64,8,512]{2,1,0:T(8,128)(2,1)} async-done(((bf16[64,8,512]{2,1,0:T(8,128)(2,1)}), bf16[64,8,512]{2,1,0:T(8,128)(2,1)}, u32[]{:S(2)}, u32[]{:S(2)}) %all-to-all-start) | async-done | bytes 524320 | tf_op jit(solution)/shard_map/all_to_all | solution.py:71
  52.1 1.9 %collective-permute-start.1 = (bf16[512,512]{1,0:T(8,128)(2,1)}, bf16[512,512]{1,0:T(8,128)(2,1)S(1)}, u32[]{:S(2)}, u32[]{:S(2)}) collective-permute-start(bf16[512,512]{1,0:T(8,128)(2,1)} %bitcast.10.rows), channel_id=1, source_target_pairs={{0,1},{1,0},{2,3},{3,2},{4,5},{5,4},{6,7},{7,6},{8,9},{9,8},{10,11... | collective-permute-start | bytes 1572872 | tf_op jit(solution)/shard_map/ppermute | solution.py:45
  54.1 0.0 collective-permute-done.3.w3
  54.1 1.7 %shard_map.79.half = f32[4,512,256]{2,1,0:T(8,128)S(1)} custom-call(bf16[512,512]{1,0:T(8,128)(2,1)} %bitcast.10.rows, bf16[3,1024,128]{2,1,0:T(8,128)(2,1)S(1)} %copy-done.1, bf16[3,1024,128]{2,1,0:T(8,128)(2,1)S(1)} %collective-permute-done.2.w1, bf16[3,1024,128]{2,1,0:T(8,128)(2,1)S(1)} %collective-permute-done.second.w2, ...), custom_call_target="tpu_custom_call" | custom-call | flops 536870912 | bytes 1048576 | tf_op jit(solution)/shard_map/pallas_call | solution.py:221
  55.9 0.3 collective-permute-done.1.rows
  56.1 0.7 shard_map.80
  56.9 17.8 %all_to_all.20.sums = bf16[4,512,256]{2,1,0:T(8,128)(2,1)S(1)} all-to-all(bf16[4,512,256]{2,1,0:T(8,128)(2,1)S(1)} %shard_map.80), channel_id=1, replica_groups={{6,0,2,4},{7,1,3,5},{14,8,10,12},{15,9,11,13},{22,16,18,20},{23,17,19,2..., dimensions={0} | all-to-all | bytes 2097152 | tf_op jit(solution)/shard_map/all_to_all | solution.py:76
  74.7 0.2 shard_map.81
  74.9 9.5 %all_to_all.21.hidden = bf16[4,512,128]{2,1,0:T(8,128)(2,1)S(1)} all-to-all(bf16[4,512,128]{2,1,0:T(8,128)(2,1)S(1)} %shard_map.81), channel_id=1, replica_groups={{4,6,0,2},{5,7,1,3},{12,14,8,10},{13,15,9,11},{20,22,16,18},{21,23,17,1..., dimensions={0} | all-to-all | bytes 1048576 | tf_op jit(solution)/shard_map/all_to_all | solution.py:76
  84.4 0.4 shard_map.83
  84.8 1.9 %collective-permute-start.4 = (bf16[512,512]{1,0:T(8,128)(2,1)S(1)}, bf16[512,512]{1,0:T(8,128)(2,1)S(1)}, u32[]{:S(2)}, u32[]{:S(2)}) collective-permute-start(bf16[512,512]{1,0:T(8,128)(2,1)S(1)} %shard_map.83), channel_id=1, source_target_pairs={{0,1},{1,0},{2,3},{3,2},{4,5},{5,4},{6,7},{7,6},{8,9},{9,8},{10,11... | collective-permute-start | bytes 1572872 | tf_op jit(solution)/shard_map/ppermute | solution.py:45
  86.8 0.5 shard_map.82.keep
  87.2 0.0 copy-start.4
  87.2 0.0 copy-start.2
  87.2 0.0 copy-start.3
  87.3 1.4 %collective-permute-done.4.given = bf16[512,512]{1,0:T(8,128)(2,1)S(1)} collective-permute-done((bf16[512,512]{1,0:T(8,128)(2,1)S(1)}, bf16[512,512]{1,0:T(8,128)(2,1)S(1)}, u32[]{:S(2)}, u32[]{:S(2)}) %collective-permute-start.4) | collective-permute-done | bytes 524320 | tf_op jit(solution)/shard_map/ppermute | solution.py:45
  88.6 0.9 shard_map.84
  89.5 14.3 %all-to-all-start.3 = ((bf16[64,8,512]{2,1,0:T(8,128)(2,1)}), bf16[64,8,512]{2,1,0:T(8,128)(2,1)S(1)}, u32[]{:S(2)}, u32[]{:S(2)}) async-start(bf16[64,8,512]{2,1,0:T(8,128)(2,1)} %bitcast.11), calls=%async_computation.3 | async-start | bytes 1048576 | tf_op jit(solution)/shard_map/all_to_all | solution.py:71
  103.8 0.1 copy.8.counts
  104.0 0.2 shard_map.73.weights
  104.2 25.5 %all-to-all-done.3 = bf16[64,8,512]{2,1,0:T(8,128)(2,1)S(1)} async-done(((bf16[64,8,512]{2,1,0:T(8,128)(2,1)}), bf16[64,8,512]{2,1,0:T(8,128)(2,1)S(1)}, u32[]{:S(2)}, u32[]{:S(2)}) %all-to-all-start.3) | async-done | bytes 524320 | tf_op jit(solution)/shard_map/all_to_all | solution.py:71
  129.7 1.0 shard_map.85
  (8 shorter events, 0.0 us)
Async XLA Ops:
  2.3 37.9 %collective-permute-start = (bf16[3,1024,128]{2,1,0:T(8,128)(2,1)}, bf16[3,1024,128]{2,1,0:T(8,128)(2,1)S(1)}, u32[]{:S(2)}, u32[]{:S(2)}) collective-permute-start(bf16[3,1024,128]{2,1,0:T(8,128)(2,1)} %get-tuple-element.10), channel_id=1, source_target_pairs={{0,4},{2,6},{4,0},{6,2},{1,5},{3,7},{5,1},{7,3},{8,12},{10,14},{12... | collective-permute-start | bytes 2359304 | tf_op jit(solution)/shard_map/ppermute | solution.py:361
  7.5 44.7 %all-to-all-start = ((bf16[64,8,512]{2,1,0:T(8,128)(2,1)}), bf16[64,8,512]{2,1,0:T(8,128)(2,1)}, u32[]{:S(2)}, u32[]{:S(2)}) async-start(bf16[64,8,512]{2,1,0:T(8,128)(2,1)} %bitcast.30), calls=%async_computation | async-start | bytes 1048576 | tf_op jit(solution)/shard_map/all_to_all | solution.py:71
  29.0 25.0 %collective-permute-start.2 = (bf16[3,1024,128]{2,1,0:T(8,128)(2,1)}, bf16[3,1024,128]{2,1,0:T(8,128)(2,1)S(1)}, u32[]{:S(2)}, u32[]{:S(2)}) collective-permute-start(bf16[3,1024,128]{2,1,0:T(8,128)(2,1)} %shard_map.77), channel_id=1, source_target_pairs={{0,2},{2,4},{4,6},{6,0},{1,3},{3,5},{5,7},{7,1},{8,10},{10,12},{12... | collective-permute-start | bytes 2359304 | tf_op jit(solution)/shard_map/ppermute | solution.py:361
  33.7 20.4 %collective-permute-start.3 = (bf16[3,1024,128]{2,1,0:T(8,128)(2,1)}, bf16[3,1024,128]{2,1,0:T(8,128)(2,1)S(1)}, u32[]{:S(2)}, u32[]{:S(2)}) collective-permute-start(bf16[3,1024,128]{2,1,0:T(8,128)(2,1)} %shard_map.78), channel_id=1, source_target_pairs={{0,6},{2,0},{4,2},{6,4},{1,7},{3,1},{5,3},{7,5},{8,14},{10,8},{12,... | collective-permute-start | bytes 2359304 | tf_op jit(solution)/shard_map/ppermute | solution.py:361
  40.2 1.1 copy-start
  41.4 12.7 %copy-start.1 = (bf16[3,1024,128]{2,1,0:T(8,128)(2,1)S(1)}, bf16[3,1024,128]{2,1,0:T(8,128)(2,1)}, u32[]{:S(2)}) copy-start(bf16[3,1024,128]{2,1,0:T(8,128)(2,1)} %shard_map.75.first.w0) | copy-start | bytes 2359300
  52.1 4.0 %collective-permute-start.1 = (bf16[512,512]{1,0:T(8,128)(2,1)}, bf16[512,512]{1,0:T(8,128)(2,1)S(1)}, u32[]{:S(2)}, u32[]{:S(2)}) collective-permute-start(bf16[512,512]{1,0:T(8,128)(2,1)} %bitcast.10.rows), channel_id=1, source_target_pairs={{0,1},{1,0},{2,3},{3,2},{4,5},{5,4},{6,7},{7,6},{8,9},{9,8},{10,11... | collective-permute-start | bytes 1572872 | tf_op jit(solution)/shard_map/ppermute | solution.py:45
  84.8 3.8 %collective-permute-start.4 = (bf16[512,512]{1,0:T(8,128)(2,1)S(1)}, bf16[512,512]{1,0:T(8,128)(2,1)S(1)}, u32[]{:S(2)}, u32[]{:S(2)}) collective-permute-start(bf16[512,512]{1,0:T(8,128)(2,1)S(1)} %shard_map.83), channel_id=1, source_target_pairs={{0,1},{1,0},{2,3},{3,2},{4,5},{5,4},{6,7},{7,6},{8,9},{9,8},{10,11... | collective-permute-start | bytes 1572872 | tf_op jit(solution)/shard_map/ppermute | solution.py:45
  87.2 16.6 %copy-start.4 = (s32[128]{0:T(128)S(1)}, s32[128]{0:T(128)}, u32[]{:S(2)}) copy-start(s32[128]{0:T(128)} %param.10) | copy-start | bytes 1540
  87.2 16.7 %copy-start.2 = (s32[64,1,8]{0,2,1:T(8,128)S(1)}, s32[64,1,8]{0,2,1:T(8,128)}, u32[]{:S(2)}) copy-start(s32[64,1,8]{0,2,1:T(8,128)} %param.8) | copy-start | bytes 6148
  87.2 16.7 %copy-start.3 = (f32[64,1,8]{0,2,1:T(8,128)S(1)}, f32[64,1,8]{0,2,1:T(8,128)}, u32[]{:S(2)}) copy-start(f32[64,1,8]{0,2,1:T(8,128)} %param.9) | copy-start | bytes 6148
  89.5 40.2 %all-to-all-start.3 = ((bf16[64,8,512]{2,1,0:T(8,128)(2,1)}), bf16[64,8,512]{2,1,0:T(8,128)(2,1)S(1)}, u32[]{:S(2)}, u32[]{:S(2)}) async-start(bf16[64,8,512]{2,1,0:T(8,128)(2,1)} %bitcast.11), calls=%async_computation.3 | async-start | bytes 1048576 | tf_op jit(solution)/shard_map/all_to_all | solution.py:71

commit v7 on v6

--- a/solution.py
+++ b/solution.py
@@ -171,6 +171,42 @@
     )(gate, up, down)
 
 
+def pack_two_kernel(distances, gate, up, down, first, second, held, sems, out_sems):
+    y = position()[0]
+    copies = [
+        block_copies(lax.rem(y + d, NY), gate, up, down, held.at[n], sems.at[n])
+        for n, d in enumerate(distances)
+    ]
+    for block in copies:
+        for copy in block:
+            copy.start()
+    sends = []
+    for n, out in enumerate((first, second)):
+        for copy in copies[n]:
+            copy.wait()
+        sends.append(pltpu.make_async_copy(held.at[n], out, out_sems.at[n]))
+        sends[-1].start()
+    for send in sends:
+        send.wait()
+
+
+def pack_two(distances, gate, up, down):
+    group = gate.shape[0] // NY
+    block = jax.ShapeDtypeStruct((3, group, HS), BF)
+    return call(
+        functools.partial(pack_two_kernel, distances),
+        (block, block),
+        [ANY, ANY, ANY],
+        (ANY, ANY),
+        vmem=WHOLE,
+        scratch_shapes=[
+            pltpu.VMEM((2, 3, group, HS), BF),
+            pltpu.SemaphoreType.DMA((2, 2 + group // HS)),
+            pltpu.SemaphoreType.DMA((2,)),
+        ],
+    )(gate, up, down)
+
+
 def ready_kernel(first, second, out, sem):
     copy = pltpu.make_async_copy(first.at[0, pl.ds(0, out.shape[0])], out, sem)
     copy.start()
@@ -355,10 +391,10 @@
 
     far = 2
     picked, first = start(far, names, tokens, *weights)
-    blocks = []
-    for d in range(NY):
-        block = first if d == far else pack(d, *weights)
-        blocks.append(lax.ppermute(block, "y", [(j, (j + d) % NY) for j in range(NY)]) if d else block)
+    near, back = pack_two((1, 3), *weights)
+    blocks = [pack(0, *weights)]
+    for d, block in ((1, near), (2, first), (3, back)):
+        blocks.append(lax.ppermute(block, "y", [(j, (j + d) % NY) for j in range(NY)]))
     arrived = exchange(picked.reshape(-1, 8, width)).reshape(rows, width)
     arrived, early = lax.optimization_barrier((arrived, ready(blocks[0], blocks[far])))
     other = swap_cores(arrived)

time: 132 us -> 132 us (level)
  waiting for transfers between devices: 37.9 us -> 39.6 us
  Pallas kernels: 14.1 us -> 12.4 us
    pallas_call x3 -> x1, Pallas kernels: 6.13 us -> 2.07 us  [pack(): call(functools.partial(pack_kernel, d), jax.ShapeDtypeStruct((3, group, H...]
    pallas_call x0 -> x1, Pallas kernels: none -> 2.42 us  [pack_two(): call(functools.partial(pack_two_kernel, distances), (block, block), [ANY,...]
    all_to_all x2, waiting for transfers between devices: 36.2 us -> 37.9 us  [exchange(): return lax.all_to_all(rows, E, 0, 0, axis_index_groups=[order], tiled=True)]
  transfers between devices with their start and end apart: 7 -> 7, of which waited for: 4 -> 4; matrix products, arithmetic and copies ran while one was open for 0% -> 0% of each run, Pallas kernels for 7% -> 5%
where the time goes in v7:
time: 132 us; the launch traced here: 131 us
  starting transfers between devices  48.8 us (37%)
  waiting for transfers between devices  39.6 us (30%)
  blocking collectives  28.3 us (21%)
  Pallas kernels  12.4 us (9%)
    all_to_all x2, waiting for transfers between devices, exchange(): return lax.all_to_all(rows, E, 0, 0, axis_index_groups=[order], tiled=True)  37.9 us
    all_to_all x2, starting transfers between devices, exchange(): return lax.all_to_all(rows, E, 0, 0, axis_index_groups=[order], tiled=True)  32.8 us
    all_to_all x2, blocking collectives, exchange_y(): lax.all_to_all(blocks, 'y', 0, 0, axis_index_groups=[order], tiled=True)  28.3 us
    ppermute x3, starting transfers between devices, local(): lax.ppermute(block, 'y', [(j, (j + d) % NY) for j in range(NY)])  12.2 us
    ppermute x2, starting transfers between devices, swap_cores(): return lax.ppermute(a, 'core', [(0, 1), (1, 0)])  3.83 us
  transfers between devices with their start and end apart: 7, of which 4 were waited for; matrix products, arithmetic and copies ran while one was open for 0% of the time, Pallas kernels for 5%

profile of v7, /device:TPU:6, one launch (start us, length us, event | category | flops | bytes accessed | tf_op | source)
XLA Modules:
  0.0 130.6 jit_solution(2368329071391339794)
XLA Ops:
  0.0 2.3 %shard_map.74 = (bf16[512,512]{1,0:T(8,128)(2,1)}, bf16[3,1024,128]{2,1,0:T(8,128)(2,1)}) custom-call(s32[8,64]{1,0:T(8,128)} %bitcast.15, bf16[128,4096]{1,0:T(8,128)(2,1)} %tokens.1, bf16[4096,128]{1,0:T(8,128)(2,1)} %bitcast.18, bf16[4096,128]{1,0:T(8,128)(2,1)} %bitcast.21, bf16[128,4096]{1,0:T(8,128)(2,1)} %bitcast.24), custom_call_target="tpu_custom_call" | custom-call | bytes 5242880 | tf_op jit(solution)/shard_map/pallas_call | solution.py:135
  2.3 5.1 %collective-permute-start = (bf16[3,1024,128]{2,1,0:T(8,128)(2,1)}, bf16[3,1024,128]{2,1,0:T(8,128)(2,1)S(1)}, u32[]{:S(2)}, u32[]{:S(2)}) collective-permute-start(bf16[3,1024,128]{2,1,0:T(8,128)(2,1)} %get-tuple-element.12), channel_id=1, source_target_pairs={{0,4},{2,6},{4,0},{6,2},{1,5},{3,7},{5,1},{7,3},{8,12},{10,14},{12... | collective-permute-start | bytes 2359304 | tf_op jit(solution)/shard_map/ppermute | solution.py:397
  7.5 19.5 %all-to-all-start = ((bf16[64,8,512]{2,1,0:T(8,128)(2,1)}), bf16[64,8,512]{2,1,0:T(8,128)(2,1)}, u32[]{:S(2)}, u32[]{:S(2)}) async-start(bf16[64,8,512]{2,1,0:T(8,128)(2,1)} %bitcast.27), calls=%async_computation | async-start | bytes 1048576 | tf_op jit(solution)/shard_map/all_to_all | solution.py:71
  27.0 2.4 %shard_map.77 = (bf16[3,1024,128]{2,1,0:T(8,128)(2,1)}, bf16[3,1024,128]{2,1,0:T(8,128)(2,1)}) custom-call(bf16[4096,128]{1,0:T(8,128)(2,1)} %bitcast.19, bf16[4096,128]{1,0:T(8,128)(2,1)} %bitcast.22, bf16[128,4096]{1,0:T(8,128)(2,1)} %bitcast.25), custom_call_target="tpu_custom_call" | custom-call | bytes 1048576 | tf_op jit(solution)/shard_map/pallas_call | solution.py:196
  29.4 2.6 %collective-permute-start.2 = (bf16[3,1024,128]{2,1,0:T(8,128)(2,1)}, bf16[3,1024,128]{2,1,0:T(8,128)(2,1)S(1)}, u32[]{:S(2)}, u32[]{:S(2)}) collective-permute-start(bf16[3,1024,128]{2,1,0:T(8,128)(2,1)} %get-tuple-element.14), channel_id=1, source_target_pairs={{0,2},{2,4},{4,6},{6,0},{1,3},{3,5},{5,7},{7,1},{8,10},{10,12},{12... | collective-permute-start | bytes 2359304 | tf_op jit(solution)/shard_map/ppermute | solution.py:397
  32.0 4.5 %collective-permute-start.3 = (bf16[3,1024,128]{2,1,0:T(8,128)(2,1)}, bf16[3,1024,128]{2,1,0:T(8,128)(2,1)S(1)}, u32[]{:S(2)}, u32[]{:S(2)}) collective-permute-start(bf16[3,1024,128]{2,1,0:T(8,128)(2,1)} %get-tuple-element.15), channel_id=1, source_target_pairs={{0,6},{2,0},{4,2},{6,4},{1,7},{3,1},{5,3},{7,5},{8,14},{10,8},{12,... | collective-permute-start | bytes 2359304 | tf_op jit(solution)/shard_map/ppermute | solution.py:397
  36.5 2.1 %shard_map.75.first.w0 = bf16[3,1024,128]{2,1,0:T(8,128)(2,1)} custom-call(bf16[4096,128]{1,0:T(8,128)(2,1)} %bitcast.20, bf16[4096,128]{1,0:T(8,128)(2,1)} %bitcast.23, bf16[128,4096]{1,0:T(8,128)(2,1)} %bitcast.26), custom_call_target="tpu_custom_call" | custom-call | bytes 1048576 | tf_op jit(solution)/shard_map/pallas_call | solution.py:164
  38.6 0.0 collective-permute-done.second.w2
  38.6 1.1 copy-done
  39.7 12.4 %all-to-all-done = bf16[64,8,512]{2,1,0:T(8,128)(2,1)} async-done(((bf16[64,8,512]{2,1,0:T(8,128)(2,1)}), bf16[64,8,512]{2,1,0:T(8,128)(2,1)}, u32[]{:S(2)}, u32[]{:S(2)}) %all-to-all-start) | async-done | bytes 524320 | tf_op jit(solution)/shard_map/all_to_all | solution.py:71
  52.1 1.9 %collective-permute-start.1 = (bf16[512,512]{1,0:T(8,128)(2,1)}, bf16[512,512]{1,0:T(8,128)(2,1)S(1)}, u32[]{:S(2)}, u32[]{:S(2)}) collective-permute-start(bf16[512,512]{1,0:T(8,128)(2,1)} %bitcast.10.rows), channel_id=1, source_target_pairs={{0,1},{1,0},{2,3},{3,2},{4,5},{5,4},{6,7},{7,6},{8,9},{9,8},{10,11... | collective-permute-start | bytes 1572872 | tf_op jit(solution)/shard_map/ppermute | solution.py:45
  54.1 0.0 collective-permute-done.2.w1
  54.1 0.0 collective-permute-done.3.w3
  54.1 1.7 %shard_map.78.half = f32[4,512,256]{2,1,0:T(8,128)S(1)} custom-call(bf16[512,512]{1,0:T(8,128)(2,1)} %bitcast.10.rows, bf16[3,1024,128]{2,1,0:T(8,128)(2,1)S(1)} %copy-done.1, bf16[3,1024,128]{2,1,0:T(8,128)(2,1)S(1)} %collective-permute-done.2.w1, bf16[3,1024,128]{2,1,0:T(8,128)(2,1)S(1)} %collective-permute-done.second.w2, ...), custom_call_target="tpu_custom_call" | custom-call | flops 536870912 | bytes 1048576 | tf_op jit(solution)/shard_map/pallas_call | solution.py:257
  55.8 0.3 collective-permute-done.1.rows
  56.1 0.7 shard_map.79
  56.9 17.8 %all_to_all.20.sums = bf16[4,512,256]{2,1,0:T(8,128)(2,1)S(1)} all-to-all(bf16[4,512,256]{2,1,0:T(8,128)(2,1)S(1)} %shard_map.79), channel_id=1, replica_groups={{6,0,2,4},{7,1,3,5},{14,8,10,12},{15,9,11,13},{22,16,18,20},{23,17,19,2..., dimensions={0} | all-to-all | bytes 2097152 | tf_op jit(solution)/shard_map/all_to_all | solution.py:76
  74.7 0.2 shard_map.80
  74.9 10.5 %all_to_all.21.hidden = bf16[4,512,128]{2,1,0:T(8,128)(2,1)S(1)} all-to-all(bf16[4,512,128]{2,1,0:T(8,128)(2,1)S(1)} %shard_map.80), channel_id=1, replica_groups={{4,6,0,2},{5,7,1,3},{12,14,8,10},{13,15,9,11},{20,22,16,18},{21,23,17,1..., dimensions={0} | all-to-all | bytes 1048576 | tf_op jit(solution)/shard_map/all_to_all | solution.py:76
  85.4 0.4 shard_map.82
  85.8 1.9 %collective-permute-start.4 = (bf16[512,512]{1,0:T(8,128)(2,1)S(1)}, bf16[512,512]{1,0:T(8,128)(2,1)S(1)}, u32[]{:S(2)}, u32[]{:S(2)}) collective-permute-start(bf16[512,512]{1,0:T(8,128)(2,1)S(1)} %shard_map.82), channel_id=1, source_target_pairs={{0,1},{1,0},{2,3},{3,2},{4,5},{5,4},{6,7},{7,6},{8,9},{9,8},{10,11... | collective-permute-start | bytes 1572872 | tf_op jit(solution)/shard_map/ppermute | solution.py:45
  87.8 0.5 shard_map.81.keep
  88.2 0.0 copy-start.4
  88.2 0.0 copy-start.2
  88.2 0.0 copy-start.3
  88.3 1.4 %collective-permute-done.4.given = bf16[512,512]{1,0:T(8,128)(2,1)S(1)} collective-permute-done((bf16[512,512]{1,0:T(8,128)(2,1)S(1)}, bf16[512,512]{1,0:T(8,128)(2,1)S(1)}, u32[]{:S(2)}, u32[]{:S(2)}) %collective-permute-start.4) | collective-permute-done | bytes 524320 | tf_op jit(solution)/shard_map/ppermute | solution.py:45
  89.6 0.8 shard_map.83
  90.5 13.3 %all-to-all-start.3 = ((bf16[64,8,512]{2,1,0:T(8,128)(2,1)}), bf16[64,8,512]{2,1,0:T(8,128)(2,1)S(1)}, u32[]{:S(2)}, u32[]{:S(2)}) async-start(bf16[64,8,512]{2,1,0:T(8,128)(2,1)} %bitcast.11), calls=%async_computation.3 | async-start | bytes 1048576 | tf_op jit(solution)/shard_map/all_to_all | solution.py:71
  103.8 0.1 copy.8.counts
  103.9 0.2 shard_map.73.weights
  104.1 25.5 %all-to-all-done.3 = bf16[64,8,512]{2,1,0:T(8,128)(2,1)S(1)} async-done(((bf16[64,8,512]{2,1,0:T(8,128)(2,1)}), bf16[64,8,512]{2,1,0:T(8,128)(2,1)S(1)}, u32[]{:S(2)}, u32[]{:S(2)}) %all-to-all-start.3) | async-done | bytes 524320 | tf_op jit(solution)/shard_map/all_to_all | solution.py:71
  129.6 1.0 shard_map.84
  (7 shorter events, 0.0 us)
Async XLA Ops:
  2.3 36.2 %collective-permute-start = (bf16[3,1024,128]{2,1,0:T(8,128)(2,1)}, bf16[3,1024,128]{2,1,0:T(8,128)(2,1)S(1)}, u32[]{:S(2)}, u32[]{:S(2)}) collective-permute-start(bf16[3,1024,128]{2,1,0:T(8,128)(2,1)} %get-tuple-element.12), channel_id=1, source_target_pairs={{0,4},{2,6},{4,0},{6,2},{1,5},{3,7},{5,1},{7,3},{8,12},{10,14},{12... | collective-permute-start | bytes 2359304 | tf_op jit(solution)/shard_map/ppermute | solution.py:397
  7.5 44.7 %all-to-all-start = ((bf16[64,8,512]{2,1,0:T(8,128)(2,1)}), bf16[64,8,512]{2,1,0:T(8,128)(2,1)}, u32[]{:S(2)}, u32[]{:S(2)}) async-start(bf16[64,8,512]{2,1,0:T(8,128)(2,1)} %bitcast.27), calls=%async_computation | async-start | bytes 1048576 | tf_op jit(solution)/shard_map/all_to_all | solution.py:71
  29.4 24.6 %collective-permute-start.2 = (bf16[3,1024,128]{2,1,0:T(8,128)(2,1)}, bf16[3,1024,128]{2,1,0:T(8,128)(2,1)S(1)}, u32[]{:S(2)}, u32[]{:S(2)}) collective-permute-start(bf16[3,1024,128]{2,1,0:T(8,128)(2,1)} %get-tuple-element.14), channel_id=1, source_target_pairs={{0,2},{2,4},{4,6},{6,0},{1,3},{3,5},{5,7},{7,1},{8,10},{10,12},{12... | collective-permute-start | bytes 2359304 | tf_op jit(solution)/shard_map/ppermute | solution.py:397
  32.0 22.1 %collective-permute-start.3 = (bf16[3,1024,128]{2,1,0:T(8,128)(2,1)}, bf16[3,1024,128]{2,1,0:T(8,128)(2,1)S(1)}, u32[]{:S(2)}, u32[]{:S(2)}) collective-permute-start(bf16[3,1024,128]{2,1,0:T(8,128)(2,1)} %get-tuple-element.15), channel_id=1, source_target_pairs={{0,6},{2,0},{4,2},{6,4},{1,7},{3,1},{5,3},{7,5},{8,14},{10,8},{12,... | collective-permute-start | bytes 2359304 | tf_op jit(solution)/shard_map/ppermute | solution.py:397
  38.6 1.1 copy-start
  39.7 14.4 %copy-start.1 = (bf16[3,1024,128]{2,1,0:T(8,128)(2,1)S(1)}, bf16[3,1024,128]{2,1,0:T(8,128)(2,1)}, u32[]{:S(2)}) copy-start(bf16[3,1024,128]{2,1,0:T(8,128)(2,1)} %shard_map.75.first.w0) | copy-start | bytes 2359300
  52.1 4.0 %collective-permute-start.1 = (bf16[512,512]{1,0:T(8,128)(2,1)}, bf16[512,512]{1,0:T(8,128)(2,1)S(1)}, u32[]{:S(2)}, u32[]{:S(2)}) collective-permute-start(bf16[512,512]{1,0:T(8,128)(2,1)} %bitcast.10.rows), channel_id=1, source_target_pairs={{0,1},{1,0},{2,3},{3,2},{4,5},{5,4},{6,7},{7,6},{8,9},{9,8},{10,11... | collective-permute-start | bytes 1572872 | tf_op jit(solution)/shard_map/ppermute | solution.py:45
  85.8 3.8 %collective-permute-start.4 = (bf16[512,512]{1,0:T(8,128)(2,1)S(1)}, bf16[512,512]{1,0:T(8,128)(2,1)S(1)}, u32[]{:S(2)}, u32[]{:S(2)}) collective-permute-start(bf16[512,512]{1,0:T(8,128)(2,1)S(1)} %shard_map.82), channel_id=1, source_target_pairs={{0,1},{1,0},{2,3},{3,2},{4,5},{5,4},{6,7},{7,6},{8,9},{9,8},{10,11... | collective-permute-start | bytes 1572872 | tf_op jit(solution)/shard_map/ppermute | solution.py:45
  88.2 15.5 %copy-start.4 = (s32[128]{0:T(128)S(1)}, s32[128]{0:T(128)}, u32[]{:S(2)}) copy-start(s32[128]{0:T(128)} %param.10) | copy-start | bytes 1540
  88.2 15.7 %copy-start.2 = (s32[64,1,8]{0,2,1:T(8,128)S(1)}, s32[64,1,8]{0,2,1:T(8,128)}, u32[]{:S(2)}) copy-start(s32[64,1,8]{0,2,1:T(8,128)} %param.8) | copy-start | bytes 6148
  88.2 15.6 %copy-start.3 = (f32[64,1,8]{0,2,1:T(8,128)S(1)}, f32[64,1,8]{0,2,1:T(8,128)}, u32[]{:S(2)}) copy-start(f32[64,1,8]{0,2,1:T(8,128)} %param.9) | copy-start | bytes 6148
  90.5 39.1 %all-to-all-start.3 = ((bf16[64,8,512]{2,1,0:T(8,128)(2,1)}), bf16[64,8,512]{2,1,0:T(8,128)(2,1)S(1)}, u32[]{:S(2)}, u32[]{:S(2)}) async-start(bf16[64,8,512]{2,1,0:T(8,128)(2,1)} %bitcast.11), calls=%async_computation.3 | async-start | bytes 1048576 | tf_op jit(solution)/shard_map/all_to_all | solution.py:71

commit v8 on v7

--- a/solution.py
+++ b/solution.py
@@ -111,13 +111,15 @@
     fetch_slots.wait()
     names = spread(slots[...].astype(F32), rows)
     hit = (names == token).astype(BF)
-    for copy in copies:
-        copy.wait()
-    sends = [pltpu.make_async_copy(held, block, out_sems.at[4])]
-    sends[0].start()
     fetch.wait()
     step = rows // 4
+    sends = []
     for n in range(4):
+        if n == 1:
+            for copy in copies:
+                copy.wait()
+            sends.append(pltpu.make_async_copy(held, block, out_sems.at[4]))
+            sends[-1].start()
         part = pl.ds(n * step, step)
         rows_out[part] = lax.dot_general(
             hit[:, n * step : (n + 1) * step], own[...], (((0,), (0,)), ((), ())), preferred_element_type=F32

time: 132 us -> 132 us (level)
  no operation moved by 1% of the time
where the time goes in v8:
time: 132 us; the launch traced here: 131 us
  starting transfers between devices  48.8 us (37%)
  waiting for transfers between devices  39.6 us (30%)
  blocking collectives  28.3 us (21%)
  Pallas kernels  12.7 us (10%)
    all_to_all x2, waiting for transfers between devices, exchange(): return lax.all_to_all(rows, E, 0, 0, axis_index_groups=[order], tiled=True)  37.9 us
    all_to_all x2, starting transfers between devices, exchange(): return lax.all_to_all(rows, E, 0, 0, axis_index_groups=[order], tiled=True)  32.8 us
    all_to_all x2, blocking collectives, exchange_y(): lax.all_to_all(blocks, 'y', 0, 0, axis_index_groups=[order], tiled=True)  28.3 us
    ppermute x3, starting transfers between devices, local(): lax.ppermute(block, 'y', [(j, (j + d) % NY) for j in range(NY)])  12.2 us
    ppermute x2, starting transfers between devices, swap_cores(): return lax.ppermute(a, 'core', [(0, 1), (1, 0)])  3.83 us
  transfers between devices with their start and end apart: 7, of which 4 were waited for; matrix products, arithmetic and copies ran while one was open for 0% of the time, Pallas kernels for 5%

profile of v8, /device:TPU:6, one launch (start us, length us, event | category | flops | bytes accessed | tf_op | source)
XLA Modules:
  0.0 130.8 jit_solution(16400977367487771717)
XLA Ops:
  0.0 2.6 %shard_map.74 = (bf16[512,512]{1,0:T(8,128)(2,1)}, bf16[3,1024,128]{2,1,0:T(8,128)(2,1)}) custom-call(s32[8,64]{1,0:T(8,128)} %bitcast.15, bf16[128,4096]{1,0:T(8,128)(2,1)} %tokens.1, bf16[4096,128]{1,0:T(8,128)(2,1)} %bitcast.18, bf16[4096,128]{1,0:T(8,128)(2,1)} %bitcast.21, bf16[128,4096]{1,0:T(8,128)(2,1)} %bitcast.24), custom_call_target="tpu_custom_call" | custom-call | bytes 5242880 | tf_op jit(solution)/shard_map/pallas_call | solution.py:137
  2.6 5.1 %collective-permute-start = (bf16[3,1024,128]{2,1,0:T(8,128)(2,1)}, bf16[3,1024,128]{2,1,0:T(8,128)(2,1)S(1)}, u32[]{:S(2)}, u32[]{:S(2)}) collective-permute-start(bf16[3,1024,128]{2,1,0:T(8,128)(2,1)} %get-tuple-element.12), channel_id=1, source_target_pairs={{0,4},{2,6},{4,0},{6,2},{1,5},{3,7},{5,1},{7,3},{8,12},{10,14},{12... | collective-permute-start | bytes 2359304 | tf_op jit(solution)/shard_map/ppermute | solution.py:399
  7.7 19.5 %all-to-all-start = ((bf16[64,8,512]{2,1,0:T(8,128)(2,1)}), bf16[64,8,512]{2,1,0:T(8,128)(2,1)}, u32[]{:S(2)}, u32[]{:S(2)}) async-start(bf16[64,8,512]{2,1,0:T(8,128)(2,1)} %bitcast.27), calls=%async_computation | async-start | bytes 1048576 | tf_op jit(solution)/shard_map/all_to_all | solution.py:71
  27.2 2.4 %shard_map.77 = (bf16[3,1024,128]{2,1,0:T(8,128)(2,1)}, bf16[3,1024,128]{2,1,0:T(8,128)(2,1)}) custom-call(bf16[4096,128]{1,0:T(8,128)(2,1)} %bitcast.19, bf16[4096,128]{1,0:T(8,128)(2,1)} %bitcast.22, bf16[128,4096]{1,0:T(8,128)(2,1)} %bitcast.25), custom_call_target="tpu_custom_call" | custom-call | bytes 1048576 | tf_op jit(solution)/shard_map/pallas_call | solution.py:198
  29.6 2.6 %collective-permute-start.2 = (bf16[3,1024,128]{2,1,0:T(8,128)(2,1)}, bf16[3,1024,128]{2,1,0:T(8,128)(2,1)S(1)}, u32[]{:S(2)}, u32[]{:S(2)}) collective-permute-start(bf16[3,1024,128]{2,1,0:T(8,128)(2,1)} %get-tuple-element.14), channel_id=1, source_target_pairs={{0,2},{2,4},{4,6},{6,0},{1,3},{3,5},{5,7},{7,1},{8,10},{10,12},{12... | collective-permute-start | bytes 2359304 | tf_op jit(solution)/shard_map/ppermute | solution.py:399
  32.2 4.5 %collective-permute-start.3 = (bf16[3,1024,128]{2,1,0:T(8,128)(2,1)}, bf16[3,1024,128]{2,1,0:T(8,128)(2,1)S(1)}, u32[]{:S(2)}, u32[]{:S(2)}) collective-permute-start(bf16[3,1024,128]{2,1,0:T(8,128)(2,1)} %get-tuple-element.15), channel_id=1, source_target_pairs={{0,6},{2,0},{4,2},{6,4},{1,7},{3,1},{5,3},{7,5},{8,14},{10,8},{12,... | collective-permute-start | bytes 2359304 | tf_op jit(solution)/shard_map/ppermute | solution.py:399
  36.7 2.1 %shard_map.75.first.w0 = bf16[3,1024,128]{2,1,0:T(8,128)(2,1)} custom-call(bf16[4096,128]{1,0:T(8,128)(2,1)} %bitcast.20, bf16[4096,128]{1,0:T(8,128)(2,1)} %bitcast.23, bf16[128,4096]{1,0:T(8,128)(2,1)} %bitcast.26), custom_call_target="tpu_custom_call" | custom-call | bytes 1048576 | tf_op jit(solution)/shard_map/pallas_call | solution.py:166
  38.8 0.0 collective-permute-done.second.w2
  38.8 1.1 copy-done
  40.0 12.4 %all-to-all-done = bf16[64,8,512]{2,1,0:T(8,128)(2,1)} async-done(((bf16[64,8,512]{2,1,0:T(8,128)(2,1)}), bf16[64,8,512]{2,1,0:T(8,128)(2,1)}, u32[]{:S(2)}, u32[]{:S(2)}) %all-to-all-start) | async-done | bytes 524320 | tf_op jit(solution)/shard_map/all_to_all | solution.py:71
  52.4 1.9 %collective-permute-start.1 = (bf16[512,512]{1,0:T(8,128)(2,1)}, bf16[512,512]{1,0:T(8,128)(2,1)S(1)}, u32[]{:S(2)}, u32[]{:S(2)}) collective-permute-start(bf16[512,512]{1,0:T(8,128)(2,1)} %bitcast.10.rows), channel_id=1, source_target_pairs={{0,1},{1,0},{2,3},{3,2},{4,5},{5,4},{6,7},{7,6},{8,9},{9,8},{10,11... | collective-permute-start | bytes 1572872 | tf_op jit(solution)/shard_map/ppermute | solution.py:45
  54.3 0.0 collective-permute-done.2.w1
  54.3 0.0 collective-permute-done.3.w3
  54.3 1.8 %shard_map.78.half = f32[4,512,256]{2,1,0:T(8,128)S(1)} custom-call(bf16[512,512]{1,0:T(8,128)(2,1)} %bitcast.10.rows, bf16[3,1024,128]{2,1,0:T(8,128)(2,1)S(1)} %copy-done.1, bf16[3,1024,128]{2,1,0:T(8,128)(2,1)S(1)} %collective-permute-done.2.w1, bf16[3,1024,128]{2,1,0:T(8,128)(2,1)S(1)} %collective-permute-done.second.w2, ...), custom_call_target="tpu_custom_call" | custom-call | flops 536870912 | bytes 1048576 | tf_op jit(solution)/shard_map/pallas_call | solution.py:259
  56.1 0.3 collective-permute-done.1.rows
  56.4 0.7 shard_map.79
  57.1 17.8 %all_to_all.20.sums = bf16[4,512,256]{2,1,0:T(8,128)(2,1)S(1)} all-to-all(bf16[4,512,256]{2,1,0:T(8,128)(2,1)S(1)} %shard_map.79), channel_id=1, replica_groups={{6,0,2,4},{7,1,3,5},{14,8,10,12},{15,9,11,13},{22,16,18,20},{23,17,19,2..., dimensions={0} | all-to-all | bytes 2097152 | tf_op jit(solution)/shard_map/all_to_all | solution.py:76
  74.9 0.2 shard_map.80
  75.1 10.5 %all_to_all.21.hidden = bf16[4,512,128]{2,1,0:T(8,128)(2,1)S(1)} all-to-all(bf16[4,512,128]{2,1,0:T(8,128)(2,1)S(1)} %shard_map.80), channel_id=1, replica_groups={{4,6,0,2},{5,7,1,3},{12,14,8,10},{13,15,9,11},{20,22,16,18},{21,23,17,1..., dimensions={0} | all-to-all | bytes 1048576 | tf_op jit(solution)/shard_map/all_to_all | solution.py:76
  85.6 0.4 shard_map.82
  86.1 1.9 %collective-permute-start.4 = (bf16[512,512]{1,0:T(8,128)(2,1)S(1)}, bf16[512,512]{1,0:T(8,128)(2,1)S(1)}, u32[]{:S(2)}, u32[]{:S(2)}) collective-permute-start(bf16[512,512]{1,0:T(8,128)(2,1)S(1)} %shard_map.82), channel_id=1, source_target_pairs={{0,1},{1,0},{2,3},{3,2},{4,5},{5,4},{6,7},{7,6},{8,9},{9,8},{10,11... | collective-permute-start | bytes 1572872 | tf_op jit(solution)/shard_map/ppermute | solution.py:45
  88.0 0.5 shard_map.81.keep
  88.5 0.0 copy-start.4
  88.5 0.0 copy-start.2
  88.5 0.0 copy-start.3
  88.5 1.4 %collective-permute-done.4.given = bf16[512,512]{1,0:T(8,128)(2,1)S(1)} collective-permute-done((bf16[512,512]{1,0:T(8,128)(2,1)S(1)}, bf16[512,512]{1,0:T(8,128)(2,1)S(1)}, u32[]{:S(2)}, u32[]{:S(2)}) %collective-permute-start.4) | collective-permute-done | bytes 524320 | tf_op jit(solution)/shard_map/ppermute | solution.py:45
  89.9 0.8 shard_map.83
  90.7 13.3 %all-to-all-start.3 = ((bf16[64,8,512]{2,1,0:T(8,128)(2,1)}), bf16[64,8,512]{2,1,0:T(8,128)(2,1)S(1)}, u32[]{:S(2)}, u32[]{:S(2)}) async-start(bf16[64,8,512]{2,1,0:T(8,128)(2,1)} %bitcast.11), calls=%async_computation.3 | async-start | bytes 1048576 | tf_op jit(solution)/shard_map/all_to_all | solution.py:71
  104.0 0.1 copy.8.counts
  104.1 0.2 shard_map.73.weights
  104.4 25.5 %all-to-all-done.3 = bf16[64,8,512]{2,1,0:T(8,128)(2,1)S(1)} async-done(((bf16[64,8,512]{2,1,0:T(8,128)(2,1)}), bf16[64,8,512]{2,1,0:T(8,128)(2,1)S(1)}, u32[]{:S(2)}, u32[]{:S(2)}) %all-to-all-start.3) | async-done | bytes 524320 | tf_op jit(solution)/shard_map/all_to_all | solution.py:71
  129.8 1.0 shard_map.84
  (7 shorter events, 0.0 us)
Async XLA Ops:
  2.6 36.2 %collective-permute-start = (bf16[3,1024,128]{2,1,0:T(8,128)(2,1)}, bf16[3,1024,128]{2,1,0:T(8,128)(2,1)S(1)}, u32[]{:S(2)}, u32[]{:S(2)}) collective-permute-start(bf16[3,1024,128]{2,1,0:T(8,128)(2,1)} %get-tuple-element.12), channel_id=1, source_target_pairs={{0,4},{2,6},{4,0},{6,2},{1,5},{3,7},{5,1},{7,3},{8,12},{10,14},{12... | collective-permute-start | bytes 2359304 | tf_op jit(solution)/shard_map/ppermute | solution.py:399
  7.7 44.7 %all-to-all-start = ((bf16[64,8,512]{2,1,0:T(8,128)(2,1)}), bf16[64,8,512]{2,1,0:T(8,128)(2,1)}, u32[]{:S(2)}, u32[]{:S(2)}) async-start(bf16[64,8,512]{2,1,0:T(8,128)(2,1)} %bitcast.27), calls=%async_computation | async-start | bytes 1048576 | tf_op jit(solution)/shard_map/all_to_all | solution.py:71
  29.6 24.7 %collective-permute-start.2 = (bf16[3,1024,128]{2,1,0:T(8,128)(2,1)}, bf16[3,1024,128]{2,1,0:T(8,128)(2,1)S(1)}, u32[]{:S(2)}, u32[]{:S(2)}) collective-permute-start(bf16[3,1024,128]{2,1,0:T(8,128)(2,1)} %get-tuple-element.14), channel_id=1, source_target_pairs={{0,2},{2,4},{4,6},{6,0},{1,3},{3,5},{5,7},{7,1},{8,10},{10,12},{12... | collective-permute-start | bytes 2359304 | tf_op jit(solution)/shard_map/ppermute | solution.py:399
  32.2 22.1 %collective-permute-start.3 = (bf16[3,1024,128]{2,1,0:T(8,128)(2,1)}, bf16[3,1024,128]{2,1,0:T(8,128)(2,1)S(1)}, u32[]{:S(2)}, u32[]{:S(2)}) collective-permute-start(bf16[3,1024,128]{2,1,0:T(8,128)(2,1)} %get-tuple-element.15), channel_id=1, source_target_pairs={{0,6},{2,0},{4,2},{6,4},{1,7},{3,1},{5,3},{7,5},{8,14},{10,8},{12,... | collective-permute-start | bytes 2359304 | tf_op jit(solution)/shard_map/ppermute | solution.py:399
  38.8 1.1 copy-start
  39.9 14.4 %copy-start.1 = (bf16[3,1024,128]{2,1,0:T(8,128)(2,1)S(1)}, bf16[3,1024,128]{2,1,0:T(8,128)(2,1)}, u32[]{:S(2)}) copy-start(bf16[3,1024,128]{2,1,0:T(8,128)(2,1)} %shard_map.75.first.w0) | copy-start | bytes 2359300
  52.4 4.0 %collective-permute-start.1 = (bf16[512,512]{1,0:T(8,128)(2,1)}, bf16[512,512]{1,0:T(8,128)(2,1)S(1)}, u32[]{:S(2)}, u32[]{:S(2)}) collective-permute-start(bf16[512,512]{1,0:T(8,128)(2,1)} %bitcast.10.rows), channel_id=1, source_target_pairs={{0,1},{1,0},{2,3},{3,2},{4,5},{5,4},{6,7},{7,6},{8,9},{9,8},{10,11... | collective-permute-start | bytes 1572872 | tf_op jit(solution)/shard_map/ppermute | solution.py:45
  86.1 3.8 %collective-permute-start.4 = (bf16[512,512]{1,0:T(8,128)(2,1)S(1)}, bf16[512,512]{1,0:T(8,128)(2,1)S(1)}, u32[]{:S(2)}, u32[]{:S(2)}) collective-permute-start(bf16[512,512]{1,0:T(8,128)(2,1)S(1)} %shard_map.82), channel_id=1, source_target_pairs={{0,1},{1,0},{2,3},{3,2},{4,5},{5,4},{6,7},{7,6},{8,9},{9,8},{10,11... | collective-permute-start | bytes 1572872 | tf_op jit(solution)/shard_map/ppermute | solution.py:45
  88.5 15.5 %copy-start.4 = (s32[128]{0:T(128)S(1)}, s32[128]{0:T(128)}, u32[]{:S(2)}) copy-start(s32[128]{0:T(128)} %param.10) | copy-start | bytes 1540
  88.5 15.7 %copy-start.2 = (s32[64,1,8]{0,2,1:T(8,128)S(1)}, s32[64,1,8]{0,2,1:T(8,128)}, u32[]{:S(2)}) copy-start(s32[64,1,8]{0,2,1:T(8,128)} %param.8) | copy-start | bytes 6148
  88.5 15.6 %copy-start.3 = (f32[64,1,8]{0,2,1:T(8,128)S(1)}, f32[64,1,8]{0,2,1:T(8,128)}, u32[]{:S(2)}) copy-start(f32[64,1,8]{0,2,1:T(8,128)} %param.9) | copy-start | bytes 6148
  90.7 39.1 %all-to-all-start.3 = ((bf16[64,8,512]{2,1,0:T(8,128)(2,1)}), bf16[64,8,512]{2,1,0:T(8,128)(2,1)S(1)}, u32[]{:S(2)}, u32[]{:S(2)}) async-start(bf16[64,8,512]{2,1,0:T(8,128)(2,1)} %bitcast.11), calls=%async_computation.3 | async-start | bytes 1048576 | tf_op jit(solution)/shard_map/all_to_all | solution.py:71
